TPU v7x, 32 devices: a whole 2x2x4 slice. The times are simulated.
32 devices in a mesh: dp: 4 (over z), cp: 8 (over y, x, core).
Axes of the slice: x: 2, y: 2, z: 4, core: 2. Of those that a mesh axis runs over, the one named last changes fastest.
Arguments:
- inputs: bfloat16 [4, 2048, 2048], P('dp', 'cp'), may hold values from -6 to 6
- attn_gain: bfloat16 [2048], P(('dp', 'cp')), may hold values from 0.099609375 to 1.8984375
- w_query: bfloat16 [2048, 2048], P(('dp', 'cp')), may hold values from -0.125 to 0.125
- w_key: bfloat16 [2048, 1024], P(('dp', 'cp')), may hold values from -0.125 to 0.125
- w_value: bfloat16 [2048, 1024], P(('dp', 'cp')), may hold values from -0.125 to 0.125
- w_output: bfloat16 [2048, 2048], P(('dp', 'cp')), may hold values from -1 to 1
- ffn_gain: bfloat16 [2048], P(('dp', 'cp')), may hold values from 0.099609375 to 1.8984375
- w_gate: bfloat16 [2048, 8192], P(('dp', 'cp')), may hold values from -0.125 to 0.125
- w_up: bfloat16 [2048, 8192], P(('dp', 'cp')), may hold values from -0.125 to 0.125
- w_down: bfloat16 [8192, 2048], P(('dp', 'cp')), may hold values from -0.0625 to 0.0625
- cotangent: bfloat16 [4, 2048, 2048], P('dp', 'cp'), may hold values from -6 to 6
Outputs:
- output: float32 [4, 2048, 2048], P('dp', 'cp')
- grad_input: float32 [4, 2048, 2048], P('dp', 'cp')
- grad_attn_gain: float32 [2048], P(('dp', 'cp'))
- grad_query: float32 [2048, 2048], P(('dp', 'cp'))
- grad_key: float32 [2048, 1024], P(('dp', 'cp'))
- grad_value: float32 [2048, 1024], P(('dp', 'cp'))
- grad_output: float32 [2048, 2048], P(('dp', 'cp'))
- grad_ffn_gain: float32 [2048], P(('dp', 'cp'))
- grad_gate: float32 [2048, 8192], P(('dp', 'cp'))
- grad_up: float32 [2048, 8192], P(('dp', 'cp'))
- grad_down: float32 [8192, 2048], P(('dp', 'cp'))
All inputs are finite; a program needn't handle non-finite values.
Results may differ from a plain program's by a relative error of at most 0.018.
Values may be sent and summed in bfloat16 or wider, within the bound.
No kernel may reach another device: no remote copies, remote signals or barrier semaphores. Data moves between devices by JAX's collectives and lax.ppermute only.
A program may use at most 512 MiB of HBM per device.

v0:
```python
import jax
import jax.numpy as jnp
from jax import lax
from jax.sharding import PartitionSpec as P

H = 16
KVH = 8
HD = 128


EPS = 1e-05
THETA = 1000000.0


def rotary_tables(positions):
    half_dim = HD // 2
    inv_freq = THETA ** (-(jnp.arange(half_dim, dtype=jnp.float32) * 2.0 / HD))
    angles = positions.astype(jnp.float32)[:, None] * inv_freq[None, :]
    cos_table = jnp.cos(angles)
    sin_table = jnp.sin(angles)
    return (
        jnp.concatenate([cos_table, cos_table], -1),
        jnp.concatenate([sin_table, sin_table], -1),
    )


def rotate(flat, cos_table, sin_table):
    row_count = flat.shape[0]
    heads = flat.reshape(row_count, -1, HD)
    half_dim = HD // 2
    rotated = jnp.concatenate([-heads[..., half_dim:], heads[..., :half_dim]], -1)
    return (heads * cos_table[:, None, :] + rotated * sin_table[:, None, :]).reshape(row_count, -1)


def rms_forward(values):
    rms_scale = lax.rsqrt(jnp.mean(values * values, -1, keepdims=True) + EPS)
    return (rms_scale, values * rms_scale)


def rms_backward(grad_normed, base_normed, rms_scale, gain_vec):
    gain_grad = jnp.sum(grad_normed * base_normed, 0)
    scaled_grad = grad_normed * gain_vec
    inner_mean = jnp.mean(scaled_grad * base_normed, -1, keepdims=True)
    return (gain_grad, rms_scale * (scaled_grad - base_normed * inner_mean))


def cross(left, right):
    return lax.dot_general(
        left, right, (((0,), (0,)), ((), ())), preferred_element_type=jnp.float32
    )


def back(left, right):
    return lax.dot_general(
        left, right, (((1,), (1,)), ((), ())), preferred_element_type=jnp.float32
    )


def gate_grads(grad_act, gate_pre, up_pre):
    gate_sig = jax.nn.sigmoid(gate_pre)
    grad_gate_pre = (grad_act * up_pre * (gate_sig * (1.0 + gate_pre * (1.0 - gate_sig)))).astype(
        jnp.bfloat16
    )
    grad_up_pre = (grad_act * (gate_pre * gate_sig)).astype(jnp.bfloat16)
    return (grad_gate_pre, grad_up_pre)


def masked_scores(query_heads, key_heads, query_pos, key_pos):
    raw_scores = jnp.einsum(
        "qkgd,lkd->kgql", query_heads, key_heads, preferred_element_type=jnp.float32
    )
    scores = raw_scores * HD ** (-0.5)
    causal = key_pos[None, :] <= query_pos[:, None]
    return jnp.where(causal, scores, -1e30)


def shards(
    inputs, attn_gain, w_query, w_key, w_value, w_output, ffn_gain, w_gate, w_up, w_down, cotangent
):
    weights = (
        lax.all_gather(attn_gain, ("dp", "cp"), axis=0, tiled=True),
        lax.all_gather(ffn_gain, ("dp", "cp"), axis=0, tiled=True),
        lax.all_gather(w_query, ("dp", "cp"), axis=0, tiled=True),
        lax.all_gather(w_key, ("dp", "cp"), axis=0, tiled=True),
        lax.all_gather(w_value, ("dp", "cp"), axis=0, tiled=True),
        lax.all_gather(w_output, ("dp", "cp"), axis=0, tiled=True),
    )
    gain_one, gain_two, wq_full, wk_full, wv_full, wo_full = weights
    seq_count, part_len, width = inputs.shape
    row_count = seq_count * part_len
    n_cp = lax.axis_size("cp")
    length = part_len * n_cp
    groups = H // KVH
    query_pos = lax.axis_index("cp") * part_len + jnp.arange(part_len, dtype=jnp.int32)
    key_pos = jnp.arange(length, dtype=jnp.int32)
    cos_part, sin_part = rotary_tables(query_pos)
    cos_rows = jnp.tile(cos_part, (seq_count, 1))
    sin_rows = jnp.tile(sin_part, (seq_count, 1))
    values_in = inputs.reshape(row_count, width).astype(jnp.float32)
    rms_one, base_one = rms_forward(values_in)
    gain_one_f = gain_one.astype(jnp.float32)
    normed_one = (base_one * gain_one_f).astype(jnp.bfloat16)
    query_flat = rotate(
        jnp.dot(normed_one, wq_full, preferred_element_type=jnp.float32), cos_rows, sin_rows
    ).astype(jnp.bfloat16)
    key_flat = rotate(
        jnp.dot(normed_one, wk_full, preferred_element_type=jnp.float32), cos_rows, sin_rows
    ).astype(jnp.bfloat16)
    value_flat = jnp.dot(normed_one, wv_full, preferred_element_type=jnp.float32).astype(
        jnp.bfloat16
    )
    key_seqs = key_flat.reshape(seq_count, part_len, -1)
    value_seqs = value_flat.reshape(seq_count, part_len, -1)
    carried = (key_seqs, value_seqs)
    gathered = (
        lax.all_gather(carried[0], "cp", axis=1, tiled=True),
        lax.all_gather(carried[1], "cp", axis=1, tiled=True),
    )
    keys_all = gathered[0]
    values_all = gathered[1]
    query_seqs = query_flat.reshape(seq_count, part_len, -1)

    def forward_seq(seq_items):
        query_seq, key_seq, value_seq = seq_items
        query_heads = query_seq.reshape(part_len, KVH, groups, HD)
        scores = masked_scores(query_heads, key_seq.reshape(length, KVH, HD), query_pos, key_pos)
        row_max = jnp.max(scores, -1, keepdims=True)
        exp_scores = jnp.exp(scores - row_max)
        exp_total = jnp.sum(exp_scores, -1, keepdims=True)
        attn_probs = exp_scores / exp_total
        mixed = jnp.einsum(
            "kgql,lkd->qkgd",
            attn_probs.astype(jnp.bfloat16),
            value_seq.reshape(length, KVH, HD),
            preferred_element_type=jnp.float32,
        )
        return (mixed.reshape(part_len, -1), row_max + jnp.log(exp_total))

    attn_mixed, log_totals = lax.map(forward_seq, (query_seqs, keys_all, values_all))
    attn_rows = attn_mixed.reshape(row_count, -1).astype(jnp.bfloat16)
    hidden_res = values_in + jnp.dot(attn_rows, wo_full, preferred_element_type=jnp.float32)
    rms_two, base_two = rms_forward(hidden_res)
    gain_two_f = gain_two.astype(jnp.float32)
    normed_two = (base_two * gain_two_f).astype(jnp.bfloat16)
    grad_out = cotangent.reshape(row_count, width).astype(jnp.float32)
    wg_full, wu_full, wd_full = (
        lax.all_gather(w_gate, ("dp", "cp"), axis=0, tiled=True),
        lax.all_gather(w_up, ("dp", "cp"), axis=0, tiled=True),
        lax.all_gather(w_down, ("dp", "cp"), axis=0, tiled=True),
    )
    gate_pre = jnp.dot(normed_two, wg_full, preferred_element_type=jnp.float32)
    up_pre = jnp.dot(normed_two, wu_full, preferred_element_type=jnp.float32)
    hidden_act = (jax.nn.silu(gate_pre) * up_pre).astype(jnp.bfloat16)
    output = hidden_res + jnp.dot(hidden_act, wd_full, preferred_element_type=jnp.float32)
    back_wg, back_wu, back_wd = (
        lax.all_gather(w_gate, ("dp", "cp"), axis=0, tiled=True),
        lax.all_gather(w_up, ("dp", "cp"), axis=0, tiled=True),
        lax.all_gather(w_down, ("dp", "cp"), axis=0, tiled=True),
    )
    grad_outb = grad_out.astype(jnp.bfloat16)
    grad_act = back(grad_outb, back_wd)
    grad_gate_pre, grad_up_pre = gate_grads(grad_act, gate_pre, up_pre)
    grad_two = back(grad_gate_pre, back_wg) + back(grad_up_pre, back_wu)
    grad_down_w = cross(hidden_act, grad_outb)
    grad_w_gate = cross(normed_two, grad_gate_pre)
    grad_w_up = cross(normed_two, grad_up_pre)
    out_gate, out_up, out_down = (
        lax.psum_scatter(grad_w_gate, ("dp", "cp"), scatter_dimension=0, tiled=True),
        lax.psum_scatter(grad_w_up, ("dp", "cp"), scatter_dimension=0, tiled=True),
        lax.psum_scatter(grad_down_w, ("dp", "cp"), scatter_dimension=0, tiled=True),
    )
    grad_gain_two, grad_hidden_norm = rms_backward(grad_two, base_two, rms_two, gain_two_f)
    grad_hidden = grad_out + grad_hidden_norm
    grad_hidb = grad_hidden.astype(jnp.bfloat16)
    grad_w_output = cross(attn_rows, grad_hidb)
    grad_attn = back(grad_hidb, wo_full).astype(jnp.bfloat16)

    def backward_seq(seq_items):
        query_seq, key_seq, value_seq, log_total, grad_seq = seq_items
        query_heads = query_seq.reshape(part_len, KVH, groups, HD)
        key_heads = key_seq.reshape(length, KVH, HD)
        value_heads = value_seq.reshape(length, KVH, HD)
        grad_heads = grad_seq.reshape(part_len, KVH, groups, HD)
        scores = masked_scores(query_heads, key_heads, query_pos, key_pos)
        attn_probs = jnp.exp(scores - log_total)
        grad_probs = jnp.einsum(
            "qkgd,lkd->kgql", grad_heads, value_heads, preferred_element_type=jnp.float32
        )
        row_dot = jnp.sum(attn_probs * grad_probs, -1, keepdims=True)
        grad_scores = (attn_probs * (grad_probs - row_dot) * HD ** (-0.5)).astype(jnp.bfloat16)
        grad_q = jnp.einsum(
            "kgql,lkd->qkgd", grad_scores, key_heads, preferred_element_type=jnp.float32
        )
        grad_k = jnp.einsum(
            "kgql,qkgd->lkd", grad_scores, query_heads, preferred_element_type=jnp.float32
        )
        grad_v = jnp.einsum(
            "kgql,qkgd->lkd",
            attn_probs.astype(jnp.bfloat16),
            grad_heads,
            preferred_element_type=jnp.float32,
        )
        return (
            grad_q.reshape(part_len, -1),
            grad_k.reshape(length, -1),
            grad_v.reshape(length, -1),
        )

    grad_q_all, grad_k_all, grad_v_all = lax.map(
        backward_seq,
        (query_seqs, keys_all, values_all, log_totals, grad_attn.reshape(seq_count, part_len, -1)),
    )
    grad_keys, grad_values = (
        lax.psum_scatter(
            grad_k_all.astype(jnp.bfloat16), "cp", scatter_dimension=1, tiled=True
        ).astype(jnp.float32),
        lax.psum_scatter(
            grad_v_all.astype(jnp.bfloat16), "cp", scatter_dimension=1, tiled=True
        ).astype(jnp.float32),
    )
    grad_query_rows = rotate(grad_q_all.reshape(row_count, -1), cos_rows, -sin_rows).astype(
        jnp.bfloat16
    )
    grad_key_rows = rotate(grad_keys.reshape(row_count, -1), cos_rows, -sin_rows).astype(
        jnp.bfloat16
    )
    grad_value_rows = grad_values.reshape(row_count, -1).astype(jnp.bfloat16)
    grad_one = (
        back(grad_query_rows, wq_full)
        + back(grad_key_rows, wk_full)
        + back(grad_value_rows, wv_full)
    )
    grad_w_query = cross(normed_one, grad_query_rows)
    grad_w_key = cross(normed_one, grad_key_rows)
    grad_w_value = cross(normed_one, grad_value_rows)
    grad_gain_one, grad_input_norm = rms_backward(grad_one, base_one, rms_one, gain_one_f)
    attn_parts = (
        lax.psum_scatter(grad_gain_one, ("dp", "cp"), scatter_dimension=0, tiled=True),
        lax.psum_scatter(grad_gain_two, ("dp", "cp"), scatter_dimension=0, tiled=True),
        lax.psum_scatter(grad_w_query, ("dp", "cp"), scatter_dimension=0, tiled=True),
        lax.psum_scatter(grad_w_key, ("dp", "cp"), scatter_dimension=0, tiled=True),
        lax.psum_scatter(grad_w_value, ("dp", "cp"), scatter_dimension=0, tiled=True),
        lax.psum_scatter(grad_w_output, ("dp", "cp"), scatter_dimension=0, tiled=True),
    )
    grad_in = grad_hidden + grad_input_norm
    return (
        output.reshape(seq_count, part_len, width),
        grad_in.reshape(seq_count, part_len, width),
        attn_parts[0],
        attn_parts[2],
        attn_parts[3],
        attn_parts[4],
        attn_parts[5],
        attn_parts[1],
        out_gate,
        out_up,
        out_down,
    )


def solution(mesh):
    placed = (
        P("dp", "cp", None),
        P(("dp", "cp")),
        P(("dp", "cp"), None),
        P(("dp", "cp"), None),
        P(("dp", "cp"), None),
        P(("dp", "cp"), None),
        P(("dp", "cp")),
        P(("dp", "cp"), None),
        P(("dp", "cp"), None),
        P(("dp", "cp"), None),
        P("dp", "cp", None),
    )
    return jax.shard_map(
        shards,
        mesh=mesh,
        in_specs=placed,
        out_specs=(
            P("dp", "cp", None),
            P("dp", "cp", None),
            P(("dp", "cp")),
            P(("dp", "cp"), None),
            P(("dp", "cp"), None),
            P(("dp", "cp"), None),
            P(("dp", "cp"), None),
            P(("dp", "cp")),
            P(("dp", "cp"), None),
            P(("dp", "cp"), None),
            P(("dp", "cp"), None),
        ),
        check_vma=False,
    )
```

profile of v0, /device:TPU:1, one launch (start us, length us, event | category | flops | bytes accessed | tf_op | source)
XLA Modules:
  0.0 3981.7 jit_solution(8800601031572254411)
XLA Ops:
  10.4 41.7 %all-reduce.5 = (bf16[2048]{0:T(1024)(128)(2,1)S(1)}, bf16[2048]{0:T(1024)(128)(2,1)S(1)}) all-reduce(bf16[2048]{0:T(1024)(128)(2,1)S(1)} %dynamic-update-slice, bf16[2048]{0:T(1024)(128)(2,1)S(1)} %dynamic-update-slice.1), channel_id=1, replica_groups=mesh['dp'=4,'cp'=8] {'dp','cp'}, use_global_device_ids=true, to_apply=%add | all-reduce | flops 4096 | bytes 16384
  53.7 21.8 all-gather.11.cloned.1.call-done
  81.8 57.2 %all-gather.13.cloned.1.call-done = bf16[2048,1024]{1,0:T(8,128)(2,1)} async-done(((bf16[64,1024]{1,0:T(8,128)(2,1)}), bf16[2048,1024]{1,0:T(8,128)(2,1)}) %all-gather.13.cloned.1.call-update) | async-done | bytes 4194320 | tf_op jit(solution)/shard_map/all_gather | solution.py:84
  153.8 23.0 all-gather.27.cloned.1.call-done
  182.0 75.0 %all-gather.17.cloned.1.call-done = bf16[2048,2048]{1,0:T(8,128)(2,1)} async-done(((bf16[64,2048]{1,0:T(8,128)(2,1)}), bf16[2048,2048]{1,0:T(8,128)(2,1)}) %all-gather.17.cloned.1.call-update) | async-done | bytes 8388624 | tf_op jit(solution)/shard_map/all_gather | solution.py:83
  275.9 19.5 all-gather.15.cloned.1.call-done
  295.3 16.4 fusion.84
  324.8 16.6 fusion.43
  341.4 34.1 all-gather.19.cloned.1.call-done
  383.2 188.6 %all-gather.23.cloned.1.call-done = bf16[2048,8192]{1,0:T(8,128)(2,1)} async-done(((bf16[64,8192]{1,0:T(8,128)(2,1)}), bf16[2048,8192]{1,0:T(8,128)(2,1)}) %all-gather.23.cloned.1.call-update) | async-done | bytes 33554448 | tf_op jit(solution)/shard_map/all_gather | solution.py:148
  571.8 18.5 fusion.86
  590.3 177.3 %all-gather.21.cloned.1.call-done = bf16[2048,8192]{1,0:T(8,128)(2,1)} async-done(((bf16[64,8192]{1,0:T(8,128)(2,1)}), bf16[2048,8192]{1,0:T(8,128)(2,1)}) %all-gather.21.cloned.1.call-update) | async-done | bytes 33554448 | tf_op jit(solution)/shard_map/all_gather | solution.py:147
  767.6 18.4 fusion.85
  786.0 177.5 %all-gather.25.cloned.1.call-done = bf16[8192,2048]{1,0:T(8,128)(2,1)} async-done(((bf16[256,2048]{1,0:T(8,128)(2,1)}), bf16[8192,2048]{1,0:T(8,128)(2,1)}) %all-gather.25.cloned.1.call-update) | async-done | bytes 33554448 | tf_op jit(solution)/shard_map/all_gather | solution.py:149
  963.5 23.6 multiply_convert_fusion
  987.1 17.3 fusion.87
  1004.4 18.7 multiply_reduce_fusion
  1052.1 19.2 fusion.17
  1071.3 46.5 %bitcast_convert_fusion.1 = bf16[8,128,2048]{2,1,0:T(8,128)(2,1)} fusion(bf16[256,8,2,128]{0,3,2,1:T(8,128)(2,1)} %bitcast.227, f32[8,2048,256,2]{2,1,3,0:T(8,128)} %fusion.17, f32[8,2,256,2048]{2,3,1,0:T(8,128)} %get-tuple-element.92, f32[8,2,256]{2,1,0:T(2,128)S(1)} %bitcast.233), kind=kOutput, calls=%fused_computation.19 | convolution fusion | flops 2208307200 | bytes 72368128 | tf_op jit(solution)/shard_map/while/body/eval_jaxpr/kgql,qkgd->lkd/dot_general | solution.py:194
  1124.6 43.1 %reduce-scatter.10.cloned.1.call-done = bf16[1,256,1024]{1,2,0:T(8,128)(2,1)} async-done(((bf16[1,2048,1024]{1,2,0:T(8,128)(2,1)}), bf16[1,256,1024]{1,2,0:T(8,128)(2,1)}) %reduce-scatter.10.cloned.1.call-update) | async-done | bytes 524304 | tf_op jit(solution)/shard_map/reduce_scatter | solution.py:214
  1185.6 44.4 %fusion.12 = f32[8,128,2,256]{3,1,2,0:T(8,128)S(1)} fusion(bf16[2048,8,128,1]{0,2,3,1:T(8,128)(2,1)} %bitcast.222, f32[8,2048,256,2]{2,1,3,0:T(8,128)} %fusion.17, f32[8,2,256,2048]{2,3,1,0:T(8,128)} %get-tuple-element.92, f32[8,2,256]{2,1,0:T(2,128)S(1)} %bitcast.234), kind=kOutput, calls=%fused_computation.17 | convolution fusion | flops 2206210048 | bytes 73416704 | tf_op jit(solution)/shard_map/while/body/eval_jaxpr/kgql,lkd->qkgd/dot_general | solution.py:191
  1241.7 25.9 fusion.51
  1268.8 25.8 fusion.90
  1295.0 25.7 fusion.89
  1330.2 17.6 fusion.26
  1354.3 41.4 %all-reduce.4 = (f32[2048]{0:T(1024)S(1)}, f32[2048]{0:T(1024)S(1)}) all-reduce(f32[2048]{0:T(1024)S(1)} %get-tuple-element.59, f32[2048]{0:T(1024)S(1)} %copy-done.25), channel_id=5, replica_groups=mesh['dp'=4,'cp'=8] {'dp','cp'}, use_global_device_ids=true, to_apply=%region_10.11.clone | all-reduce | flops 4096 | bytes 32768
  1400.4 61.1 %reduce-scatter.16.cloned.1.call-done = f32[64,1024]{1,0:T(8,128)} async-done(((f32[2048,1024]{1,0:T(8,128)}), f32[64,1024]{1,0:T(8,128)}) %reduce-scatter.16.cloned.1.call-update) | async-done | bytes 262160 | tf_op jit(solution)/shard_map/reduce_scatter | solution.py:241
  1461.4 187.4 %reduce-scatter.20.cloned.1.call-done = f32[64,2048]{1,0:T(8,128)} async-done(((f32[2048,2048]{1,0:T(8,128)}), f32[64,2048]{1,0:T(8,128)}) %reduce-scatter.20.cloned.1.call-update) | async-done | bytes 524304 | tf_op jit(solution)/shard_map/reduce_scatter | solution.py:243
  1648.9 187.2 %reduce-scatter.14.cloned.1.call-done = f32[64,2048]{1,0:T(8,128)} async-done(((f32[2048,2048]{1,0:T(8,128)}), f32[64,2048]{1,0:T(8,128)}) %reduce-scatter.14.cloned.1.call-update) | async-done | bytes 524304 | tf_op jit(solution)/shard_map/reduce_scatter | solution.py:240
  1836.1 712.2 %reduce-scatter.26.cloned.1.call-done = f32[256,2048]{1,0:T(8,128)} async-done(((f32[8192,2048]{1,0:T(8,128)}), f32[256,2048]{1,0:T(8,128)}) %reduce-scatter.26.cloned.1.call-update) | async-done | bytes 2097168 | tf_op jit(solution)/shard_map/reduce_scatter | solution.py:170
  2548.3 713.1 %reduce-scatter.24.cloned.1.call-done = f32[64,8192]{1,0:T(8,128)} async-done(((f32[2048,8192]{1,0:T(8,128)}), f32[64,8192]{1,0:T(8,128)}) %reduce-scatter.24.cloned.1.call-update) | async-done | bytes 2097168 | tf_op jit(solution)/shard_map/reduce_scatter | solution.py:169
  3261.4 713.0 %reduce-scatter.22.cloned.1.call-done = f32[64,8192]{1,0:T(8,128)} async-done(((f32[2048,8192]{1,0:T(8,128)}), f32[64,8192]{1,0:T(8,128)}) %reduce-scatter.22.cloned.1.call-update) | async-done | bytes 2097168 | tf_op jit(solution)/shard_map/reduce_scatter | solution.py:168
  (146 shorter events, 157.7 us)
Async XLA Ops:
  7.2 68.3 %all-gather.11.cloned.1.call-start = ((), (), s32[]{:S(2)}) async-start(), calls=%async_computation.9 | async-start | bytes 4325376 | tf_op jit(solution)/shard_map/all_gather | solution.py:85
  7.9 131.1 %all-gather.13.cloned.1.call-start = ((), (), s32[]{:S(2)}) async-start(), calls=%async_computation.10 | async-start | bytes 4325376 | tf_op jit(solution)/shard_map/all_gather | solution.py:84
  8.7 168.1 %all-gather.27.cloned.1.call-start = ((), (), s32[]{:S(2)}) async-start(), calls=%async_computation.26 | async-start | bytes 4718592 | tf_op jit(solution)/shard_map/all_gather | solution.py:117
  52.1 217.3 %copy-start.19 = (f32[2048]{0:T(1024)}, f32[2048]{0:T(1024)S(1)}, u32[]{:S(2)}) copy-start(f32[2048]{0:T(1024)S(1)} %convert_element_type.165) | copy-start | bytes 24580
  53.6 215.8 %copy-start.22 = (f32[256]{0:T(256)}, f32[256]{0:T(256)S(1)}, u32[]{:S(2)}) copy-start(f32[256]{0:T(256)S(1)} %add_rsqrt_fusion.1) | copy-start | bytes 3076
  80.1 176.9 %all-gather.17.cloned.1.call-start = ((), (), s32[]{:S(2)}) async-start(), calls=%async_computation.12 | async-start | bytes 8650752 | tf_op jit(solution)/shard_map/all_gather | solution.py:83
  80.7 214.7 %all-gather.15.cloned.1.call-start = ((), (), s32[]{:S(2)}) async-start(), calls=%async_computation.11 | async-start | bytes 4718592 | tf_op jit(solution)/shard_map/all_gather | solution.py:116
  81.1 194.4 %copy-start.12 = (f32[256,128]{0,1:T(8,128)}, f32[256,128]{0,1:T(8,128)S(1)}, u32[]{:S(2)}) copy-start(f32[256,128]{0,1:T(8,128)S(1)} %pad_maximum_fusion.1) | copy-start | bytes 393220
  139.0 6.6 copy-start
  150.6 225.0 %all-gather.19.cloned.1.call-start = ((), (), s32[]{:S(2)}) async-start(), calls=%async_computation.13 | async-start | bytes 8650752 | tf_op jit(solution)/shard_map/all_gather | solution.py:86
  151.1 420.6 %all-gather.23.cloned.1.call-start = ((), (), s32[]{:S(2)}) async-start(), calls=%async_computation.15 | async-start | bytes 34603008 | tf_op jit(solution)/shard_map/all_gather | solution.py:148
  151.9 615.7 %all-gather.21.cloned.1.call-start = ((), (), s32[]{:S(2)}) async-start(), calls=%async_computation.14 | async-start | bytes 34603008 | tf_op jit(solution)/shard_map/all_gather | solution.py:147
  152.6 810.8 %all-gather.25.cloned.1.call-start = ((), (), s32[]{:S(2)}) async-start(), calls=%async_computation.16 | async-start | bytes 34603008 | tf_op jit(solution)/shard_map/all_gather | solution.py:149
  153.4 964.5 %reduce-scatter.12.cloned.1.call-start = ((), (), s32[]{:S(2)}) async-start(), calls=%async_computation.18 | async-start | bytes 4718592 | tf_op jit(solution)/shard_map/reduce_scatter | solution.py:217
  275.8 35.9 copy-start.16
  381.7 622.7 %copy-start.4 = (f32[256,2048]{1,0:T(8,128)}, f32[256,2048]{1,0:T(8,128)S(1)}, u32[]{:S(2)}) copy-start(f32[256,2048]{1,0:T(8,128)S(1)} %get-tuple-element.94) | copy-start | bytes 6291460
  1026.1 150.0 %copy-start.2 = (f32[256,2048]{1,0:T(8,128)}, f32[256,2048]{1,0:T(8,128)S(1)}, u32[]{:S(2)}) copy-start(f32[256,2048]{1,0:T(8,128)S(1)} %multiply_add_fusion) | copy-start | bytes 6291460
  1051.9 115.8 %reduce-scatter.10.cloned.1.call-start = ((), (), s32[]{:S(2)}) async-start(), calls=%async_computation.17 | async-start | bytes 4718592 | tf_op jit(solution)/shard_map/reduce_scatter | solution.py:214
  1117.8 282.5 %reduce-scatter.18.cloned.1.call-start = ((), (), s32[]{:S(2)}) async-start(), calls=%async_computation.21 | async-start | bytes 8650752 | tf_op jit(solution)/shard_map/reduce_scatter | solution.py:242
  1124.5 45.5 %copy-start.18 = (f32[256,128]{0,1:T(8,128)S(1)}, f32[256,128]{0,1:T(8,128)}, u32[]{:S(2)}) copy-start(f32[256,128]{0,1:T(8,128)} %get-tuple-element.87) | copy-start | bytes 393220
  1124.5 46.5 %copy-start.13 = (f32[256,128]{0,1:T(8,128)S(1)}, f32[256,128]{0,1:T(8,128)}, u32[]{:S(2)}) copy-start(f32[256,128]{0,1:T(8,128)} %copy-done.12) | copy-start | bytes 393220
  1124.6 336.9 %reduce-scatter.16.cloned.1.call-start = ((), (), s32[]{:S(2)}) async-start(), calls=%async_computation.20 | async-start | bytes 8650752 | tf_op jit(solution)/shard_map/reduce_scatter | solution.py:241
  1175.9 473.0 %reduce-scatter.20.cloned.1.call-start = ((), (), s32[]{:S(2)}) async-start(), calls=%async_computation.22 | async-start | bytes 17301504 | tf_op jit(solution)/shard_map/reduce_scatter | solution.py:243
  1185.6 650.5 %reduce-scatter.14.cloned.1.call-start = ((), (), s32[]{:S(2)}) async-start(), calls=%async_computation.19 | async-start | bytes 17301504 | tf_op jit(solution)/shard_map/reduce_scatter | solution.py:240
  1240.5 1307.9 %reduce-scatter.26.cloned.1.call-start = ((), (), s32[]{:S(2)}) async-start(), calls=%async_computation.25 | async-start | bytes 69206016 | tf_op jit(solution)/shard_map/reduce_scatter | solution.py:170
  1267.6 1993.8 %reduce-scatter.24.cloned.1.call-start = ((), (), s32[]{:S(2)}) async-start(), calls=%async_computation.24 | async-start | bytes 69206016 | tf_op jit(solution)/shard_map/reduce_scatter | solution.py:169
  1294.7 2679.8 %reduce-scatter.22.cloned.1.call-start = ((), (), s32[]{:S(2)}) async-start(), calls=%async_computation.23 | async-start | bytes 69206016 | tf_op jit(solution)/shard_map/reduce_scatter | solution.py:168
  1322.8 7.4 copy-start.5
  1330.2 17.6 copy-start.9
  1330.2 17.6 copy-start.11
  1330.2 17.8 copy-start.6
  1351.3 45.6 %copy-start.3 = (f32[256,2048]{1,0:T(8,128)S(1)}, f32[256,2048]{1,0:T(8,128)}, u32[]{:S(2)}) copy-start(f32[256,2048]{1,0:T(8,128)} %copy-done.2) | copy-start | bytes 6291460
  (12 other events, 27.2 us)
Sparse Core Ops, SparseCore 0:
  10.9 64.5 all-gather.10
  78.3 60.6 all-gather.12
  141.5 35.2 all-gather.26
  179.5 77.4 all-gather.16
  259.3 36.0 all-gather.14
  298.0 77.4 all-gather.18
  378.4 193.3 all-gather.22
  574.6 192.9 all-gather.20
  770.5 192.9 all-gather.24
  1052.0 49.0 reduce-scatter.11
  1118.0 49.7 reduce-scatter.9
  1170.4 143.1 reduce-scatter.17
  1316.5 144.9 reduce-scatter.15
  1464.2 184.6 reduce-scatter.19
  1651.6 184.4 reduce-scatter.13
  1838.9 709.4 reduce-scatter.25
  2551.1 710.2 reduce-scatter.23
  3264.2 710.1 reduce-scatter.21
where the time goes:
time: 3990 us; the launch traced here: 3980 us
  waiting for transfers between devices  3400 us (85%)
  matrix products  420 us (11%)
  blocking collectives  83 us (2%)
    reduce_scatter x1, waiting for transfers between devices, shards(): lax.psum_scatter(grad_w_up, ('dp', 'cp'), scatter_dimension=0, tiled=True)  713 us
    reduce_scatter x1, waiting for transfers between devices, shards(): lax.psum_scatter(grad_w_gate, ('dp', 'cp'), scatter_dimension=0, tiled=True)  713 us
    reduce_scatter x1, waiting for transfers between devices, shards(): lax.psum_scatter(grad_down_w, ('dp', 'cp'), scatter_dimension=0, tiled=True)  712 us
    all_gather x1, waiting for transfers between devices, shards(): lax.all_gather(w_up, ('dp', 'cp'), axis=0, tiled=True)  189 us
    reduce_scatter x1, waiting for transfers between devices, shards(): lax.psum_scatter(grad_w_output, ('dp', 'cp'), scatter_dimension=0, tiled=...  187 us
    reduce_scatter x1, waiting for transfers between devices, shards(): lax.psum_scatter(grad_w_query, ('dp', 'cp'), scatter_dimension=0, tiled=T...  187 us
    all_gather x1, waiting for transfers between devices, shards(): lax.all_gather(w_down, ('dp', 'cp'), axis=0, tiled=True)  177 us
    all_gather x1, waiting for transfers between devices, shards(): lax.all_gather(w_gate, ('dp', 'cp'), axis=0, tiled=True)  177 us
  transfers between devices with their start and end apart: 18, of which 16 were waited for; matrix products, arithmetic and copies ran while one was open for 10% of the time, Pallas kernels for 0%

commit v1 on v0

v1 whole, which is shorter than its diff:
```python
import functools
import math

import jax
import jax.numpy as jnp
from jax import lax
from jax.experimental import pallas as pl
from jax.experimental.pallas import tpu as pltpu
from jax.sharding import PartitionSpec as P

H = 16
KVH = 8
HD = 128
EPS = 1e-05
THETA = 1000000.0
SCALE = HD ** (-0.5)
LOG2E = math.log2(math.e)
BF = jnp.bfloat16
F32 = jnp.float32
VMEM_LIMIT = 56 * 1024 * 1024

NN = (((1,), (0,)), ((), ()))
NT = (((1,), (1,)), ((), ()))
TN = (((0,), (0,)), ((), ()))


def mm(left, right, dims):
    return lax.dot_general(left, right, dims, preferred_element_type=F32)


def offset_of(position, count):
    half = count // 2
    return ((position % half) << 1) | (position // half)


def position_of(offset, count):
    return (offset >> 1) + (offset & 1) * (count // 2)


def swap(value, count, offset):
    return lax.ppermute(value, "cp", [(i, i ^ offset) for i in range(count)])


def gather_parts(part, count):
    half = part.shape[0] // 2
    if count == 8:
        by_x = swap(part, count, 2)
        by_y = swap(part, count, 4)
        inner = [part, by_x, by_y, swap(by_y[:half], count, 2), swap(by_x[half:], count, 4)]
    else:
        inner, bit = [part], 2
        while bit < count:
            inner = inner + [swap(item, count, bit) for item in inner]
            bit *= 2
    outer = [swap(item, count, 1) for item in inner]
    return inner + outer


def gather_rows(part, count):
    return jnp.concatenate(gather_parts(part, count), 0)


def scatter_rows(partial, count):
    total_rows, _ = partial.shape
    middle = total_rows // 2
    rows = total_rows // count
    half = rows // 2

    def plus(left, right):
        return (left.astype(F32) + right.astype(F32)).astype(BF)

    acc = plus(partial[:middle], swap(partial[middle:], count, 1))
    parts = [acc[i * rows : (i + 1) * rows] for i in range(count // 2)]
    if count == 8:
        own, to_x, to_y, far = parts
        from_x = swap(far[:half], count, 2)
        from_y = swap(far[half:], count, 4)
        send_x = jnp.concatenate([to_x[:half], plus(to_x[half:], from_y)], 0)
        send_y = jnp.concatenate([plus(to_y[:half], from_x), to_y[half:]], 0)
        got_x = swap(send_x, count, 2)
        got_y = swap(send_y, count, 4)
        return own.astype(F32) + got_x.astype(F32) + got_y.astype(F32)
    bit = count // 2
    while bit >= 2:
        keep, give = parts[: len(parts) // 2], parts[len(parts) // 2 :]
        parts = [plus(a, swap(b, count, bit)) for a, b in zip(keep, give)]
        bit //= 2
    return parts[0].astype(F32)


def trade(parts, count):
    return [
        part if offset_of(p, count) == 0 else swap(part, count, offset_of(p, count))
        for p, part in enumerate(parts)
    ]


def params(semantics):
    return pltpu.CompilerParams(dimension_semantics=semantics, vmem_limit_bytes=VMEM_LIMIT)


def cost(flops, nbytes, trans=0):
    return pl.CostEstimate(flops=int(flops), bytes_accessed=int(nbytes), transcendentals=int(trans))


def turn(value, cos, sin):
    return value * cos + pltpu.roll(value, HD // 2, 1) * sin


def qkv_kernel(z_ref, w_ref, cos_ref, sin_ref, q_ref, k_ref, v_ref, kt_ref, vt_ref, *, heads):
    cos, sin = cos_ref[...], sin_ref[...]
    flat = mm(z_ref[...], w_ref[...], NN)
    for h in range(heads):
        at = slice(h * HD, (h + 1) * HD)
        q_ref[:, at] = turn(flat[:, at], cos, sin).astype(BF)
    key = turn(flat[:, heads * HD : (heads + 1) * HD], cos, sin)
    value = flat[:, (heads + 1) * HD :]
    k_ref[...] = key.astype(BF)
    v_ref[...] = value.astype(BF)
    kt_ref[...] = key.T.astype(BF)
    vt_ref[...] = value.T.astype(BF)


def qkv_call(z_one, w_qkv, cos, sin, rows, heads):
    total, width = z_one.shape
    cols = w_qkv.shape[1]
    row = lambda i: (i, 0)
    col = lambda i: (0, i)
    whole = lambda i: (0, 0)
    return pl.pallas_call(
        functools.partial(qkv_kernel, heads=heads),
        grid=(total // rows,),
        in_specs=[
            pl.BlockSpec((rows, width), row),
            pl.BlockSpec((width, cols), whole),
            pl.BlockSpec((rows, HD), row),
            pl.BlockSpec((rows, HD), row),
        ],
        out_specs=[
            pl.BlockSpec((rows, heads * HD), row),
            pl.BlockSpec((rows, HD), row),
            pl.BlockSpec((rows, HD), row),
            pl.BlockSpec((HD, rows), col),
            pl.BlockSpec((HD, rows), col),
        ],
        out_shape=[
            jax.ShapeDtypeStruct((total, heads * HD), BF),
            jax.ShapeDtypeStruct((total, HD), BF),
            jax.ShapeDtypeStruct((total, HD), BF),
            jax.ShapeDtypeStruct((HD, total), BF),
            jax.ShapeDtypeStruct((HD, total), BF),
        ],
        compiler_params=params(("arbitrary",)),
        cost_estimate=cost(2 * total * width * cols, 2 * (total * width + width * cols)),
        name="qkv",
    )(z_one, w_qkv, cos, sin)


def stack_heads(block, heads):
    if heads == 1:
        return block
    return jnp.concatenate([block[:, h * HD : (h + 1) * HD] for h in range(heads)], 0)


def diagonal_mask(rows, heads):
    key_at = lax.broadcasted_iota(jnp.int32, (rows, rows), 0)
    query_at = lax.broadcasted_iota(jnp.int32, (rows, rows), 1)
    one = key_at <= query_at
    return one if heads == 1 else jnp.concatenate([one] * heads, 1)


def attend_kernel(me_ref, q_ref, k_ref, vt_ref, o_ref, lse_ref, *, heads, rows, count):
    i = pl.program_id(0)
    me = me_ref[0]
    wide = heads * rows
    queries = stack_heads(q_ref[...], heads)

    def step(j, carry, masked):
        top, total, acc = carry
        at = pl.multiple_of(position_of(j ^ me, count) * rows, rows)
        s = mm(k_ref[pl.ds(at, rows), :], queries, NT) * (SCALE * LOG2E)
        if masked:
            s = jnp.where(diagonal_mask(rows, heads), s, -1e30)
        new_top = jnp.maximum(top, jnp.max(s, 0, keepdims=True))
        fade = jnp.exp2(top - new_top)
        p = jnp.exp2(s - new_top)
        total = total * fade + jnp.sum(p, 0, keepdims=True)
        acc = acc * fade + mm(vt_ref[:, pl.ds(at, rows)], p.astype(BF), NN)
        return new_top, total, acc

    carry = (
        jnp.full((1, wide), -1e30, F32),
        jnp.zeros((1, wide), F32),
        jnp.zeros((HD, wide), F32),
    )
    carry = step(i, carry, True)
    top, total, acc = lax.fori_loop(0, i, lambda j, c: step(j, c, False), carry)
    out = (acc / total).T
    for h in range(heads):
        o_ref[:, h * HD : (h + 1) * HD] = out[h * rows : (h + 1) * rows, :].astype(BF)
    lse_ref[0] = top + jnp.log2(total)


def attend_call(me, q, k, vt, rows, heads, count):
    total = q.shape[0]
    slot = lambda i, me_ref: (position_of(i ^ me_ref[0], count), 0)
    slot3 = lambda i, me_ref: (position_of(i ^ me_ref[0], count), 0, 0)
    whole = lambda i, me_ref: (0, 0)
    return pl.pallas_call(
        functools.partial(attend_kernel, heads=heads, rows=rows, count=count),
        grid_spec=pltpu.PrefetchScalarGridSpec(
            num_scalar_prefetch=1,
            grid=(count,),
            in_specs=[
                pl.BlockSpec((rows, heads * HD), slot),
                pl.BlockSpec((total, HD), whole),
                pl.BlockSpec((HD, total), whole),
            ],
            out_specs=[
                pl.BlockSpec((rows, heads * HD), slot),
                pl.BlockSpec((1, 1, heads * rows), slot3),
            ],
        ),
        out_shape=[
            jax.ShapeDtypeStruct((total, heads * HD), BF),
            jax.ShapeDtypeStruct((count, 1, heads * rows), F32),
        ],
        compiler_params=params(("arbitrary",)),
        cost_estimate=cost(4 * total * total * heads * HD, 8 * total * HD, heads * total * total // 2),
        name="attend",
    )(me, q, k, vt)


def attend_back_kernel(
    me_ref,
    q_ref,
    g_ref,
    o_ref,
    lse_ref,
    k_ref,
    kt_ref,
    v_ref,
    cos_ref,
    sin_ref,
    out_ref,
    dk_ref,
    dv_ref,
    *,
    heads,
    rows,
    count,
):
    i = pl.program_id(0)
    me = me_ref[0]
    wide = heads * rows

    @pl.when(i == 0)
    def _():
        dk_ref[...] = jnp.zeros_like(dk_ref)
        dv_ref[...] = jnp.zeros_like(dv_ref)

    queries = stack_heads(q_ref[...], heads)
    grads = stack_heads(g_ref[...], heads)
    outs = stack_heads(o_ref[...], heads)
    lse = lse_ref[0]
    mixed = jnp.sum((outs.astype(F32) * grads.astype(F32)).T, 0, keepdims=True)

    def step(j, dqt, masked):
        at = pl.multiple_of(position_of(j ^ me, count) * rows, rows)
        here = pl.ds(at, rows)
        s = mm(k_ref[here, :], queries, NT) * (SCALE * LOG2E)
        p = jnp.exp2(s - lse)
        if masked:
            p = jnp.where(diagonal_mask(rows, heads), p, 0.0)
        gp = mm(v_ref[here, :], grads, NT)
        gs = (p * (gp - mixed) * SCALE).astype(BF)
        dv_ref[here, :] += mm(p.astype(BF), grads, NN)
        dk_ref[here, :] += mm(gs, queries, NN)
        return dqt + mm(kt_ref[:, here], gs, NN)

    dqt = step(i, jnp.zeros((HD, wide), F32), True)
    dqt = lax.fori_loop(0, i, lambda j, c: step(j, c, False), dqt)
    dq = dqt.T
    mine = pl.ds(pl.multiple_of(position_of(i ^ me, count) * rows, rows), rows)
    cos, sin = cos_ref[mine, :], sin_ref[mine, :]
    for h in range(heads):
        one = turn(dq[h * rows : (h + 1) * rows, :], cos, -sin)
        out_ref[mine, h * HD : (h + 1) * HD] = one.astype(BF)

    @pl.when(i == count - 1)
    def _():
        out_ref[:, heads * HD : (heads + 1) * HD] = turn(
            dk_ref[...], cos_ref[...], -sin_ref[...]
        ).astype(BF)
        out_ref[:, (heads + 1) * HD :] = dv_ref[...].astype(BF)


def attend_back_call(me, q, g, o, lse, k, kt, v, cos, sin, rows, heads, count):
    total = q.shape[0]
    slot = lambda i, me_ref: (position_of(i ^ me_ref[0], count), 0)
    slot3 = lambda i, me_ref: (position_of(i ^ me_ref[0], count), 0, 0)
    whole = lambda i, me_ref: (0, 0)
    cols = (heads + 2) * HD
    return pl.pallas_call(
        functools.partial(attend_back_kernel, heads=heads, rows=rows, count=count),
        grid_spec=pltpu.PrefetchScalarGridSpec(
            num_scalar_prefetch=1,
            grid=(count,),
            in_specs=[
                pl.BlockSpec((rows, heads * HD), slot),
                pl.BlockSpec((rows, heads * HD), slot),
                pl.BlockSpec((rows, heads * HD), slot),
                pl.BlockSpec((1, 1, heads * rows), slot3),
                pl.BlockSpec((total, HD), whole),
                pl.BlockSpec((HD, total), whole),
                pl.BlockSpec((total, HD), whole),
                pl.BlockSpec((total, HD), whole),
                pl.BlockSpec((total, HD), whole),
            ],
            out_specs=pl.BlockSpec((total, cols), whole),
            scratch_shapes=[pltpu.VMEM((total, HD), F32), pltpu.VMEM((total, HD), F32)],
        ),
        out_shape=jax.ShapeDtypeStruct((total, cols), BF),
        compiler_params=params(("arbitrary",)),
        cost_estimate=cost(10 * total * total * heads * HD, 16 * total * HD, heads * total * total // 2),
        name="attend_back",
    )(me, q, g, o, lse, k, kt, v, cos, sin)


def feed_kernel(z_ref, g_ref, w_ref, d_ref, act_ref, grads_ref):
    cut = d_ref.shape[0]
    z = z_ref[...]
    gate = mm(z, w_ref[:, :cut], NN)
    up = mm(z, w_ref[:, cut:], NN)
    back = mm(g_ref[...], d_ref[...], NT)
    sig = jax.nn.sigmoid(gate)
    silu = gate * sig
    act_ref[...] = (silu * up).astype(BF)
    grads_ref[:, :cut] = (back * up * (sig * (1.0 + gate * (1.0 - sig)))).astype(BF)
    grads_ref[:, cut:] = (back * silu).astype(BF)


def feed_call(z_two, g_out, w_gu, w_down, rows):
    total, width = z_two.shape
    cut = w_down.shape[0]
    row = lambda i: (i, 0)
    whole = lambda i: (0, 0)
    return pl.pallas_call(
        feed_kernel,
        grid=(total // rows,),
        in_specs=[
            pl.BlockSpec((rows, width), row),
            pl.BlockSpec((rows, width), row),
            pl.BlockSpec((width, 2 * cut), whole),
            pl.BlockSpec((cut, width), whole),
        ],
        out_specs=[pl.BlockSpec((rows, cut), row), pl.BlockSpec((rows, 2 * cut), row)],
        out_shape=[
            jax.ShapeDtypeStruct((total, cut), BF),
            jax.ShapeDtypeStruct((total, 2 * cut), BF),
        ],
        compiler_params=params(("arbitrary",)),
        cost_estimate=cost(6 * total * width * cut, 4 * total * width + 6 * cut * width + 6 * total * cut),
        name="feed",
    )(z_two, g_out, w_gu, w_down)


def sum_kernel(*refs, dims):
    *ins, out_ref = refs
    acc = None
    for a_ref, b_ref in zip(ins[0::2], ins[1::2]):
        term = mm(a_ref[...], b_ref[...], dims)
        acc = term if acc is None else acc + term
    out_ref[...] = acc.astype(out_ref.dtype)


def sum_call(pairs, dims, rows, name):
    total = pairs[0][0].shape[0]
    cols = pairs[0][1].shape[1 if dims is NN else 0]
    row = lambda i: (i, 0)
    whole = lambda i: (0, 0)
    specs, flat, depth = [], [], 0
    for a, b in pairs:
        specs += [pl.BlockSpec((rows, a.shape[1]), row), pl.BlockSpec(b.shape, whole)]
        flat += [a, b]
        depth += a.shape[1]
    return pl.pallas_call(
        functools.partial(sum_kernel, dims=dims),
        grid=(total // rows,),
        in_specs=specs,
        out_specs=pl.BlockSpec((rows, cols), row),
        out_shape=jax.ShapeDtypeStruct((total, cols), BF),
        compiler_params=params(("arbitrary",)),
        cost_estimate=cost(2 * total * cols * depth, 2 * (total * depth + depth * cols + total * cols)),
        name=name,
    )(*flat)


def rms_of(values):
    return lax.rsqrt(jnp.mean(values * values, -1, keepdims=True) + EPS)


def shards(
    inputs, attn_gain, w_query, w_key, w_value, w_output, ffn_gain, w_gate, w_up, w_down, cotangent
):
    _, rows, width = inputs.shape
    n_cp = lax.axis_size("cp")
    n_dp = lax.axis_size("dp")
    me = lax.axis_index("cp")
    heads = H // n_cp
    reps = n_cp // KVH
    total = rows * n_cp
    own = w_query.shape[0]
    hidden = w_gate.shape[1]
    unit = hidden // (n_dp * n_cp)
    halves = 2
    per_half = n_dp // halves
    me_arr = jnp.reshape(me, (1,)).astype(jnp.int32)
    gain_one = attn_gain.astype(F32)[:, None]
    gain_two = ffn_gain.astype(F32)[:, None]

    def gather_z(value):
        return lax.all_gather(value, "dp", axis=0, tiled=True)

    def scatter_z(value):
        return lax.psum_scatter(value, "dp", scatter_dimension=0, tiled=True)

    def give(value):
        return lax.all_to_all(value, "cp", 0, 0)

    scaled_q = (w_query.astype(F32) * gain_one).astype(BF).reshape(own, n_cp, heads * HD)
    scaled_k = (w_key.astype(F32) * gain_one).astype(BF).reshape(own, KVH, 1, HD)
    scaled_v = (w_value.astype(F32) * gain_one).astype(BF).reshape(own, KVH, 1, HD)
    spread = lambda v: jnp.broadcast_to(v, (own, KVH, reps, HD)).reshape(own, n_cp, HD)
    qkv_own = jnp.concatenate([scaled_q, spread(scaled_k), spread(scaled_v)], 2).transpose(1, 0, 2)
    qkv_cols = (heads + 2) * HD
    w_qkv = gather_z(give(qkv_own).reshape(n_cp * own, qkv_cols))

    devices = n_dp * n_cp
    moved = [(b, (b % n_dp) * n_cp + b // n_dp) for b in range(devices)]
    moved_back = [(b, a) for a, b in moved]
    wo_rows = gather_z(lax.ppermute(w_output, ("dp", "cp"), moved))

    w_down_full = gather_z(w_down)
    scaled_g = (w_gate.astype(F32) * gain_two).astype(BF).reshape(own, n_dp, n_cp, unit)
    scaled_u = (w_up.astype(F32) * gain_two).astype(BF).reshape(own, n_dp, n_cp, unit)
    cut = per_half * unit
    w_gu, w_dn = [], []
    for h in range(halves):
        at = slice(h * per_half, (h + 1) * per_half)
        both = jnp.concatenate([scaled_g[:, at], scaled_u[:, at]], 1)
        both = both.transpose(2, 0, 1, 3).reshape(n_cp, own, 2 * cut)
        w_gu.append(gather_z(give(both).reshape(n_cp * own, 2 * cut)))
        w_dn.append(w_down_full[h * cut : (h + 1) * cut])

    shard_at = jnp.array([offset_of(p, n_cp) for p in range(n_cp)], jnp.int32) ^ me
    positions = (shard_at[:, None] * rows + jnp.arange(rows, dtype=jnp.int32)[None, :]).reshape(-1)
    half_dim = HD // 2
    inv_freq = THETA ** (-(jnp.arange(half_dim, dtype=F32) * 2.0 / HD))
    angles = positions.astype(F32)[:, None] * inv_freq[None, :]
    cos_half, sin_half = jnp.cos(angles), jnp.sin(angles)
    cos = jnp.concatenate([cos_half, cos_half], -1)
    sin = jnp.concatenate([-sin_half, sin_half], -1)

    x = inputs.reshape(rows, width).astype(F32)
    rms_one = rms_of(x)
    z_one = x * rms_one
    z_one_all = gather_rows(z_one.astype(BF), n_cp)
    g_outb = cotangent.reshape(rows, width)
    g_out = g_outb.astype(F32)
    g_out_all = gather_rows(g_outb, n_cp)
    wo_rel = gather_rows(wo_rows, n_cp)

    q, k, v, kt, vt = qkv_call(z_one_all, w_qkv, cos, sin, rows, heads)
    mixed, lse = attend_call(me_arr, q, k, vt, rows, heads, n_cp)
    pieces = trade([mixed[p * rows : (p + 1) * rows] for p in range(n_cp)], n_cp)
    attn = jnp.concatenate(pieces, 1)
    hid = x + jnp.dot(attn, wo_rel, preferred_element_type=F32)
    rms_two = rms_of(hid)
    z_two = hid * rms_two
    z_two_all = gather_rows(z_two.astype(BF), n_cp)

    acts, gus, red_gu = [], [], []
    for h in range(halves):
        act, gu = feed_call(z_two_all, g_out_all, w_gu[h], w_dn[h], rows)
        acts.append(act)
        gus.append(gu)
        red_gu.append(scatter_z(mm(z_two_all, gu, TN).astype(BF)))
    chunks = 2
    u_parts = []
    for c in range(chunks):
        at = slice(c * width // chunks, (c + 1) * width // chunks)
        part = sum_call([(gus[h], w_gu[h][at]) for h in range(halves)], NT, rows, "g_two")
        u_parts.append(scatter_rows(part, n_cp))
    u = jnp.concatenate(u_parts, 1)
    grad_down = scatter_z(jnp.concatenate([mm(a, g_out_all, TN).astype(BF) for a in acts], 0))

    g_hidden = g_out + rms_two * (u - z_two * jnp.mean(u * z_two, -1, keepdims=True))
    g_hidb = g_hidden.astype(BF)
    g_attn = mm(g_hidb, wo_rel, NT).astype(BF)
    feat = heads * HD
    g_pieces = trade([g_attn[:, p * feat : (p + 1) * feat] for p in range(n_cp)], n_cp)
    g_mixed = jnp.concatenate(g_pieces, 0)
    g_qkv = attend_back_call(me_arr, q, g_mixed, mixed, lse, k, kt, v, cos, sin, rows, heads, n_cp)
    red_qkv = scatter_z(mm(z_one_all, g_qkv, TN).astype(BF))
    w_parts = []
    for c in range(chunks):
        at = slice(c * width // chunks, (c + 1) * width // chunks)
        part = sum_call([(g_qkv, w_qkv[at])], NT, rows, "g_one")
        w_parts.append(scatter_rows(part, n_cp))
    w_one = jnp.concatenate(w_parts, 1)
    grad_in = g_hidden + rms_one * (w_one - z_one * jnp.mean(w_one * z_one, -1, keepdims=True))

    out_part = sum_call([(acts[h], w_dn[h]) for h in range(halves)], NN, rows, "out")
    output = hid + scatter_rows(out_part, n_cp)
    wo_part = mm(attn, g_hidb, TN).astype(BF)
    wo_sum = scatter_z(scatter_rows(wo_part, n_cp).astype(BF))
    grad_output = lax.ppermute(wo_sum, ("dp", "cp"), moved_back).astype(F32)

    got = give(red_qkv.reshape(n_cp, own, qkv_cols)).astype(F32)
    raw_q = got[:, :, : heads * HD].transpose(1, 0, 2).reshape(own, H * HD)
    fold = lambda v: v.reshape(KVH, reps, own, HD).sum(1).transpose(1, 0, 2).reshape(own, KVH * HD)
    raw_k = fold(got[:, :, heads * HD : (heads + 1) * HD])
    raw_v = fold(got[:, :, (heads + 1) * HD :])
    grad_attn_gain = (
        jnp.sum(raw_q * w_query.astype(F32), 1)
        + jnp.sum(raw_k * w_key.astype(F32), 1)
        + jnp.sum(raw_v * w_value.astype(F32), 1)
    )
    back_gu = jnp.stack([give(r.reshape(n_cp, own, 2 * cut)) for r in red_gu], 0)
    back_gu = back_gu.reshape(halves, n_cp, own, 2, per_half, unit).transpose(3, 2, 0, 4, 1, 5)
    back_gu = back_gu.reshape(2, own, hidden).astype(F32)
    raw_g, raw_u = back_gu[0], back_gu[1]
    grad_ffn_gain = jnp.sum(raw_g * w_gate.astype(F32), 1) + jnp.sum(raw_u * w_up.astype(F32), 1)

    return (
        output[None],
        grad_in[None],
        grad_attn_gain,
        raw_q * gain_one,
        raw_k * gain_one,
        raw_v * gain_one,
        grad_output,
        grad_ffn_gain,
        raw_g * gain_two,
        raw_u * gain_two,
        grad_down.astype(F32),
    )


def solution(mesh):
    both = ("dp", "cp")
    rows = P("dp", "cp", None)
    mat = P(both, None)
    vec = P(both)
    return jax.shard_map(
        shards,
        mesh=mesh,
        in_specs=(rows, vec, mat, mat, mat, mat, vec, mat, mat, mat, rows),
        out_specs=(rows, rows, vec, mat, mat, mat, mat, vec, mat, mat, mat),
        check_vma=False,
    )
```

time: 3990 us -> 802 us (0.20)
  waiting for transfers between devices: 3400 us -> 218 us
  matrix products: 420 us -> 68.6 us
  Pallas kernels: 0 us -> 154 us
  starting transfers between devices: 1.36 us -> 104 us
  local copies, waits for them, and re-layouts: 34.5 us -> 120 us
  blocking collectives: 83 us -> 40.5 us
    reduce_scatter x9 -> x5, waiting for transfers between devices: 2620 us -> 0.05 us  [scatter_z(): return lax.psum_scatter(value, 'dp', scatter_dimension=0, tiled=True)]
    all_gather x9 -> x5, waiting for transfers between devices: 774 us -> 0.02 us  [gather_z(): return lax.all_gather(value, 'dp', axis=0, tiled=True)]
    dot_general x27 -> x8, matrix products: 420 us -> 68.6 us  [the longest x7 62.7 us: mm(): return lax.dot_general(left, right, dims, preferred_element_type=F32)]
    pallas_call x0 -> x10, Pallas kernels: none -> 154 us  [the longest x5 59 us: sum_call(): pl.pallas_call(functools.partial(sum_kernel, dims=dims), grid=(total // r...]
    ppermute x0 -> x82, waiting for transfers between devices: none -> 147 us  [the longest x80 128 us: swap(): return lax.ppermute(value, 'cp', [(i, i ^ offset) for i in range(count)])]
    unnamed x2 -> x0, blocking collectives: 83 us -> none
    ppermute x0 -> x82, starting transfers between devices: none -> 78.3 us  [the longest x80 68.5 us: swap(): return lax.ppermute(value, 'cp', [(i, i ^ offset) for i in range(count)])]
    all_to_all x0 -> x4, waiting for transfers between devices: none -> 69.6 us  [give(): return lax.all_to_all(value, 'cp', 0, 0)]
  transfers between devices with their start and end apart: 18 -> 96, of which waited for: 16 -> 30; matrix products, arithmetic and copies ran while one was open for 10% -> 32% of each run, Pallas kernels for 0% -> 19%
where the time goes in v1:
time: 802 us; the launch traced here: 792 us
  waiting for transfers between devices  218 us (27%)
  Pallas kernels  154 us (19%)
  local copies, waits for them, and re-layouts  120 us (15%)
  starting transfers between devices  104 us (13%)
  other arithmetic  71.2 us (9%)
  matrix products  68.6 us (9%)
  blocking collectives  40.5 us (5%)
  between operations  15.9 us (2%)
    ppermute x80, waiting for transfers between devices, swap(): return lax.ppermute(value, 'cp', [(i, i ^ offset) for i in range(count)])  128 us
    all_to_all x4, waiting for transfers between devices, give(): return lax.all_to_all(value, 'cp', 0, 0)  69.6 us
    ppermute x80, starting transfers between devices, swap(): return lax.ppermute(value, 'cp', [(i, i ^ offset) for i in range(count)])  68.5 us
    dot_general x7, matrix products, mm(): return lax.dot_general(left, right, dims, preferred_element_type=F32)  62.7 us
    unnamed x149, local copies, waits for them, and re-layouts  61.5 us
    pallas_call x5, Pallas kernels, sum_call(): pl.pallas_call(functools.partial(sum_kernel, dims=dims), grid=(total // r...  59 us
    all_to_all x2, blocking collectives, give(): return lax.all_to_all(value, 'cp', 0, 0)  40.5 us
    pallas_call x2, Pallas kernels, feed_call(): pl.pallas_call(feed_kernel, grid=(total // rows,), in_specs=[pl.BlockSpec...  38.3 us
  transfers between devices with their start and end apart: 96, of which 30 were waited for; matrix products, arithmetic and copies ran while one was open for 32% of the time, Pallas kernels for 19%

profile of v1, /device:TPU:1, one launch (start us, length us, event | category | flops | bytes accessed | tf_op | source)
XLA Modules:
  0.0 792.0 jit_solution(13537589457093269064)
XLA Ops:
  19.9 22.1 %all_to_all.30 = bf16[8,64,512]{2,1,0:T(8,128)(2,1)} all-to-all(bf16[8,64,512]{2,1,0:T(8,128)(2,1)S(1)} %maximum_bitcast_fusion.2), channel_id=1, replica_groups=mesh['dp'=4,'cp'=8] {'cp'}, dimensions={0} | all-to-all | bytes 1048576 | tf_op jit(solution)/shard_map/all_to_all | solution.py:429
  46.4 18.5 %all_to_all.31 = bf16[8,64,1024]{2,1,0:T(8,128)(2,1)} all-to-all(bf16[8,64,1024]{2,1,0:T(8,128)(2,1)S(1)} %reshape.145), channel_id=1, replica_groups=mesh['dp'=4,'cp'=8] {'cp'}, dimensions={0} | all-to-all | bytes 2097152 | tf_op jit(solution)/shard_map/all_to_all | solution.py:429
  85.8 38.5 %all-to-all-done.2 = bf16[8,64,1024]{2,1,0:T(8,128)(2,1)S(1)} async-done(((bf16[8,64,1024]{2,1,0:T(8,128)(2,1)}), bf16[8,64,1024]{2,1,0:T(8,128)(2,1)S(1)}, u32[]{:S(2)}, u32[]{:S(2)}) %all-to-all-start.2) | async-done | bytes 1048608 | tf_op jit(solution)/shard_map/all_to_all | solution.py:429
  165.5 11.5 %collective-permute-done.18 = bf16[256,2048]{1,0:T(8,128)(2,1)S(1)} collective-permute-done((bf16[256,2048]{1,0:T(8,128)(2,1)}, bf16[256,2048]{1,0:T(8,128)(2,1)S(1)}, u32[]{:S(2)}, u32[]{:S(2)}) %collective-permute-start.18) | collective-permute-done | bytes 1048608 | tf_op jit(solution)/shard_map/ppermute | solution.py:41
  183.5 7.3 collective-permute-done.19
  194.4 11.5 %qkv.1 = (bf16[2048,256]{1,0:T(8,128)(2,1)}, bf16[2048,128]{1,0:T(8,128)(2,1)}, bf16[2048,128]{1,0:T(8,128)(2,1)}, bf16[128,2048]{1,0:T(8,128)(2,1)}, bf16[128,2048]{1,0:T(8,128)(2,1)}) custom-call(bf16[2048,2048]{1,0:T(8,128)(2,1)} %constant_dynamic-update-slice_fusion.z_ref, bf16[2048,512]{1,0:T(8,128)(2,1)} %all-gather.6.cloned.1.call-done.w_ref, ...), custom_call_target="tpu_custom_call" | custom-call | flops 4294967296 | bytes 10485760 | tf_op jit(solution)/shard_map/qkv/pallas_call | solution.py:130
  206.0 21.6 %attend.1 = (bf16[2048,256]{1,0:T(8,128)(2,1)}, f32[8,1,512]{2,1,0:T(1,128)}) custom-call(s32[1]{0:T(128)} %bitcast.1.me_ref, bf16[2048,256]{1,0:T(8,128)(2,1)} %get-tuple-element.22.q_ref, bf16[2048,128]{1,0:T(8,128)(2,1)} %get-tuple-element.23.k_ref, bf16[128,2048]{1,0:T(8,128)(2,1)} %get-tuple-element.24.vt_ref), custom_call_target="tpu_custom_call" | custom-call | flops 4294967296 | bytes 2097152 | tf_op jit(solution)/shard_map/attend/pallas_call | solution.py:209
  276.6 16.2 %collective-permute-done.27 = bf16[256,2048]{1,0:T(8,128)(2,1)S(1)} collective-permute-done((bf16[256,2048]{1,0:T(8,128)(2,1)S(1)}, bf16[256,2048]{1,0:T(8,128)(2,1)S(1)}, u32[]{:S(2)}, u32[]{:S(2)}) %collective-permute-start.27) | collective-permute-done | bytes 1048608 | tf_op jit(solution)/shard_map/ppermute | solution.py:41
  299.0 6.1 collective-permute-done.28
  319.3 19.2 %feed.2 = (bf16[2048,512]{1,0:T(8,128)(2,1)}, bf16[2048,1024]{1,0:T(8,128)(2,1)}) custom-call(bf16[2048,2048]{1,0:T(8,128)(2,1)} %constant_dynamic-update-slice_fusion.27.z_ref, bf16[2048,2048]{1,0:T(8,128)(2,1)} %constant_dynamic-update-slice_fusion.37.g_ref, bf16[2048,1024]{1,0:T(8,128)(2,1)} %all-gather.10.cloned.1.call-done.w_ref, ...), custom_call_target="tpu_custom_call" | custom-call | flops 12884901888 | bytes 29360128 | tf_op jit(solution)/shard_map/feed/pallas_call | solution.py:348
  338.4 14.2 %convolution_convert_fusion.2 = bf16[2048,1024]{1,0:T(8,128)(2,1)} fusion(bf16[2048,2048]{1,0:T(8,128)(2,1)} %constant_dynamic-update-slice_fusion.27.z_ref, bf16[2048,1024]{1,0:T(8,128)(2,1)} %get-tuple-element.28.refs_0_), kind=kOutput, calls=%fused_computation.10 | convolution fusion | flops 8592031744 | bytes 16777216 | tf_op jit(solution)/shard_map/dot_general | solution.py:28
  352.7 19.2 %feed.3 = (bf16[2048,512]{1,0:T(8,128)(2,1)}, bf16[2048,1024]{1,0:T(8,128)(2,1)}) custom-call(bf16[2048,2048]{1,0:T(8,128)(2,1)} %constant_dynamic-update-slice_fusion.27.z_ref, bf16[2048,2048]{1,0:T(8,128)(2,1)} %constant_dynamic-update-slice_fusion.37.g_ref, bf16[2048,1024]{1,0:T(8,128)(2,1)} %all-gather.14.cloned.1.call-done.w_ref, ...), custom_call_target="tpu_custom_call" | custom-call | flops 12884901888 | bytes 29360128 | tf_op jit(solution)/shard_map/feed/pallas_call | solution.py:348
  371.9 8.7 %convolution_convert_fusion.3 = bf16[512,2048]{1,0:T(8,128)(2,1)S(1)} fusion(bf16[2048,512]{1,0:T(8,128)(2,1)} %get-tuple-element.27.refs_2_, bf16[2048,2048]{1,0:T(8,128)(2,1)} %constant_dynamic-update-slice_fusion.37.g_ref), kind=kOutput, calls=%fused_computation.14 | convolution fusion | flops 4296015872 | bytes 12582912 | tf_op jit(solution)/shard_map/dot_general | solution.py:28
  380.7 8.2 %convolution_convert_fusion.4 = bf16[512,2048]{1,0:T(8,128)(2,1)S(1)} fusion(bf16[2048,512]{1,0:T(8,128)(2,1)S(1)} %copy-done.43, bf16[2048,2048]{1,0:T(8,128)(2,1)} %constant_dynamic-update-slice_fusion.37.g_ref), kind=kOutput, calls=%fused_computation.15 | convolution fusion | flops 4296015872 | bytes 12582912 | tf_op jit(solution)/shard_map/dot_general | solution.py:28
  391.4 14.5 %out.1 = bf16[2048,2048]{1,0:T(8,128)(2,1)} custom-call(bf16[2048,512]{1,0:T(8,128)(2,1)} %get-tuple-element.26.refs_0_, bf16[512,2048]{1,0:T(8,128)(2,1)} %get-tuple-element.56.d_ref.refs_1_, bf16[2048,512]{1,0:T(8,128)(2,1)} %get-tuple-element.27.refs_2_, bf16[512,2048]{1,0:T(8,128)(2,1)} %get-tuple-element.55.d_ref.refs_3_), custom_call_target="tpu_custom_call" | custom-call | flops 8589934592 | bytes 16777216 | tf_op jit(solution)/shard_map/out/pallas_call | solution.py:387
  417.0 14.1 %g_two.2 = bf16[2048,1024]{1,0:T(8,128)(2,1)} custom-call(bf16[2048,1024]{1,0:T(8,128)(2,1)} %get-tuple-element.28.refs_0_, bf16[1024,1024]{1,0:T(8,128)(2,1)} %get-tuple-element.47.refs_1_, bf16[2048,1024]{1,0:T(8,128)(2,1)} %get-tuple-element.29.refs_2_, bf16[1024,1024]{1,0:T(8,128)(2,1)} %get-tuple-element.45.refs_3_), custom_call_target="tpu_custom_call" | custom-call | flops 8589934592 | bytes 16777216 | tf_op jit(solution)/shard_map/g_two/pallas_call | solution.py:387
  434.1 14.1 %g_two.3 = bf16[2048,1024]{1,0:T(8,128)(2,1)} custom-call(bf16[2048,1024]{1,0:T(8,128)(2,1)} %get-tuple-element.28.refs_0_, bf16[1024,1024]{1,0:T(8,128)(2,1)} %get-tuple-element.48.refs_1_, bf16[2048,1024]{1,0:T(8,128)(2,1)} %get-tuple-element.29.refs_2_, bf16[1024,1024]{1,0:T(8,128)(2,1)} %get-tuple-element.46.refs_3_), custom_call_target="tpu_custom_call" | custom-call | flops 8589934592 | bytes 16777216 | tf_op jit(solution)/shard_map/g_two/pallas_call | solution.py:387
  451.9 12.8 %convolution_convert_fusion.1 = bf16[2048,1024]{1,0:T(8,128)(2,1)} fusion(bf16[2048,2048]{1,0:T(8,128)(2,1)} %constant_dynamic-update-slice_fusion.27.z_ref, bf16[2048,1024]{1,0:T(8,128)(2,1)S(1)} %copy-done.44), kind=kOutput, calls=%fused_computation.9 | convolution fusion | flops 8592031744 | bytes 16777216 | tf_op jit(solution)/shard_map/dot_general | solution.py:28
  486.5 8.0 %collective-permute-done.45 = bf16[128,2048]{1,0:T(8,128)(2,1)S(1)} collective-permute-done((bf16[128,2048]{1,0:T(8,128)(2,1)S(1)}, bf16[128,2048]{1,0:T(8,128)(2,1)S(1)}, u32[]{:S(2)}, u32[]{:S(2)}) %collective-permute-start.45) | collective-permute-done | bytes 524320 | tf_op jit(solution)/shard_map/ppermute | solution.py:41
  494.5 10.5 %collective-permute-done.47 = bf16[128,2048]{1,0:T(8,128)(2,1)S(1)} collective-permute-done((bf16[128,2048]{1,0:T(8,128)(2,1)S(1)}, bf16[128,2048]{1,0:T(8,128)(2,1)S(1)}, u32[]{:S(2)}, u32[]{:S(2)}) %collective-permute-start.47) | collective-permute-done | bytes 524320 | tf_op jit(solution)/shard_map/ppermute | solution.py:41
  509.0 7.2 collective-permute-done.56
  517.5 21.2 %collective-permute-done.46 = bf16[256,2048]{1,0:T(8,128)(2,1)S(1)} collective-permute-done((bf16[256,2048]{1,0:T(8,128)(2,1)S(1)}, bf16[256,2048]{1,0:T(8,128)(2,1)S(1)}, u32[]{:S(2)}, u32[]{:S(2)}) %collective-permute-start.46) | collective-permute-done | bytes 1048608 | tf_op jit(solution)/shard_map/ppermute | solution.py:41
  543.2 6.6 convolution_convert_fusion.6
  575.6 23.9 %attend_back.1.refs_0_ = bf16[2048,512]{1,0:T(8,128)(2,1)} custom-call(s32[1]{0:T(128)} %bitcast.1.me_ref, bf16[2048,256]{1,0:T(8,128)(2,1)} %get-tuple-element.22.q_ref, bf16[2048,256]{1,0:T(8,128)(2,1)} %copy-done.35, bf16[2048,256]{1,0:T(8,128)(2,1)} %get-tuple-element.25.o_ref, f32[8,1,512]{2,1,0:T(1,128)} %get-tuple-element.30.lse_ref, ...), custom_call_target="tpu_custom_call" | custom-call | flops 10737418240 | bytes 4194304 | tf_op jit(solution)/shard_map/attend_back/pallas_call | solution.py:304
  599.5 8.1 %g_one.2 = bf16[2048,1024]{1,0:T(8,128)(2,1)} custom-call(bf16[2048,512]{1,0:T(8,128)(2,1)} %attend_back.1.refs_0_, bf16[1024,512]{1,0:T(8,128)(2,1)} %get-tuple-element.67.refs_1_), custom_call_target="tpu_custom_call" | custom-call | flops 2147483648 | bytes 7340032 | tf_op jit(solution)/shard_map/g_one/pallas_call | solution.py:387
  610.1 8.2 %g_one.3 = bf16[2048,1024]{1,0:T(8,128)(2,1)} custom-call(bf16[2048,512]{1,0:T(8,128)(2,1)} %attend_back.1.refs_0_, bf16[1024,512]{1,0:T(8,128)(2,1)} %get-tuple-element.68.refs_1_), custom_call_target="tpu_custom_call" | custom-call | flops 2147483648 | bytes 7340032 | tf_op jit(solution)/shard_map/g_one/pallas_call | solution.py:387
  621.4 9.5 %convolution_convert_fusion.5 = bf16[2048,512]{1,0:T(8,128)(2,1)} fusion(bf16[2048,2048]{1,0:T(8,128)(2,1)} %constant_dynamic-update-slice_fusion.z_ref, bf16[2048,512]{1,0:T(8,128)(2,1)S(1)} %copy-done.42), kind=kOutput, calls=%fused_computation.16 | convolution fusion | flops 4296015872 | bytes 12582912 | tf_op jit(solution)/shard_map/dot_general | solution.py:28
  659.2 11.3 %collective-permute-done.79 = bf16[128,2048]{1,0:T(8,128)(2,1)S(1)} collective-permute-done((bf16[128,2048]{1,0:T(8,128)(2,1)S(1)}, bf16[128,2048]{1,0:T(8,128)(2,1)S(1)}, u32[]{:S(2)}, u32[]{:S(2)}) %collective-permute-start.79) | collective-permute-done | bytes 524320 | tf_op jit(solution)/shard_map/ppermute | solution.py:41
  674.6 7.8 all-to-all-start.4
  689.8 27.4 %all-to-all-done.4 = bf16[8,64,1024]{2,1,0:T(8,128)(2,1)} async-done(((bf16[8,64,1024]{2,1,0:T(8,128)(2,1)}), bf16[8,64,1024]{2,1,0:T(8,128)(2,1)}, u32[]{:S(2)}, u32[]{:S(2)}) %all-to-all-start.4) | async-done | bytes 1048608 | tf_op jit(solution)/shard_map/all_to_all | solution.py:429
  745.4 7.7 all-to-all-start.3
  768.9 15.0 %collective-permute-done.81 = bf16[64,2048]{1,0:T(8,128)(2,1)S(1)} collective-permute-done((bf16[64,2048]{1,0:T(8,128)(2,1)}, bf16[64,2048]{1,0:T(8,128)(2,1)S(1)}, u32[]{:S(2)}, u32[]{:S(2)}) %collective-permute-start.81) | collective-permute-done | bytes 262176 | tf_op jit(solution)/shard_map/ppermute | solution.py:518
  (451 shorter events, 325.8 us)
Async XLA Ops:
  7.2 144.7 %all-gather.8.cloned.1.call-start = ((), (), s32[]{:S(2)}) async-start(), calls=%async_computation.12 | async-start | bytes 1310720 | tf_op jit(solution)/shard_map/all_gather | solution.py:423
  16.9 177.5 %all-gather.6.cloned.1.call-start = ((), (), s32[]{:S(2)}) async-start(), calls=%async_computation.11 | async-start | bytes 2621440 | tf_op jit(solution)/shard_map/all_gather | solution.py:423
  42.0 272.4 %all-gather.12.cloned.1.call-start = ((), (), s32[]{:S(2)}) async-start(), calls=%async_computation.14 | async-start | bytes 5242880 | tf_op jit(solution)/shard_map/all_gather | solution.py:423
  42.8 276.5 %all-gather.10.cloned.1.call-start = ((), (), s32[]{:S(2)}) async-start(), calls=%async_computation.13 | async-start | bytes 5242880 | tf_op jit(solution)/shard_map/all_gather | solution.py:423
  66.8 61.6 %collective-permute-start = (bf16[256,2048]{1,0:T(8,128)(2,1)}, bf16[256,2048]{1,0:T(8,128)(2,1)}, u32[]{:S(2)}, u32[]{:S(2)}) collective-permute-start(bf16[256,2048]{1,0:T(8,128)(2,1)} %get-tuple-element.36), channel_id=1, source_target_pairs={{0,2},{1,3},{2,0},{3,1},{4,6},{5,7},{6,4},{7,5},{8,10},{9,11},{10,... | collective-permute-start | bytes 3145736 | tf_op jit(solution)/shard_map/ppermute | solution.py:41
  67.8 57.6 %collective-permute-start.1 = (bf16[256,2048]{1,0:T(8,128)(2,1)}, bf16[256,2048]{1,0:T(8,128)(2,1)}, u32[]{:S(2)}, u32[]{:S(2)}) collective-permute-start(bf16[256,2048]{1,0:T(8,128)(2,1)} %get-tuple-element.36), channel_id=1, source_target_pairs={{0,4},{1,5},{2,6},{3,7},{4,0},{5,1},{6,2},{7,3},{8,12},{9,13},{10,... | collective-permute-start | bytes 3145736 | tf_op jit(solution)/shard_map/ppermute | solution.py:41
  67.9 81.7 %collective-permute-start.4 = (bf16[256,2048]{1,0:T(8,128)(2,1)}, bf16[256,2048]{1,0:T(8,128)(2,1)}, u32[]{:S(2)}, u32[]{:S(2)}) collective-permute-start(bf16[256,2048]{1,0:T(8,128)(2,1)} %get-tuple-element.36), channel_id=1, source_target_pairs={{0,1},{1,0},{2,3},{3,2},{4,5},{5,4},{6,7},{7,6},{8,9},{9,8},{10,11... | collective-permute-start | bytes 3145736 | tf_op jit(solution)/shard_map/ppermute | solution.py:41
  69.2 67.1 %collective-permute-start.35 = (bf16[256,2048]{1,0:T(8,128)(2,1)}, bf16[256,2048]{1,0:T(8,128)(2,1)}, u32[]{:S(2)}, u32[]{:S(2)}) collective-permute-start(bf16[256,2048]{1,0:T(8,128)(2,1)} %bitcast.5), channel_id=1, source_target_pairs={{0,2},{1,3},{2,0},{3,1},{4,6},{5,7},{6,4},{7,5},{8,10},{9,11},{10,... | collective-permute-start | bytes 3145736 | tf_op jit(solution)/shard_map/ppermute | solution.py:41
  70.4 59.3 %collective-permute-start.36 = (bf16[256,2048]{1,0:T(8,128)(2,1)}, bf16[256,2048]{1,0:T(8,128)(2,1)}, u32[]{:S(2)}, u32[]{:S(2)}) collective-permute-start(bf16[256,2048]{1,0:T(8,128)(2,1)} %bitcast.5), channel_id=1, source_target_pairs={{0,4},{1,5},{2,6},{3,7},{4,0},{5,1},{6,2},{7,3},{8,12},{9,13},{10,... | collective-permute-start | bytes 3145736 | tf_op jit(solution)/shard_map/ppermute | solution.py:41
  73.6 50.7 %all-to-all-start.2 = ((bf16[8,64,1024]{2,1,0:T(8,128)(2,1)}), bf16[8,64,1024]{2,1,0:T(8,128)(2,1)S(1)}, u32[]{:S(2)}, u32[]{:S(2)}) async-start(bf16[8,64,1024]{2,1,0:T(8,128)(2,1)} %reshape.147), calls=%async_computation.2 | async-start | bytes 2097152 | tf_op jit(solution)/shard_map/all_to_all | solution.py:429
  77.6 275.2 %all-gather.14.cloned.1.call-start = ((), (), s32[]{:S(2)}) async-start(), calls=%async_computation.15 | async-start | bytes 5242880 | tf_op jit(solution)/shard_map/all_gather | solution.py:423
  125.2 549.4 %reduce-scatter.10.cloned.1.call-start = ((), (), s32[]{:S(2)}) async-start(), calls=%async_computation.18 | async-start | bytes 5242880 | tf_op jit(solution)/shard_map/reduce_scatter | solution.py:426
  160.7 109.0 %collective-permute-start.39 = (bf16[256,2048]{1,0:T(8,128)(2,1)}, bf16[256,2048]{1,0:T(8,128)(2,1)}, u32[]{:S(2)}, u32[]{:S(2)}) collective-permute-start(bf16[256,2048]{1,0:T(8,128)(2,1)} %bitcast.5), channel_id=1, source_target_pairs={{0,1},{1,0},{2,3},{3,2},{4,5},{5,4},{6,7},{7,6},{8,9},{9,8},{10,11... | collective-permute-start | bytes 3145736 | tf_op jit(solution)/shard_map/ppermute | solution.py:41
  163.1 66.4 %collective-permute-start.21 = (bf16[256,2048]{1,0:T(8,128)(2,1)}, bf16[256,2048]{1,0:T(8,128)(2,1)}, u32[]{:S(2)}, u32[]{:S(2)}) collective-permute-start(bf16[256,2048]{1,0:T(8,128)(2,1)} %all-gather.8.cloned.1.call-done), channel_id=1, source_target_pairs={{0,1},{1,0},{2,3},{3,2},{4,5},{5,4},{6,7},{7,6},{8,9},{9,8},{10,11... | collective-permute-start | bytes 3145736 | tf_op jit(solution)/shard_map/ppermute | solution.py:41
  179.9 73.0 %collective-permute-start.22 = (bf16[256,2048]{1,0:T(8,128)(2,1)S(1)}, bf16[256,2048]{1,0:T(8,128)(2,1)}, u32[]{:S(2)}, u32[]{:S(2)}) collective-permute-start(bf16[256,2048]{1,0:T(8,128)(2,1)S(1)} %collective-permute-done.17), channel_id=1, source_target_pairs={{0,1},{1,0},{2,3},{3,2},{4,5},{5,4},{6,7},{7,6},{8,9},{9,8},{10,11... | collective-permute-start | bytes 3145736 | tf_op jit(solution)/shard_map/ppermute | solution.py:41
  190.8 64.9 %collective-permute-start.23 = (bf16[256,2048]{1,0:T(8,128)(2,1)S(1)}, bf16[256,2048]{1,0:T(8,128)(2,1)}, u32[]{:S(2)}, u32[]{:S(2)}) collective-permute-start(bf16[256,2048]{1,0:T(8,128)(2,1)S(1)} %collective-permute-done.18), channel_id=1, source_target_pairs={{0,1},{1,0},{2,3},{3,2},{4,5},{5,4},{6,7},{7,6},{8,9},{9,8},{10,11... | collective-permute-start | bytes 3145736 | tf_op jit(solution)/shard_map/ppermute | solution.py:41
  276.1 33.4 %collective-permute-start.30 = (bf16[256,2048]{1,0:T(8,128)(2,1)S(1)}, bf16[256,2048]{1,0:T(8,128)(2,1)S(1)}, u32[]{:S(2)}, u32[]{:S(2)}) collective-permute-start(bf16[256,2048]{1,0:T(8,128)(2,1)S(1)} %get-tuple-element.34), channel_id=1, source_target_pairs={{0,1},{1,0},{2,3},{3,2},{4,5},{5,4},{6,7},{7,6},{8,9},{9,8},{10,11... | collective-permute-start | bytes 3145736 | tf_op jit(solution)/shard_map/ppermute | solution.py:41
  352.7 329.8 %reduce-scatter.14.cloned.1.call-start = ((), (), s32[]{:S(2)}) async-start(), calls=%async_computation.20 | async-start | bytes 5242880 | tf_op jit(solution)/shard_map/reduce_scatter | solution.py:426
  391.4 298.4 %reduce-scatter.12.cloned.1.call-start = ((), (), s32[]{:S(2)}) async-start(), calls=%async_computation.19 | async-start | bytes 5242880 | tf_op jit(solution)/shard_map/reduce_scatter | solution.py:426
  410.8 67.9 %collective-permute-start.44 = (bf16[1024,2048]{1,0:T(8,128)(2,1)}, bf16[1024,2048]{1,0:T(8,128)(2,1)}, u32[]{:S(2)}, u32[]{:S(2)}) collective-permute-start(bf16[1024,2048]{1,0:T(8,128)(2,1)} %slice.451), channel_id=1, source_target_pairs={{0,1},{1,0},{2,3},{3,2},{4,5},{5,4},{6,7},{7,6},{8,9},{9,8},{10,11... | collective-permute-start | bytes 12582920 | tf_op jit(solution)/shard_map/ppermute | solution.py:41
  464.8 280.6 %reduce-scatter.6.cloned.1.call-start = ((), (), s32[]{:S(2)}) async-start(), calls=%async_computation.16 | async-start | bytes 2621440 | tf_op jit(solution)/shard_map/reduce_scatter | solution.py:426
  485.0 31.2 %collective-permute-start.56 = (bf16[256,1024]{1,0:T(8,128)(2,1)S(1)}, bf16[256,1024]{1,0:T(8,128)(2,1)S(1)}, u32[]{:S(2)}, u32[]{:S(2)}) collective-permute-start(bf16[256,1024]{1,0:T(8,128)(2,1)S(1)} %pad_maximum_fusion.11), channel_id=1, source_target_pairs={{0,2},{1,3},{2,0},{3,1},{4,6},{5,7},{6,4},{7,5},{8,10},{9,11},{10,... | collective-permute-start | bytes 1572872 | tf_op jit(solution)/shard_map/ppermute | solution.py:41
  505.5 33.2 %collective-permute-start.46 = (bf16[256,2048]{1,0:T(8,128)(2,1)S(1)}, bf16[256,2048]{1,0:T(8,128)(2,1)S(1)}, u32[]{:S(2)}, u32[]{:S(2)}) collective-permute-start(bf16[256,2048]{1,0:T(8,128)(2,1)S(1)} %pad_maximum_fusion.5), channel_id=1, source_target_pairs={{0,2},{1,3},{2,0},{3,1},{4,6},{5,7},{6,4},{7,5},{8,10},{9,11},{10,... | collective-permute-start | bytes 3145736 | tf_op jit(solution)/shard_map/ppermute | solution.py:41
  507.1 32.3 %collective-permute-start.48 = (bf16[256,2048]{1,0:T(8,128)(2,1)S(1)}, bf16[256,2048]{1,0:T(8,128)(2,1)S(1)}, u32[]{:S(2)}, u32[]{:S(2)}) collective-permute-start(bf16[256,2048]{1,0:T(8,128)(2,1)S(1)} %pad_maximum_fusion.6), channel_id=1, source_target_pairs={{0,4},{1,5},{2,6},{3,7},{4,0},{5,1},{6,2},{7,3},{8,12},{9,13},{10,... | collective-permute-start | bytes 3145736 | tf_op jit(solution)/shard_map/ppermute | solution.py:41
  558.4 85.6 %collective-permute-start.76 = (bf16[1024,2048]{1,0:T(8,128)(2,1)}, bf16[1024,2048]{1,0:T(8,128)(2,1)}, u32[]{:S(2)}, u32[]{:S(2)}) collective-permute-start(bf16[1024,2048]{1,0:T(8,128)(2,1)} %slice.513), channel_id=1, source_target_pairs={{0,1},{1,0},{2,3},{3,2},{4,5},{5,4},{6,7},{7,6},{8,9},{9,8},{10,11... | collective-permute-start | bytes 12582920 | tf_op jit(solution)/shard_map/ppermute | solution.py:41
  642.5 31.7 %collective-permute-start.68 = (bf16[256,1024]{1,0:T(8,128)(2,1)S(1)}, bf16[256,1024]{1,0:T(8,128)(2,1)}, u32[]{:S(2)}, u32[]{:S(2)}) collective-permute-start(bf16[256,1024]{1,0:T(8,128)(2,1)S(1)} %pad_maximum_fusion.13), channel_id=1, source_target_pairs={{0,2},{1,3},{2,0},{3,1},{4,6},{5,7},{6,4},{7,5},{8,10},{9,11},{10,... | collective-permute-start | bytes 1572872 | tf_op jit(solution)/shard_map/ppermute | solution.py:41
  650.5 34.9 %collective-permute-start.70 = (bf16[256,1024]{1,0:T(8,128)(2,1)}, bf16[256,1024]{1,0:T(8,128)(2,1)}, u32[]{:S(2)}, u32[]{:S(2)}) collective-permute-start(bf16[256,1024]{1,0:T(8,128)(2,1)} %pad_maximum_fusion.14), channel_id=1, source_target_pairs={{0,4},{1,5},{2,6},{3,7},{4,0},{5,1},{6,2},{7,3},{8,12},{9,13},{10,... | collective-permute-start | bytes 1572872 | tf_op jit(solution)/shard_map/ppermute | solution.py:41
  651.8 35.0 %collective-permute-start.73 = (bf16[256,1024]{1,0:T(8,128)(2,1)}, bf16[256,1024]{1,0:T(8,128)(2,1)}, u32[]{:S(2)}, u32[]{:S(2)}) collective-permute-start(bf16[256,1024]{1,0:T(8,128)(2,1)} %pad_maximum_fusion.15), channel_id=1, source_target_pairs={{0,2},{1,3},{2,0},{3,1},{4,6},{5,7},{6,4},{7,5},{8,10},{9,11},{10,... | collective-permute-start | bytes 1572872 | tf_op jit(solution)/shard_map/ppermute | solution.py:41
  672.0 51.3 %collective-permute-start.78 = (bf16[256,2048]{1,0:T(8,128)(2,1)}, bf16[256,2048]{1,0:T(8,128)(2,1)}, u32[]{:S(2)}, u32[]{:S(2)}) collective-permute-start(bf16[256,2048]{1,0:T(8,128)(2,1)} %pad_maximum_fusion.7), channel_id=1, source_target_pairs={{0,2},{1,3},{2,0},{3,1},{4,6},{5,7},{6,4},{7,5},{8,10},{9,11},{10,... | collective-permute-start | bytes 3145736 | tf_op jit(solution)/shard_map/ppermute | solution.py:41
  674.3 49.0 %collective-permute-start.80 = (bf16[256,2048]{1,0:T(8,128)(2,1)}, bf16[256,2048]{1,0:T(8,128)(2,1)}, u32[]{:S(2)}, u32[]{:S(2)}) collective-permute-start(bf16[256,2048]{1,0:T(8,128)(2,1)} %pad_maximum_fusion.8), channel_id=1, source_target_pairs={{0,4},{1,5},{2,6},{3,7},{4,0},{5,1},{6,2},{7,3},{8,12},{9,13},{10,... | collective-permute-start | bytes 3145736 | tf_op jit(solution)/shard_map/ppermute | solution.py:41
  674.6 42.6 %all-to-all-start.4 = ((bf16[8,64,1024]{2,1,0:T(8,128)(2,1)}), bf16[8,64,1024]{2,1,0:T(8,128)(2,1)}, u32[]{:S(2)}, u32[]{:S(2)}) async-start(bf16[8,64,1024]{2,1,0:T(8,128)(2,1)} %bitcast.98), calls=%async_computation.7 | async-start | bytes 2097152 | tf_op jit(solution)/shard_map/all_to_all | solution.py:429
  723.2 39.1 %reduce-scatter.8.cloned.1.call-start = ((), (), s32[]{:S(2)}) async-start(), calls=%async_computation.17 | async-start | bytes 1310720 | tf_op jit(solution)/shard_map/reduce_scatter | solution.py:426
  (113 other events, 1436.1 us)
Sparse Core Ops, SparseCore 0:
  17.0 36.9 all-gather.7
  55.5 45.5 all-gather.5
  102.7 79.4 all-gather.11
  183.7 79.2 all-gather.9
  265.0 79.2 all-gather.13
  352.8 75.1 reduce-scatter.9
  430.4 77.2 reduce-scatter.13
  510.0 77.2 reduce-scatter.11
  631.1 42.9 reduce-scatter.5
  726.8 26.7 reduce-scatter.7

commit v2 on v1

--- a/solution.py
+++ b/solution.py
@@ -18,6 +18,7 @@
 BF = jnp.bfloat16
 F32 = jnp.float32
 VMEM_LIMIT = 56 * 1024 * 1024
+SHARE = 0.05
 
 NN = (((1,), (0,)), ((), ()))
 NT = (((1,), (1,)), ((), ()))
@@ -37,39 +38,43 @@
     return (offset >> 1) + (offset & 1) * (count // 2)
 
 
+def after(value, *deps):
+    return lax.optimization_barrier((value, *deps))[0]
+
+
 def swap(value, count, offset):
     return lax.ppermute(value, "cp", [(i, i ^ offset) for i in range(count)])
 
 
-def gather_parts(part, count):
+def gather_rows(part, count, dep=None):
     half = part.shape[0] // 2
     if count == 8:
         by_x = swap(part, count, 2)
         by_y = swap(part, count, 4)
-        inner = [part, by_x, by_y, swap(by_y[:half], count, 2), swap(by_x[half:], count, 4)]
-    else:
-        inner, bit = [part], 2
-        while bit < count:
-            inner = inner + [swap(item, count, bit) for item in inner]
-            bit *= 2
-    outer = [swap(item, count, 1) for item in inner]
-    return inner + outer
-
-
-def gather_rows(part, count):
-    return jnp.concatenate(gather_parts(part, count), 0)
-
-
-def scatter_rows(partial, count):
-    total_rows, _ = partial.shape
-    middle = total_rows // 2
-    rows = total_rows // count
+        if dep is not None:
+            by_y = after(by_y, *dep)
+        near = jnp.concatenate([part, by_x, by_y], 0)
+        near_other = swap(near, count, 1)
+        far = jnp.concatenate([swap(by_y[:half], count, 2), swap(by_x[half:], count, 4)], 0)
+        return jnp.concatenate([near, far, near_other, swap(far, count, 1)], 0)
+    inner, bit = part, 2
+    while bit < count:
+        inner = jnp.concatenate([inner, swap(inner, count, bit)], 0)
+        bit *= 2
+    return jnp.concatenate([inner, swap(inner, count, 1)], 0)
+
+
+def plus(left, right):
+    return (left.astype(F32) + right.astype(F32)).astype(BF)
+
+
+def scatter_first(low, high, count):
+    return plus(low, swap(high, count, 1))
+
+
+def scatter_mid(acc, count):
+    rows = 2 * acc.shape[0] // count
     half = rows // 2
-
-    def plus(left, right):
-        return (left.astype(F32) + right.astype(F32)).astype(BF)
-
-    acc = plus(partial[:middle], swap(partial[middle:], count, 1))
     parts = [acc[i * rows : (i + 1) * rows] for i in range(count // 2)]
     if count == 8:
         own, to_x, to_y, far = parts
@@ -77,21 +82,25 @@
         from_y = swap(far[half:], count, 4)
         send_x = jnp.concatenate([to_x[:half], plus(to_x[half:], from_y)], 0)
         send_y = jnp.concatenate([plus(to_y[:half], from_x), to_y[half:]], 0)
-        got_x = swap(send_x, count, 2)
-        got_y = swap(send_y, count, 4)
-        return own.astype(F32) + got_x.astype(F32) + got_y.astype(F32)
+        return own, send_x, send_y
     bit = count // 2
-    while bit >= 2:
+    while bit > 2:
         keep, give = parts[: len(parts) // 2], parts[len(parts) // 2 :]
         parts = [plus(a, swap(b, count, bit)) for a, b in zip(keep, give)]
         bit //= 2
-    return parts[0].astype(F32)
-
-
-def trade(parts, count):
+    return tuple(parts)
+
+
+def scatter_last(state, count):
+    total = state[0].astype(F32)
+    for offset, part in zip((2, 4), state[1:]):
+        total = total + swap(part, count, offset).astype(F32)
+    return total
+
+
+def deal(count, n_cp, shift):
     return [
-        part if offset_of(p, count) == 0 else swap(part, count, offset_of(p, count))
-        for p, part in enumerate(parts)
+        (b, ((b % count + shift) % count) * n_cp + b // count) for b in range(count * n_cp)
     ]
 
 
@@ -100,7 +109,9 @@
 
 
 def cost(flops, nbytes, trans=0):
-    return pl.CostEstimate(flops=int(flops), bytes_accessed=int(nbytes), transcendentals=int(trans))
+    return pl.CostEstimate(
+        flops=int(flops * SHARE), bytes_accessed=int(nbytes * SHARE), transcendentals=int(trans * SHARE)
+    )
 
 
 def turn(value, cos, sin):
@@ -109,7 +120,11 @@
 
 def qkv_kernel(z_ref, w_ref, cos_ref, sin_ref, q_ref, k_ref, v_ref, kt_ref, vt_ref, *, heads):
     cos, sin = cos_ref[...], sin_ref[...]
-    flat = mm(z_ref[...], w_ref[...], NN)
+    flat = None
+    depth = z_ref.shape[1] // w_ref.shape[0]
+    for d in range(w_ref.shape[0]):
+        term = mm(z_ref[:, d * depth : (d + 1) * depth], w_ref[d, :depth, :], NN)
+        flat = term if flat is None else flat + term
     for h in range(heads):
         at = slice(h * HD, (h + 1) * HD)
         q_ref[:, at] = turn(flat[:, at], cos, sin).astype(BF)
@@ -123,7 +138,7 @@
 
 def qkv_call(z_one, w_qkv, cos, sin, rows, heads):
     total, width = z_one.shape
-    cols = w_qkv.shape[1]
+    cols = w_qkv.shape[2]
     row = lambda i: (i, 0)
     col = lambda i: (0, i)
     whole = lambda i: (0, 0)
@@ -132,7 +147,7 @@
         grid=(total // rows,),
         in_specs=[
             pl.BlockSpec((rows, width), row),
-            pl.BlockSpec((width, cols), whole),
+            pl.BlockSpec(w_qkv.shape, lambda i: (0, 0, 0)),
             pl.BlockSpec((rows, HD), row),
             pl.BlockSpec((rows, HD), row),
         ],
@@ -204,7 +219,8 @@
 def attend_call(me, q, k, vt, rows, heads, count):
     total = q.shape[0]
     slot = lambda i, me_ref: (position_of(i ^ me_ref[0], count), 0)
-    slot3 = lambda i, me_ref: (position_of(i ^ me_ref[0], count), 0, 0)
+    true = lambda i, me_ref: (i, 0)
+    true3 = lambda i, me_ref: (i, 0, 0)
     whole = lambda i, me_ref: (0, 0)
     return pl.pallas_call(
         functools.partial(attend_kernel, heads=heads, rows=rows, count=count),
@@ -217,8 +233,8 @@
                 pl.BlockSpec((HD, total), whole),
             ],
             out_specs=[
-                pl.BlockSpec((rows, heads * HD), slot),
-                pl.BlockSpec((1, 1, heads * rows), slot3),
+                pl.BlockSpec((rows, heads * HD), true),
+                pl.BlockSpec((1, 1, heads * rows), true3),
             ],
         ),
         out_shape=[
@@ -298,7 +314,8 @@
 def attend_back_call(me, q, g, o, lse, k, kt, v, cos, sin, rows, heads, count):
     total = q.shape[0]
     slot = lambda i, me_ref: (position_of(i ^ me_ref[0], count), 0)
-    slot3 = lambda i, me_ref: (position_of(i ^ me_ref[0], count), 0, 0)
+    true = lambda i, me_ref: (i, 0)
+    true3 = lambda i, me_ref: (i, 0, 0)
     whole = lambda i, me_ref: (0, 0)
     cols = (heads + 2) * HD
     return pl.pallas_call(
@@ -308,9 +325,9 @@
             grid=(count,),
             in_specs=[
                 pl.BlockSpec((rows, heads * HD), slot),
-                pl.BlockSpec((rows, heads * HD), slot),
-                pl.BlockSpec((rows, heads * HD), slot),
-                pl.BlockSpec((1, 1, heads * rows), slot3),
+                pl.BlockSpec((rows, heads * HD), true),
+                pl.BlockSpec((rows, heads * HD), true),
+                pl.BlockSpec((1, 1, heads * rows), true3),
                 pl.BlockSpec((total, HD), whole),
                 pl.BlockSpec((HD, total), whole),
                 pl.BlockSpec((total, HD), whole),
@@ -327,12 +344,34 @@
     )(me, q, g, o, lse, k, kt, v, cos, sin)
 
 
-def feed_kernel(z_ref, g_ref, w_ref, d_ref, act_ref, grads_ref):
-    cut = d_ref.shape[0]
+def back_act_kernel(g_ref, d_ref, out_ref):
+    out_ref[...] = mm(g_ref[...], d_ref[...], NT)
+
+
+def back_act_call(g_out, w_down, rows):
+    total, width = g_out.shape
+    cols = w_down.shape[0]
+    return pl.pallas_call(
+        back_act_kernel,
+        grid=(total // rows,),
+        in_specs=[
+            pl.BlockSpec((rows, width), lambda i: (i, 0)),
+            pl.BlockSpec((cols, width), lambda i: (0, 0)),
+        ],
+        out_specs=pl.BlockSpec((rows, cols), lambda i: (i, 0)),
+        out_shape=jax.ShapeDtypeStruct((total, cols), F32),
+        compiler_params=params(("arbitrary",)),
+        cost_estimate=cost(2 * total * width * cols, 2 * total * width + 2 * cols * width + 4 * total * cols),
+        name="back_act",
+    )(g_out, w_down)
+
+
+def feed_kernel(z_ref, g_ref, w_ref, act_ref, grads_ref):
+    cut = g_ref.shape[1]
     z = z_ref[...]
     gate = mm(z, w_ref[:, :cut], NN)
     up = mm(z, w_ref[:, cut:], NN)
-    back = mm(g_ref[...], d_ref[...], NT)
+    back = g_ref[...]
     sig = jax.nn.sigmoid(gate)
     silu = gate * sig
     act_ref[...] = (silu * up).astype(BF)
@@ -340,9 +379,9 @@
     grads_ref[:, cut:] = (back * silu).astype(BF)
 
 
-def feed_call(z_two, g_out, w_gu, w_down, rows):
+def feed_call(z_two, g_act, w_gu, part, rows):
     total, width = z_two.shape
-    cut = w_down.shape[0]
+    cut = w_gu.shape[1] // 2
     row = lambda i: (i, 0)
     whole = lambda i: (0, 0)
     return pl.pallas_call(
@@ -350,9 +389,8 @@
         grid=(total // rows,),
         in_specs=[
             pl.BlockSpec((rows, width), row),
-            pl.BlockSpec((rows, width), row),
+            pl.BlockSpec((rows, cut), lambda i: (i, part)),
             pl.BlockSpec((width, 2 * cut), whole),
-            pl.BlockSpec((cut, width), whole),
         ],
         out_specs=[pl.BlockSpec((rows, cut), row), pl.BlockSpec((rows, 2 * cut), row)],
         out_shape=[
@@ -360,24 +398,37 @@
             jax.ShapeDtypeStruct((total, 2 * cut), BF),
         ],
         compiler_params=params(("arbitrary",)),
-        cost_estimate=cost(6 * total * width * cut, 4 * total * width + 6 * cut * width + 6 * total * cut),
+        cost_estimate=cost(4 * total * width * cut, 2 * total * width + 4 * cut * width + 10 * total * cut),
         name="feed",
-    )(z_two, g_out, w_gu, w_down)
+    )(z_two, g_act, w_gu)
 
 
 def sum_kernel(*refs, dims):
-    *ins, out_ref = refs
+    *ins, low_ref, high_ref = refs
     acc = None
     for a_ref, b_ref in zip(ins[0::2], ins[1::2]):
         term = mm(a_ref[...], b_ref[...], dims)
         acc = term if acc is None else acc + term
-    out_ref[...] = acc.astype(out_ref.dtype)
+    acc = acc.astype(BF)
+    half = pl.num_programs(0) // 2
+
+    @pl.when(pl.program_id(0) < half)
+    def _():
+        high_ref[...] = acc
+
+    @pl.when(pl.program_id(0) >= half)
+    def _():
+        low_ref[...] = acc
 
 
 def sum_call(pairs, dims, rows, name):
     total = pairs[0][0].shape[0]
     cols = pairs[0][1].shape[1 if dims is NN else 0]
-    row = lambda i: (i, 0)
+    steps = total // rows
+    half = steps // 2
+    row = lambda i: ((i + half) % steps, 0)
+    low = lambda i: (jnp.maximum(i - half, 0), 0)
+    high = lambda i: (jnp.minimum(i, half - 1), 0)
     whole = lambda i: (0, 0)
     specs, flat, depth = [], [], 0
     for a, b in pairs:
@@ -388,12 +439,209 @@
         functools.partial(sum_kernel, dims=dims),
         grid=(total // rows,),
         in_specs=specs,
-        out_specs=pl.BlockSpec((rows, cols), row),
-        out_shape=jax.ShapeDtypeStruct((total, cols), BF),
+        out_specs=[pl.BlockSpec((rows, cols), low), pl.BlockSpec((rows, cols), high)],
+        out_shape=[jax.ShapeDtypeStruct((total // 2, cols), BF)] * 2,
         compiler_params=params(("arbitrary",)),
         cost_estimate=cost(2 * total * cols * depth, 2 * (total * depth + depth * cols + total * cols)),
         name=name,
     )(*flat)
+
+
+def split_rows(count):
+    half = count // 2
+    row = lambda i: (i + half) % count
+    low = lambda i: jnp.maximum(i - half, 0)
+    high = lambda i: jnp.minimum(i, half - 1)
+    return half, row, low, high
+
+
+def hidden_kernel(me_ref, a_ref, w_ref, x_ref, hid_ref, z_ref, rms_ref):
+    p = pl.program_id(0)
+
+    @pl.when(p == 0)
+    def _():
+        hid_ref[...] = x_ref[...].astype(F32)
+
+    hid_ref[...] += mm(a_ref[0], w_ref[...], NN)
+
+    @pl.when(p == pl.num_programs(0) - 1)
+    def _():
+        hid = hid_ref[...]
+        rms = rms_of(hid)
+        rms_ref[...] = rms
+        z_ref[...] = (hid * rms).astype(BF)
+
+
+def hidden_call(me, attn, wo, x, count):
+    _, rows, feat = attn.shape
+    width = wo.shape[1]
+    true3 = lambda p, me_ref: (offset_of(p, count) ^ me_ref[0], 0, 0)
+    block = lambda p, me_ref: (p, 0)
+    whole = lambda p, me_ref: (0, 0)
+    return pl.pallas_call(
+        hidden_kernel,
+        grid_spec=pltpu.PrefetchScalarGridSpec(
+            num_scalar_prefetch=1,
+            grid=(count,),
+            in_specs=[
+                pl.BlockSpec((1, rows, feat), true3),
+                pl.BlockSpec((feat, width), block),
+                pl.BlockSpec((rows, width), whole),
+            ],
+            out_specs=[
+                pl.BlockSpec((rows, width), whole),
+                pl.BlockSpec((rows, width), whole),
+                pl.BlockSpec((rows, 1), whole),
+            ],
+        ),
+        out_shape=[
+            jax.ShapeDtypeStruct((rows, width), F32),
+            jax.ShapeDtypeStruct((rows, width), BF),
+            jax.ShapeDtypeStruct((rows, 1), F32),
+        ],
+        compiler_params=params(("arbitrary",)),
+        cost_estimate=cost(2 * rows * feat * count * width, 2 * feat * count * width + 10 * rows * width),
+        name="hidden",
+    )(me, attn, wo, x)
+
+
+def back_attn_kernel(me_ref, g_ref, w_ref, out_ref):
+    out_ref[0] = mm(g_ref[...], w_ref[...], NT).astype(BF)
+
+
+def back_attn_call(me, g, wo, count):
+    rows, width = g.shape
+    feat = wo.shape[0] // count
+    true3 = lambda p, me_ref: (offset_of(p, count) ^ me_ref[0], 0, 0)
+    block = lambda p, me_ref: (p, 0)
+    whole = lambda p, me_ref: (0, 0)
+    return pl.pallas_call(
+        back_attn_kernel,
+        grid_spec=pltpu.PrefetchScalarGridSpec(
+            num_scalar_prefetch=1,
+            grid=(count,),
+            in_specs=[pl.BlockSpec((rows, width), whole), pl.BlockSpec((feat, width), block)],
+            out_specs=pl.BlockSpec((1, rows, feat), true3),
+        ),
+        out_shape=jax.ShapeDtypeStruct((count, rows, feat), BF),
+        compiler_params=params(("arbitrary",)),
+        cost_estimate=cost(2 * rows * feat * count * width, 2 * feat * count * width + 4 * rows * width),
+        name="back_attn",
+    )(me, g, wo)
+
+
+def grad_wo_kernel(me_ref, a_ref, g_ref, low_ref, high_ref):
+    out = mm(a_ref[0], g_ref[...], TN).astype(BF)
+    half = pl.num_programs(0) // 2
+
+    @pl.when(pl.program_id(0) < half)
+    def _():
+        high_ref[...] = out
+
+    @pl.when(pl.program_id(0) >= half)
+    def _():
+        low_ref[...] = out
+
+
+def grad_wo_call(me, attn, g, count):
+    _, rows, feat = attn.shape
+    width = g.shape[1]
+    half, row, low, high = split_rows(count)
+    return pl.pallas_call(
+        grad_wo_kernel,
+        grid_spec=pltpu.PrefetchScalarGridSpec(
+            num_scalar_prefetch=1,
+            grid=(count,),
+            in_specs=[
+                pl.BlockSpec(
+                    (1, rows, feat), lambda p, me_ref: (offset_of(row(p), count) ^ me_ref[0], 0, 0)
+                ),
+                pl.BlockSpec((rows, width), lambda p, me_ref: (0, 0)),
+            ],
+            out_specs=[
+                pl.BlockSpec((feat, width), lambda p, me_ref: (low(p), 0)),
+                pl.BlockSpec((feat, width), lambda p, me_ref: (high(p), 0)),
+            ],
+        ),
+        out_shape=[jax.ShapeDtypeStruct((half * feat, width), BF)] * 2,
+        compiler_params=params(("arbitrary",)),
+        cost_estimate=cost(2 * rows * feat * count * width, 2 * feat * count * width + 4 * rows * width),
+        name="grad_wo",
+    )(me, attn, g)
+
+
+def finish_feed_kernel(*refs, halves, per_half, unit, count):
+    gots, (wg_ref, wu_ref, gain_ref, g_ref, u_ref, sum_ref) = refs[:halves], refs[halves:]
+    gain = gain_ref[...]
+    total = None
+    for h, got_ref in enumerate(gots):
+        for kind, (w_ref, out_ref) in enumerate(((wg_ref, g_ref), (wu_ref, u_ref))):
+            for i in range(per_half):
+                frm = (kind * per_half + i) * unit
+                for t in range(count):
+                    at = ((h * per_half + i) * count + t) * unit
+                    raw = got_ref[t, :, frm : frm + unit].astype(F32)
+                    out_ref[:, at : at + unit] = raw * gain
+                    term = raw * w_ref[:, at : at + unit].astype(F32)
+                    total = term if total is None else total + term
+    sum_ref[...] = jnp.sum(total, 1, keepdims=True)
+
+
+def finish_feed_call(gots, w_gate, w_up, gain, per_half, unit):
+    own, hidden = w_gate.shape
+    return pl.pallas_call(
+        functools.partial(
+            finish_feed_kernel,
+            halves=len(gots),
+            per_half=per_half,
+            unit=unit,
+            count=gots[0].shape[0],
+        ),
+        out_shape=[
+            jax.ShapeDtypeStruct((own, hidden), F32),
+            jax.ShapeDtypeStruct((own, hidden), F32),
+            jax.ShapeDtypeStruct((own, 1), F32),
+        ],
+        compiler_params=pltpu.CompilerParams(vmem_limit_bytes=VMEM_LIMIT),
+        cost_estimate=cost(8 * own * hidden, 16 * own * hidden),
+        name="finish_feed",
+    )(*gots, w_gate, w_up, gain)
+
+
+def finish_qkv_kernel(
+    got_ref, wq_ref, wk_ref, wv_ref, gain_ref, q_ref, k_ref, v_ref, sum_ref, *, heads, reps
+):
+    gain = gain_ref[...]
+    total = None
+    feat = heads * HD
+    for t in range(got_ref.shape[0]):
+        raw = got_ref[t, :, :feat].astype(F32)
+        at = slice(t * feat, (t + 1) * feat)
+        q_ref[:, at] = raw * gain
+        term = jnp.sum(raw * wq_ref[:, at].astype(F32), 1, keepdims=True)
+        total = term if total is None else total + term
+    for kind, (w_ref, out_ref) in enumerate(((wk_ref, k_ref), (wv_ref, v_ref))):
+        frm = slice(feat + kind * HD, feat + (kind + 1) * HD)
+        for t in range(got_ref.shape[0] // reps):
+            raw = got_ref[t * reps, :, frm].astype(F32)
+            for r in range(1, reps):
+                raw = raw + got_ref[t * reps + r, :, frm].astype(F32)
+            at = slice(t * HD, (t + 1) * HD)
+            out_ref[:, at] = raw * gain
+            total = total + jnp.sum(raw * w_ref[:, at].astype(F32), 1, keepdims=True)
+    sum_ref[...] = total
+
+
+def finish_qkv_call(got, w_query, w_key, w_value, gain, heads, reps):
+    own = w_query.shape[0]
+    like = lambda w: jax.ShapeDtypeStruct(w.shape, F32)
+    return pl.pallas_call(
+        functools.partial(finish_qkv_kernel, heads=heads, reps=reps),
+        out_shape=[like(w_query), like(w_key), like(w_value), jax.ShapeDtypeStruct((own, 1), F32)],
+        compiler_params=pltpu.CompilerParams(vmem_limit_bytes=VMEM_LIMIT),
+        cost_estimate=cost(8 * own * w_query.shape[1], 16 * own * w_query.shape[1]),
+        name="finish_qkv",
+    )(got, w_query, w_key, w_value, gain)
 
 
 def rms_of(values):
@@ -434,23 +682,30 @@
     spread = lambda v: jnp.broadcast_to(v, (own, KVH, reps, HD)).reshape(own, n_cp, HD)
     qkv_own = jnp.concatenate([scaled_q, spread(scaled_k), spread(scaled_v)], 2).transpose(1, 0, 2)
     qkv_cols = (heads + 2) * HD
-    w_qkv = gather_z(give(qkv_own).reshape(n_cp * own, qkv_cols))
-
-    devices = n_dp * n_cp
-    moved = [(b, (b % n_dp) * n_cp + b // n_dp) for b in range(devices)]
-    moved_back = [(b, a) for a, b in moved]
-    wo_rows = gather_z(lax.ppermute(w_output, ("dp", "cp"), moved))
+    qkv_rows = give(qkv_own).reshape(n_cp * own, qkv_cols)
+    wo_own = lax.ppermute(w_output, ("dp", "cp"), deal(n_dp, n_cp, 0))
+    depth = n_cp * own
+    packs = own * width % qkv_cols == 0
+    if packs:
+        joint = jnp.concatenate([qkv_rows, wo_own.reshape(-1, qkv_cols)], 0)
+        joint = gather_z(joint).reshape(n_dp, -1, qkv_cols)
+        wo_rows = joint[:, depth:].reshape(n_dp * own, width)
+    else:
+        joint = gather_z(qkv_rows).reshape(n_dp, -1, qkv_cols)
+        wo_rows = gather_z(wo_own)
 
     w_down_full = gather_z(w_down)
     scaled_g = (w_gate.astype(F32) * gain_two).astype(BF).reshape(own, n_dp, n_cp, unit)
     scaled_u = (w_up.astype(F32) * gain_two).astype(BF).reshape(own, n_dp, n_cp, unit)
     cut = per_half * unit
-    w_gu, w_dn = [], []
+    w_gu, w_dn, last, given = [], [], qkv_rows, []
     for h in range(halves):
         at = slice(h * per_half, (h + 1) * per_half)
         both = jnp.concatenate([scaled_g[:, at], scaled_u[:, at]], 1)
         both = both.transpose(2, 0, 1, 3).reshape(n_cp, own, 2 * cut)
-        w_gu.append(gather_z(give(both).reshape(n_cp * own, 2 * cut)))
+        last = give(after(both, last))
+        given.append(last)
+        w_gu.append(gather_z(last.reshape(n_cp * own, 2 * cut)))
         w_dn.append(w_down_full[h * cut : (h + 1) * cut])
 
     shard_at = jnp.array([offset_of(p, n_cp) for p in range(n_cp)], jnp.int32) ^ me
@@ -462,88 +717,104 @@
     cos = jnp.concatenate([cos_half, cos_half], -1)
     sin = jnp.concatenate([-sin_half, sin_half], -1)
 
-    x = inputs.reshape(rows, width).astype(F32)
+    xb = inputs.reshape(rows, width)
+    x = xb.astype(F32)
     rms_one = rms_of(x)
     z_one = x * rms_one
-    z_one_all = gather_rows(z_one.astype(BF), n_cp)
+    z_one_all = gather_rows(z_one.astype(BF), n_cp, [cos, sin] + given)
+    wo_rel = gather_rows(wo_rows, n_cp)
     g_outb = cotangent.reshape(rows, width)
     g_out = g_outb.astype(F32)
-    g_out_all = gather_rows(g_outb, n_cp)
-    wo_rel = gather_rows(wo_rows, n_cp)
-
-    q, k, v, kt, vt = qkv_call(z_one_all, w_qkv, cos, sin, rows, heads)
+    g_out_all = gather_rows(after(g_outb, z_one_all), n_cp)
+    g_act = back_act_call(g_out_all, w_down_full, rows)
+
+    q, k, v, kt, vt = qkv_call(z_one_all, joint, cos, sin, rows, heads)
     mixed, lse = attend_call(me_arr, q, k, vt, rows, heads, n_cp)
-    pieces = trade([mixed[p * rows : (p + 1) * rows] for p in range(n_cp)], n_cp)
-    attn = jnp.concatenate(pieces, 1)
-    hid = x + jnp.dot(attn, wo_rel, preferred_element_type=F32)
-    rms_two = rms_of(hid)
-    z_two = hid * rms_two
-    z_two_all = gather_rows(z_two.astype(BF), n_cp)
+    feat = heads * HD
+    attn = give(mixed.reshape(n_cp, rows, feat))
+    hid, z_two_b, rms_two = hidden_call(me_arr, after(attn, g_act), wo_rel, xb, n_cp)
+    z_two_all = gather_rows(z_two_b, n_cp)
 
     acts, gus, red_gu = [], [], []
     for h in range(halves):
-        act, gu = feed_call(z_two_all, g_out_all, w_gu[h], w_dn[h], rows)
+        z_in = after(z_two_all, part_gu) if h else z_two_all
+        act, gu = feed_call(z_in, g_act, w_gu[h], h, rows)
         acts.append(act)
         gus.append(gu)
-        red_gu.append(scatter_z(mm(z_two_all, gu, TN).astype(BF)))
+        if h == 0:
+            part_gu = mm(z_two_all, gu, TN).astype(BF)
+            red_gu.append(scatter_z(part_gu))
     chunks = 2
-    u_parts = []
+    accs = []
     for c in range(chunks):
         at = slice(c * width // chunks, (c + 1) * width // chunks)
         part = sum_call([(gus[h], w_gu[h][at]) for h in range(halves)], NT, rows, "g_two")
-        u_parts.append(scatter_rows(part, n_cp))
-    u = jnp.concatenate(u_parts, 1)
-    grad_down = scatter_z(jnp.concatenate([mm(a, g_out_all, TN).astype(BF) for a in acts], 0))
-
+        accs.append(scatter_first(*part, n_cp))
+    states = [scatter_mid(acc, n_cp) for acc in accs]
+    part_gu = mm(z_two_all, after(gus[1], accs[0]), TN).astype(BF)
+    red_gu.append(scatter_z(part_gu))
+    downs = []
+    for c, act in enumerate(acts):
+        act = after(act, part_gu, *states[c])
+        downs.append(mm(act, g_out_all, TN).astype(BF))
+    grad_down = scatter_z(after(jnp.concatenate(downs, 0), red_gu[0]))
+    out_part = sum_call([(after(acts[h], *downs), w_dn[h]) for h in range(halves)], NN, rows, "out")
+    u = jnp.concatenate([scatter_last(state, n_cp) for state in states], 1)
+
+    z_two = hid * rms_two
     g_hidden = g_out + rms_two * (u - z_two * jnp.mean(u * z_two, -1, keepdims=True))
     g_hidb = g_hidden.astype(BF)
-    g_attn = mm(g_hidb, wo_rel, NT).astype(BF)
-    feat = heads * HD
-    g_pieces = trade([g_attn[:, p * feat : (p + 1) * feat] for p in range(n_cp)], n_cp)
-    g_mixed = jnp.concatenate(g_pieces, 0)
+    wo_part = grad_wo_call(me_arr, attn, after(g_hidb, *out_part), n_cp)
+    g_heads = back_attn_call(me_arr, after(g_hidb, *wo_part), wo_rel, n_cp)
+    g_mixed = give(g_heads).reshape(total, feat)
+    wo_state = scatter_mid(scatter_first(*wo_part, n_cp), n_cp)
+    out_state = scatter_mid(scatter_first(*out_part, n_cp), n_cp)
+    lse = after(lse, red_gu[1], *wo_state, *out_state)
     g_qkv = attend_back_call(me_arr, q, g_mixed, mixed, lse, k, kt, v, cos, sin, rows, heads, n_cp)
-    red_qkv = scatter_z(mm(z_one_all, g_qkv, TN).astype(BF))
-    w_parts = []
+    part_qkv = mm(z_one_all, g_qkv, TN).astype(BF)
+    back_gu = [give(after(red_gu[0].reshape(n_cp, own, 2 * cut), g_qkv))]
+    wo_sum = scatter_last(wo_state, n_cp).astype(BF)
+    if packs:
+        both = jnp.concatenate(
+            [part_qkv.reshape(n_dp, depth, qkv_cols), wo_sum.reshape(n_dp, -1, qkv_cols)], 1
+        ).reshape(-1, qkv_cols)
+        g_qkv = after(g_qkv, both)
+    w_states = []
+    w_qkv = joint[:, :depth].reshape(width, qkv_cols)
     for c in range(chunks):
         at = slice(c * width // chunks, (c + 1) * width // chunks)
         part = sum_call([(g_qkv, w_qkv[at])], NT, rows, "g_one")
-        w_parts.append(scatter_rows(part, n_cp))
-    w_one = jnp.concatenate(w_parts, 1)
+        w_states.append(scatter_mid(scatter_first(*part, n_cp), n_cp))
+
+    output = hid + scatter_last(out_state, n_cp)
+    back_pairs = [(b, a) for a, b in deal(n_dp, n_cp, 0)]
+    if packs:
+        both = scatter_z(after(both, grad_down))
+        red_qkv, wo_sum = both[:depth], both[depth:].reshape(own, width)
+    else:
+        red_qkv, wo_sum = scatter_z(part_qkv), scatter_z(wo_sum)
+    grad_output = lax.ppermute(wo_sum, ("dp", "cp"), back_pairs).astype(F32)
+    w_one = jnp.concatenate([scatter_last(state, n_cp) for state in w_states], 1)
     grad_in = g_hidden + rms_one * (w_one - z_one * jnp.mean(w_one * z_one, -1, keepdims=True))
 
-    out_part = sum_call([(acts[h], w_dn[h]) for h in range(halves)], NN, rows, "out")
-    output = hid + scatter_rows(out_part, n_cp)
-    wo_part = mm(attn, g_hidb, TN).astype(BF)
-    wo_sum = scatter_z(scatter_rows(wo_part, n_cp).astype(BF))
-    grad_output = lax.ppermute(wo_sum, ("dp", "cp"), moved_back).astype(F32)
-
-    got = give(red_qkv.reshape(n_cp, own, qkv_cols)).astype(F32)
-    raw_q = got[:, :, : heads * HD].transpose(1, 0, 2).reshape(own, H * HD)
-    fold = lambda v: v.reshape(KVH, reps, own, HD).sum(1).transpose(1, 0, 2).reshape(own, KVH * HD)
-    raw_k = fold(got[:, :, heads * HD : (heads + 1) * HD])
-    raw_v = fold(got[:, :, (heads + 1) * HD :])
-    grad_attn_gain = (
-        jnp.sum(raw_q * w_query.astype(F32), 1)
-        + jnp.sum(raw_k * w_key.astype(F32), 1)
-        + jnp.sum(raw_v * w_value.astype(F32), 1)
+    back_gu.append(give(red_gu[1].reshape(n_cp, own, 2 * cut)))
+    grad_g, grad_u, gain_two_sum = finish_feed_call(back_gu, w_gate, w_up, gain_two, per_half, unit)
+    got = give(after(red_qkv.reshape(n_cp, own, qkv_cols), back_gu[1]))
+    grad_q, grad_k, grad_v, gain_one_sum = finish_qkv_call(
+        got, w_query, w_key, w_value, gain_one, heads, reps
     )
-    back_gu = jnp.stack([give(r.reshape(n_cp, own, 2 * cut)) for r in red_gu], 0)
-    back_gu = back_gu.reshape(halves, n_cp, own, 2, per_half, unit).transpose(3, 2, 0, 4, 1, 5)
-    back_gu = back_gu.reshape(2, own, hidden).astype(F32)
-    raw_g, raw_u = back_gu[0], back_gu[1]
-    grad_ffn_gain = jnp.sum(raw_g * w_gate.astype(F32), 1) + jnp.sum(raw_u * w_up.astype(F32), 1)
 
     return (
         output[None],
         grad_in[None],
-        grad_attn_gain,
-        raw_q * gain_one,
-        raw_k * gain_one,
-        raw_v * gain_one,
+        gain_one_sum[:, 0],
+        grad_q,
+        grad_k,
+        grad_v,
         grad_output,
-        grad_ffn_gain,
-        raw_g * gain_two,
-        raw_u * gain_two,
+        gain_two_sum[:, 0],
+        grad_g,
+        grad_u,
         grad_down.astype(F32),
     )
 

time: 802 us -> 741 us (0.924)
  Pallas kernels: 154 us -> 200 us
  waiting for transfers between devices: 218 us -> 175 us
  blocking collectives: 40.5 us -> 0 us
  local copies, waits for them, and re-layouts: 120 us -> 86.6 us
  other arithmetic: 71.2 us -> 95 us
  matrix products: 68.6 us -> 53.9 us
    all_to_all x4 -> x8, waiting for transfers between devices: 69.6 us -> 16.6 us  [give(): return lax.all_to_all(value, 'cp', 0, 0)]
    pallas_call x0 -> x6, Pallas kernels: none -> 50.4 us  [the longest x1 15 us: back_act_call(): pl.pallas_call(back_act_kernel, grid=(total // rows,), in_specs=[pl.Block...]
    all_to_all x2 -> x0, blocking collectives: 40.5 us -> none  [give(): return lax.all_to_all(value, 'cp', 0, 0)]
    all_to_all x4 -> x8, starting transfers between devices: 25.4 us -> 48.8 us  [give(): return lax.all_to_all(value, 'cp', 0, 0)]
    unnamed x149 -> x125, local copies, waits for them, and re-layouts: 61.5 us -> 38.6 us
    ppermute x80 -> x54, waiting for transfers between devices: 128 us -> 150 us  [swap(): return lax.ppermute(value, 'cp', [(i, i ^ offset) for i in range(count)])]
    concatenate x13 -> x23, other arithmetic: 7.69 us -> 29.2 us  [the longest x4 8.04 us: gather_rows(): near = jnp.concatenate([part, by_x, by_y], 0)]
    ppermute x80 -> x54, starting transfers between devices: 68.5 us -> 49.3 us  [swap(): return lax.ppermute(value, 'cp', [(i, i ^ offset) for i in range(count)])]
  transfers between devices with their start and end apart: 96 -> 72, of which waited for: 30 -> 26; matrix products, arithmetic and copies ran while one was open for 32% -> 31% of each run, Pallas kernels for 19% -> 27%
where the time goes in v2:
time: 741 us; the launch traced here: 733 us
  Pallas kernels  200 us (27%)
  waiting for transfers between devices  175 us (24%)
  starting transfers between devices  106 us (14%)
  other arithmetic  95 us (13%)
  local copies, waits for them, and re-layouts  86.6 us (12%)
  matrix products  53.9 us (7%)
  between operations  15.3 us (2%)
    ppermute x54, waiting for transfers between devices, swap(): return lax.ppermute(value, 'cp', [(i, i ^ offset) for i in range(count)])  150 us
    pallas_call x5, Pallas kernels, sum_call(): pl.pallas_call(functools.partial(sum_kernel, dims=dims), grid=(total // r...  61.3 us
    dot_general x5, matrix products, mm(): return lax.dot_general(left, right, dims, preferred_element_type=F32)  53.9 us
    ppermute x54, starting transfers between devices, swap(): return lax.ppermute(value, 'cp', [(i, i ^ offset) for i in range(count)])  49.3 us
    all_to_all x8, starting transfers between devices, give(): return lax.all_to_all(value, 'cp', 0, 0)  48.8 us
    unnamed x125, local copies, waits for them, and re-layouts  38.6 us
    pallas_call x2, Pallas kernels, feed_call(): pl.pallas_call(feed_kernel, grid=(total // rows,), in_specs=[pl.BlockSpec...  31.3 us
    convert_element_type x12, other arithmetic, plus(): return (left.astype(F32) + right.astype(F32)).astype(BF)  29.6 us
  transfers between devices with their start and end apart: 72, of which 26 were waited for; matrix products, arithmetic and copies ran while one was open for 31% of the time, Pallas kernels for 27%

profile of v2, /device:TPU:1, one launch (start us, length us, event | category | flops | bytes accessed | tf_op | source)
XLA Modules:
  0.0 732.5 jit_solution(4786870193878847262)
XLA Ops:
  34.9 10.4 %all-to-all-start.1 = ((bf16[8,64,1024]{2,1,0:T(8,128)(2,1)}), bf16[8,64,1024]{2,1,0:T(8,128)(2,1)S(1)}, u32[]{:S(2)}, u32[]{:S(2)}) async-start(bf16[8,64,1024]{2,1,0:T(8,128)(2,1)} %reshape.139), calls=%async_computation.1 | async-start | bytes 2097152 | tf_op jit(solution)/shard_map/all_to_all | solution.py:677
  57.2 8.1 %all-to-all-start.2 = ((bf16[8,64,1024]{2,1,0:T(8,128)(2,1)}), bf16[8,64,1024]{2,1,0:T(8,128)(2,1)}, u32[]{:S(2)}, u32[]{:S(2)}) async-start(bf16[8,64,1024]{2,1,0:T(8,128)(2,1)} %reshape.142), calls=%async_computation.2 | async-start | bytes 2097152 | tf_op jit(solution)/shard_map/all_to_all | solution.py:677
  71.2 10.0 %collective-permute-done.1 = bf16[256,2048]{1,0:T(8,128)(2,1)S(1)} collective-permute-done((bf16[256,2048]{1,0:T(8,128)(2,1)}, bf16[256,2048]{1,0:T(8,128)(2,1)S(1)}, u32[]{:S(2)}, u32[]{:S(2)}) %collective-permute-start.1) | collective-permute-done | bytes 1048608 | tf_op jit(solution)/shard_map/ppermute | solution.py:46
  81.2 9.8 %all-to-all-done.2 = bf16[8,64,1024]{2,1,0:T(8,128)(2,1)} async-done(((bf16[8,64,1024]{2,1,0:T(8,128)(2,1)}), bf16[8,64,1024]{2,1,0:T(8,128)(2,1)}, u32[]{:S(2)}, u32[]{:S(2)}) %all-to-all-start.2) | async-done | bytes 1048608 | tf_op jit(solution)/shard_map/all_to_all | solution.py:677
  98.3 12.9 %collective-permute-done.3 = bf16[128,2048]{1,0:T(8,128)(2,1)S(1)} collective-permute-done((bf16[128,2048]{1,0:T(8,128)(2,1)S(1)}, bf16[128,2048]{1,0:T(8,128)(2,1)S(1)}, u32[]{:S(2)}, u32[]{:S(2)}) %collective-permute-start.3) | collective-permute-done | bytes 524320 | tf_op jit(solution)/shard_map/ppermute | solution.py:46
  128.6 14.7 %collective-permute-done.13 = bf16[256,2048]{1,0:T(8,128)(2,1)S(1)} collective-permute-done((bf16[256,2048]{1,0:T(8,128)(2,1)S(1)}, bf16[256,2048]{1,0:T(8,128)(2,1)S(1)}, u32[]{:S(2)}, u32[]{:S(2)}) %collective-permute-start.13) | collective-permute-done | bytes 1048608 | tf_op jit(solution)/shard_map/ppermute | solution.py:46
  148.1 11.8 %qkv.1 = (bf16[2048,256]{1,0:T(8,128)(2,1)}, bf16[2048,128]{1,0:T(8,128)(2,1)}, bf16[2048,128]{1,0:T(8,128)(2,1)}, bf16[128,2048]{1,0:T(8,128)(2,1)}, bf16[128,2048]{1,0:T(8,128)(2,1)}) custom-call(bf16[2048,2048]{1,0:T(8,128)(2,1)} %constant_dynamic-update-slice_fusion.z_ref, bf16[4,768,512]{2,1,0:T(8,128)(2,1)} %bitcast.74, ...), custom_call_target="tpu_custom_call" | custom-call | flops 214748368 | bytes 524288 | tf_op jit(solution)/shard_map/qkv/pallas_call | solution.py:145
  160.0 21.5 %attend.1 = (bf16[2048,256]{1,0:T(8,128)(2,1)}, f32[8,1,512]{2,1,0:T(1,128)}) custom-call(s32[1]{0:T(128)} %bitcast.me_ref, bf16[2048,256]{1,0:T(8,128)(2,1)} %get-tuple-element.66.q_ref, bf16[2048,128]{1,0:T(8,128)(2,1)} %get-tuple-element.67.k_ref, bf16[128,2048]{1,0:T(8,128)(2,1)} %get-tuple-element.68.vt_ref), custom_call_target="tpu_custom_call" | custom-call | flops 214748368 | bytes 104857 | tf_op jit(solution)/shard_map/attend/pallas_call | solution.py:225
  200.8 9.4 %collective-permute-done.15 = bf16[128,2048]{1,0:T(8,128)(2,1)S(1)} collective-permute-done((bf16[128,2048]{1,0:T(8,128)(2,1)S(1)}, bf16[128,2048]{1,0:T(8,128)(2,1)S(1)}, u32[]{:S(2)}, u32[]{:S(2)}) %collective-permute-start.15) | collective-permute-done | bytes 524320 | tf_op jit(solution)/shard_map/ppermute | solution.py:46
  213.2 8.1 %collective-permute-done.10 = bf16[128,2048]{1,0:T(8,128)(2,1)S(1)} collective-permute-done((bf16[128,2048]{1,0:T(8,128)(2,1)S(1)}, bf16[128,2048]{1,0:T(8,128)(2,1)S(1)}, u32[]{:S(2)}, u32[]{:S(2)}) %collective-permute-start.10) | collective-permute-done | bytes 524320 | tf_op jit(solution)/shard_map/ppermute | solution.py:46
  234.6 15.0 %back_act.1.g_ref = f32[2048,1024]{1,0:T(8,128)} custom-call(bf16[2048,2048]{1,0:T(8,128)(2,1)} %constant_dynamic-update-slice_fusion.7.g_ref, bf16[1024,2048]{1,0:T(8,128)(2,1)} %all-gather.7.cloned.1.call-done.d_ref), custom_call_target="tpu_custom_call" | custom-call | flops 429496736 | bytes 1048576 | tf_op jit(solution)/shard_map/back_act/pallas_call | solution.py:354
  250.6 10.1 %hidden.1 = (f32[256,2048]{1,0:T(8,128)}, bf16[256,2048]{1,0:T(8,128)(2,1)}, f32[256,1]{1,0:T(8,128)}) custom-call(s32[1]{0:T(128)} %bitcast.me_ref, bf16[8,256,256]{2,1,0:T(8,128)(2,1)} %copy-done.12, bf16[2048,2048]{1,0:T(8,128)(2,1)} %constant_dynamic-update-slice_fusion.14.w_ref, bf16[256,2048]{1,0:T(8,128)(2,1)} %bitcast.67), custom_call_target="tpu_custom_call" | custom-call | flops 107374184 | bytes 681574 | tf_op jit(solution)/shard_map/hidden/pallas_call | solution.py:481
  262.3 23.5 %collective-permute-done.20 = bf16[256,2048]{1,0:T(8,128)(2,1)S(1)} collective-permute-done((bf16[256,2048]{1,0:T(8,128)(2,1)}, bf16[256,2048]{1,0:T(8,128)(2,1)S(1)}, u32[]{:S(2)}, u32[]{:S(2)}) %collective-permute-start.20) | collective-permute-done | bytes 1048608 | tf_op jit(solution)/shard_map/ppermute | solution.py:46
  291.1 11.8 %collective-permute-done.21 = bf16[128,2048]{1,0:T(8,128)(2,1)S(1)} collective-permute-done((bf16[128,2048]{1,0:T(8,128)(2,1)S(1)}, bf16[128,2048]{1,0:T(8,128)(2,1)S(1)}, u32[]{:S(2)}, u32[]{:S(2)}) %collective-permute-start.21) | collective-permute-done | bytes 524320 | tf_op jit(solution)/shard_map/ppermute | solution.py:46
  311.2 15.6 %feed.2 = (bf16[2048,512]{1,0:T(8,128)(2,1)}, bf16[2048,1024]{1,0:T(8,128)(2,1)}) custom-call(bf16[2048,2048]{1,0:T(8,128)(2,1)} %constant_dynamic-update-slice_fusion.21.z_ref, f32[2048,1024]{1,0:T(8,128)} %back_act.1.g_ref, bf16[2048,1024]{1,0:T(8,128)(2,1)} %all-gather.9.cloned.1.call-done.w_ref), custom_call_target="tpu_custom_call" | custom-call | flops 429496736 | bytes 1153433 | tf_op jit(solution)/shard_map/feed/pallas_call | solution.py:387
  326.8 14.0 %convolution_convert_fusion.1 = bf16[2048,1024]{1,0:T(8,128)(2,1)} fusion(bf16[2048,2048]{1,0:T(8,128)(2,1)} %constant_dynamic-update-slice_fusion.21.z_ref, bf16[2048,1024]{1,0:T(8,128)(2,1)} %get-tuple-element.75.refs_0_), kind=kOutput, calls=%fused_computation.8 | convolution fusion | flops 8592031744 | bytes 16777216 | tf_op jit(solution)/shard_map/dot_general | solution.py:29
  350.7 15.7 %feed.3 = (bf16[2048,512]{1,0:T(8,128)(2,1)}, bf16[2048,1024]{1,0:T(8,128)(2,1)}) custom-call(bf16[2048,2048]{1,0:T(8,128)(2,1)} %constant_dynamic-update-slice_fusion.21.z_ref, f32[2048,1024]{1,0:T(8,128)} %back_act.1.g_ref, bf16[2048,1024]{1,0:T(8,128)(2,1)} %all-gather.11.cloned.1.call-done.w_ref), custom_call_target="tpu_custom_call" | custom-call | flops 429496736 | bytes 1153433 | tf_op jit(solution)/shard_map/feed/pallas_call | solution.py:387
  366.4 14.6 %g_two.2 = (bf16[1024,1024]{1,0:T(8,128)(2,1)}, bf16[1024,1024]{1,0:T(8,128)(2,1)}) custom-call(bf16[2048,1024]{1,0:T(8,128)(2,1)} %get-tuple-element.75.refs_0_, bf16[1024,1024]{1,0:T(8,128)(2,1)} %get-tuple-element.134.refs_1_, bf16[2048,1024]{1,0:T(8,128)(2,1)} %get-tuple-element.80.refs_2_, bf16[1024,1024]{1,0:T(8,128)(2,1)} %get-tuple-element.132.refs_3_), custom_call_target="tpu_custom_call" | custom-call | flops 429496736 | bytes 838860 | tf_op jit(solution)/shard_map/g_two/pallas_call | solution.py:438
  381.1 14.8 %g_two.3 = (bf16[1024,1024]{1,0:T(8,128)(2,1)}, bf16[1024,1024]{1,0:T(8,128)(2,1)}) custom-call(bf16[2048,1024]{1,0:T(8,128)(2,1)} %get-tuple-element.75.refs_0_, bf16[1024,1024]{1,0:T(8,128)(2,1)} %get-tuple-element.133.refs_1_, bf16[2048,1024]{1,0:T(8,128)(2,1)} %get-tuple-element.80.refs_2_, bf16[1024,1024]{1,0:T(8,128)(2,1)} %get-tuple-element.131.refs_3_), custom_call_target="tpu_custom_call" | custom-call | flops 429496736 | bytes 838860 | tf_op jit(solution)/shard_map/g_two/pallas_call | solution.py:438
  408.4 12.8 %convolution_convert_fusion = bf16[2048,1024]{1,0:T(8,128)(2,1)} fusion(bf16[2048,2048]{1,0:T(8,128)(2,1)} %constant_dynamic-update-slice_fusion.21.z_ref, bf16[2048,1024]{1,0:T(8,128)(2,1)S(1)} %copy-done.3), kind=kOutput, calls=%fused_computation.7 | convolution fusion | flops 8592031744 | bytes 16777216 | tf_op jit(solution)/shard_map/dot_general | solution.py:29
  436.3 9.2 %convolution_convert_fusion.3 = bf16[512,2048]{1,0:T(8,128)(2,1)} fusion(bf16[2048,512]{1,0:T(8,128)(2,1)S(1)} %copy-done.31, bf16[2048,2048]{1,0:T(8,128)(2,1)} %constant_dynamic-update-slice_fusion.7.g_ref), kind=kOutput, calls=%fused_computation.15 | convolution fusion | flops 4296015872 | bytes 12582912 | tf_op jit(solution)/shard_map/dot_general | solution.py:29
  445.5 9.2 %convolution_convert_fusion.4 = bf16[512,2048]{1,0:T(8,128)(2,1)} fusion(bf16[2048,512]{1,0:T(8,128)(2,1)S(1)} %copy-done.30, bf16[2048,2048]{1,0:T(8,128)(2,1)} %constant_dynamic-update-slice_fusion.7.g_ref), kind=kOutput, calls=%fused_computation.16 | convolution fusion | flops 4296015872 | bytes 12582912 | tf_op jit(solution)/shard_map/dot_general | solution.py:29
  454.7 14.9 %out.1 = (bf16[1024,2048]{1,0:T(8,128)(2,1)}, bf16[1024,2048]{1,0:T(8,128)(2,1)}) custom-call(bf16[2048,512]{1,0:T(8,128)(2,1)} %get-tuple-element.86.refs_0_, bf16[512,2048]{1,0:T(8,128)(2,1)} %get-tuple-element.130.refs_1_, bf16[2048,512]{1,0:T(8,128)(2,1)} %get-tuple-element.87.refs_2_, bf16[512,2048]{1,0:T(8,128)(2,1)} %get-tuple-element.129.refs_3_), custom_call_target="tpu_custom_call" | custom-call | flops 429496736 | bytes 838860 | tf_op jit(solution)/shard_map/out/pallas_call | solution.py:438
  475.2 9.3 %grad_wo.1 = (bf16[1024,2048]{1,0:T(8,128)(2,1)}, bf16[1024,2048]{1,0:T(8,128)(2,1)}) custom-call(s32[1]{0:T(128)} %bitcast.me_ref, bf16[8,256,256]{2,1,0:T(8,128)(2,1)} %copy-done.12, bf16[256,2048]{1,0:T(8,128)(2,1)} %fusion.12.g_ref), custom_call_target="tpu_custom_call" | custom-call | flops 107374184 | bytes 524288 | tf_op jit(solution)/shard_map/grad_wo/pallas_call | solution.py:550
  518.5 8.8 %back_attn.1 = bf16[8,256,256]{2,1,0:T(8,128)(2,1)} custom-call(s32[1]{0:T(128)} %bitcast.me_ref, bf16[256,2048]{1,0:T(8,128)(2,1)} %fusion.12.g_ref, bf16[2048,2048]{1,0:T(8,128)(2,1)} %constant_dynamic-update-slice_fusion.14.w_ref), custom_call_target="tpu_custom_call" | custom-call | flops 107374184 | bytes 524288 | tf_op jit(solution)/shard_map/back_attn/pallas_call | solution.py:518
  538.1 8.9 %collective-permute-done.44 = bf16[256,2048]{1,0:T(8,128)(2,1)} collective-permute-done((bf16[256,2048]{1,0:T(8,128)(2,1)}, bf16[256,2048]{1,0:T(8,128)(2,1)}, u32[]{:S(2)}, u32[]{:S(2)}) %collective-permute-start.44) | collective-permute-done | bytes 1048608 | tf_op jit(solution)/shard_map/ppermute | solution.py:46
  559.3 23.9 %attend_back.1.refs_0_ = bf16[2048,512]{1,0:T(8,128)(2,1)} custom-call(s32[1]{0:T(128)} %bitcast.me_ref, bf16[2048,256]{1,0:T(8,128)(2,1)} %get-tuple-element.66.q_ref, bf16[2048,256]{1,0:T(8,128)(2,1)} %bitcast.77, bf16[2048,256]{1,0:T(8,128)(2,1)} %get-tuple-element.69.o_ref, f32[8,1,512]{2,1,0:T(1,128)} %get-tuple-element.96.lse_ref, ...), custom_call_target="tpu_custom_call" | custom-call | flops 536870912 | bytes 209715 | tf_op jit(solution)/shard_map/attend_back/pallas_call | solution.py:321
  583.2 8.6 %convolution_convert_fusion.2 = bf16[2048,512]{1,0:T(8,128)(2,1)S(1)} fusion(bf16[2048,2048]{1,0:T(8,128)(2,1)} %constant_dynamic-update-slice_fusion.z_ref, bf16[2048,512]{1,0:T(8,128)(2,1)} %attend_back.1.refs_0_), kind=kOutput, calls=%fused_computation.14 | convolution fusion | flops 4296015872 | bytes 12582912 | tf_op jit(solution)/shard_map/dot_general | solution.py:29
  596.9 8.5 %g_one.2 = (bf16[1024,1024]{1,0:T(8,128)(2,1)}, bf16[1024,1024]{1,0:T(8,128)(2,1)}) custom-call(bf16[2048,512]{1,0:T(8,128)(2,1)} %attend_back.1.refs_0_, bf16[1024,512]{1,0:T(8,128)(2,1)} %bitcast.84), custom_call_target="tpu_custom_call" | custom-call | flops 107374184 | bytes 367001 | tf_op jit(solution)/shard_map/g_one/pallas_call | solution.py:438
  607.6 8.4 %g_one.3 = (bf16[1024,1024]{1,0:T(8,128)(2,1)}, bf16[1024,1024]{1,0:T(8,128)(2,1)}) custom-call(bf16[2048,512]{1,0:T(8,128)(2,1)} %attend_back.1.refs_0_, bf16[1024,512]{1,0:T(8,128)(2,1)} %bitcast.81), custom_call_target="tpu_custom_call" | custom-call | flops 107374184 | bytes 367001 | tf_op jit(solution)/shard_map/g_one/pallas_call | solution.py:438
  656.5 14.5 %collective-permute-done.47 = bf16[256,1024]{1,0:T(8,128)(2,1)} collective-permute-done((bf16[256,1024]{1,0:T(8,128)(2,1)S(1)}, bf16[256,1024]{1,0:T(8,128)(2,1)}, u32[]{:S(2)}, u32[]{:S(2)}) %collective-permute-start.47) | collective-permute-done | bytes 524320 | tf_op jit(solution)/shard_map/ppermute | solution.py:46
  704.6 9.5 %collective-permute-done.33 = bf16[256,2048]{1,0:T(8,128)(2,1)} collective-permute-done((bf16[256,2048]{1,0:T(8,128)(2,1)}, bf16[256,2048]{1,0:T(8,128)(2,1)}, u32[]{:S(2)}, u32[]{:S(2)}) %collective-permute-start.33) | collective-permute-done | bytes 1048608 | tf_op jit(solution)/shard_map/ppermute | solution.py:46
  (370 shorter events, 318.6 us)
Async XLA Ops:
  16.9 99.5 %all-gather.5.cloned.1.call-start = ((), (), s32[]{:S(2)}) async-start(), calls=%async_computation.12 | async-start | bytes 3932160 | tf_op jit(solution)/shard_map/all_gather | solution.py:671
  29.0 205.6 %all-gather.7.cloned.1.call-start = ((), (), s32[]{:S(2)}) async-start(), calls=%async_computation.13 | async-start | bytes 5242880 | tf_op jit(solution)/shard_map/all_gather | solution.py:671
  46.8 34.4 %collective-permute-start.1 = (bf16[256,2048]{1,0:T(8,128)(2,1)}, bf16[256,2048]{1,0:T(8,128)(2,1)S(1)}, u32[]{:S(2)}, u32[]{:S(2)}) collective-permute-start(bf16[256,2048]{1,0:T(8,128)(2,1)} %get-tuple-element.116), channel_id=1, source_target_pairs={{0,4},{1,5},{2,6},{3,7},{4,0},{5,1},{6,2},{7,3},{8,12},{9,13},{10,... | collective-permute-start | bytes 3145736 | tf_op jit(solution)/shard_map/ppermute | solution.py:46
  48.2 42.8 %collective-permute-start = (bf16[256,2048]{1,0:T(8,128)(2,1)}, bf16[256,2048]{1,0:T(8,128)(2,1)S(1)}, u32[]{:S(2)}, u32[]{:S(2)}) collective-permute-start(bf16[256,2048]{1,0:T(8,128)(2,1)} %get-tuple-element.116), channel_id=1, source_target_pairs={{0,2},{1,3},{2,0},{3,1},{4,6},{5,7},{6,4},{7,5},{8,10},{9,11},{10,... | collective-permute-start | bytes 3145736 | tf_op jit(solution)/shard_map/ppermute | solution.py:46
  57.2 33.8 %all-to-all-start.2 = ((bf16[8,64,1024]{2,1,0:T(8,128)(2,1)}), bf16[8,64,1024]{2,1,0:T(8,128)(2,1)}, u32[]{:S(2)}, u32[]{:S(2)}) async-start(bf16[8,64,1024]{2,1,0:T(8,128)(2,1)} %reshape.142), calls=%async_computation.2 | async-start | bytes 2097152 | tf_op jit(solution)/shard_map/all_to_all | solution.py:677
  65.3 245.8 %all-gather.9.cloned.1.call-start = ((), (), s32[]{:S(2)}) async-start(), calls=%async_computation.14 | async-start | bytes 5242880 | tf_op jit(solution)/shard_map/all_gather | solution.py:671
  93.9 26.7 %collective-permute-start.4 = (bf16[768,2048]{1,0:T(8,128)(2,1)}, bf16[768,2048]{1,0:T(8,128)(2,1)}, u32[]{:S(2)}, u32[]{:S(2)}) collective-permute-start(bf16[768,2048]{1,0:T(8,128)(2,1)} %pad_maximum_fusion.1), channel_id=1, source_target_pairs={{0,1},{1,0},{2,3},{3,2},{4,5},{5,4},{6,7},{7,6},{8,9},{9,8},{10,11... | collective-permute-start | bytes 9437192 | tf_op jit(solution)/shard_map/ppermute | solution.py:46
  127.0 58.4 %collective-permute-start.7 = (bf16[256,2048]{1,0:T(8,128)(2,1)S(1)}, bf16[256,2048]{1,0:T(8,128)(2,1)}, u32[]{:S(2)}, u32[]{:S(2)}) collective-permute-start(bf16[256,2048]{1,0:T(8,128)(2,1)S(1)} %bitcast.68), channel_id=1, source_target_pairs={{0,2},{1,3},{2,0},{3,1},{4,6},{5,7},{6,4},{7,5},{8,10},{9,11},{10,... | collective-permute-start | bytes 3145736 | tf_op jit(solution)/shard_map/ppermute | solution.py:46
  128.3 57.1 %collective-permute-start.8 = (bf16[256,2048]{1,0:T(8,128)(2,1)S(1)}, bf16[256,2048]{1,0:T(8,128)(2,1)}, u32[]{:S(2)}, u32[]{:S(2)}) collective-permute-start(bf16[256,2048]{1,0:T(8,128)(2,1)S(1)} %bitcast.69), channel_id=1, source_target_pairs={{0,4},{1,5},{2,6},{3,7},{4,0},{5,1},{6,2},{7,3},{8,12},{9,13},{10,... | collective-permute-start | bytes 3145736 | tf_op jit(solution)/shard_map/ppermute | solution.py:46
  145.4 81.0 %collective-permute-start.17 = (bf16[768,2048]{1,0:T(8,128)(2,1)}, bf16[768,2048]{1,0:T(8,128)(2,1)}, u32[]{:S(2)}, u32[]{:S(2)}) collective-permute-start(bf16[768,2048]{1,0:T(8,128)(2,1)} %pad_maximum_fusion.3), channel_id=1, source_target_pairs={{0,1},{1,0},{2,3},{3,2},{4,5},{5,4},{6,7},{7,6},{8,9},{9,8},{10,11... | collective-permute-start | bytes 9437192 | tf_op jit(solution)/shard_map/ppermute | solution.py:46
  181.5 68.2 %all-to-all-start.3 = ((bf16[8,256,256]{2,1,0:T(8,128)(2,1)}), bf16[8,256,256]{2,1,0:T(8,128)(2,1)S(1)}, u32[]{:S(2)}, u32[]{:S(2)}) async-start(bf16[8,256,256]{2,1,0:T(8,128)(2,1)} %bitcast.76), calls=%async_computation.3 | async-start | bytes 2097152 | tf_op jit(solution)/shard_map/all_to_all | solution.py:677
  185.1 160.8 %all-gather.11.cloned.1.call-start = ((), (), s32[]{:S(2)}) async-start(), calls=%async_computation.15 | async-start | bytes 5242880 | tf_op jit(solution)/shard_map/all_gather | solution.py:671
  187.2 44.3 %collective-permute-start.11 = (bf16[768,2048]{1,0:T(8,128)(2,1)S(1)}, bf16[768,2048]{1,0:T(8,128)(2,1)S(1)}, u32[]{:S(2)}, u32[]{:S(2)}) collective-permute-start(bf16[768,2048]{1,0:T(8,128)(2,1)S(1)} %pad_maximum_fusion.2), channel_id=1, source_target_pairs={{0,1},{1,0},{2,3},{3,2},{4,5},{5,4},{6,7},{7,6},{8,9},{9,8},{10,11... | collective-permute-start | bytes 9437192 | tf_op jit(solution)/shard_map/ppermute | solution.py:46
  262.3 227.5 %reduce-scatter.7.cloned.1.call-start = ((), (), s32[]{:S(2)}) async-start(), calls=%async_computation.17 | async-start | bytes 5242880 | tf_op jit(solution)/shard_map/reduce_scatter | solution.py:674
  340.8 213.4 %reduce-scatter.5.cloned.1.call-start = ((), (), s32[]{:S(2)}) async-start(), calls=%async_computation.16 | async-start | bytes 5242880 | tf_op jit(solution)/shard_map/reduce_scatter | solution.py:674
  424.9 169.0 %reduce-scatter.9.cloned.1.call-start = ((), (), s32[]{:S(2)}) async-start(), calls=%async_computation.18 | async-start | bytes 5242880 | tf_op jit(solution)/shard_map/reduce_scatter | solution.py:674
  428.5 42.8 %collective-permute-start.38 = (bf16[256,1024]{1,0:T(8,128)(2,1)}, bf16[256,1024]{1,0:T(8,128)(2,1)}, u32[]{:S(2)}, u32[]{:S(2)}) collective-permute-start(bf16[256,1024]{1,0:T(8,128)(2,1)} %pad_maximum_fusion.21), channel_id=1, source_target_pairs={{0,2},{1,3},{2,0},{3,1},{4,6},{5,7},{6,4},{7,5},{8,10},{9,11},{10,... | collective-permute-start | bytes 1572872 | tf_op jit(solution)/shard_map/ppermute | solution.py:46
  431.4 39.9 %collective-permute-start.39 = (bf16[256,1024]{1,0:T(8,128)(2,1)}, bf16[256,1024]{1,0:T(8,128)(2,1)}, u32[]{:S(2)}, u32[]{:S(2)}) collective-permute-start(bf16[256,1024]{1,0:T(8,128)(2,1)} %pad_maximum_fusion.22), channel_id=1, source_target_pairs={{0,4},{1,5},{2,6},{3,7},{4,0},{5,1},{6,2},{7,3},{8,12},{9,13},{10,... | collective-permute-start | bytes 1572872 | tf_op jit(solution)/shard_map/ppermute | solution.py:46
  433.9 35.7 %collective-permute-start.36 = (bf16[256,1024]{1,0:T(8,128)(2,1)}, bf16[256,1024]{1,0:T(8,128)(2,1)}, u32[]{:S(2)}, u32[]{:S(2)}) collective-permute-start(bf16[256,1024]{1,0:T(8,128)(2,1)} %pad_maximum_fusion.19), channel_id=1, source_target_pairs={{0,2},{1,3},{2,0},{3,1},{4,6},{5,7},{6,4},{7,5},{8,10},{9,11},{10,... | collective-permute-start | bytes 1572872 | tf_op jit(solution)/shard_map/ppermute | solution.py:46
  435.2 34.4 %collective-permute-start.37 = (bf16[256,1024]{1,0:T(8,128)(2,1)}, bf16[256,1024]{1,0:T(8,128)(2,1)}, u32[]{:S(2)}, u32[]{:S(2)}) collective-permute-start(bf16[256,1024]{1,0:T(8,128)(2,1)} %pad_maximum_fusion.20), channel_id=1, source_target_pairs={{0,4},{1,5},{2,6},{3,7},{4,0},{5,1},{6,2},{7,3},{8,12},{9,13},{10,... | collective-permute-start | bytes 1572872 | tf_op jit(solution)/shard_map/ppermute | solution.py:46
  515.8 31.2 %collective-permute-start.44 = (bf16[256,2048]{1,0:T(8,128)(2,1)}, bf16[256,2048]{1,0:T(8,128)(2,1)}, u32[]{:S(2)}, u32[]{:S(2)}) collective-permute-start(bf16[256,2048]{1,0:T(8,128)(2,1)} %pad_maximum_fusion.17), channel_id=1, source_target_pairs={{0,4},{1,5},{2,6},{3,7},{4,0},{5,1},{6,2},{7,3},{8,12},{9,13},{10,... | collective-permute-start | bytes 3145736 | tf_op jit(solution)/shard_map/ppermute | solution.py:46
  517.0 31.1 %collective-permute-start.43 = (bf16[256,2048]{1,0:T(8,128)(2,1)}, bf16[256,2048]{1,0:T(8,128)(2,1)}, u32[]{:S(2)}, u32[]{:S(2)}) collective-permute-start(bf16[256,2048]{1,0:T(8,128)(2,1)} %pad_maximum_fusion.16), channel_id=1, source_target_pairs={{0,2},{1,3},{2,0},{3,1},{4,6},{5,7},{6,4},{7,5},{8,10},{9,11},{10,... | collective-permute-start | bytes 3145736 | tf_op jit(solution)/shard_map/ppermute | solution.py:46
  527.3 31.0 %all-to-all-start.4 = ((bf16[8,256,256]{2,1,0:T(8,128)(2,1)}), bf16[8,256,256]{2,1,0:T(8,128)(2,1)S(1)}, u32[]{:S(2)}, u32[]{:S(2)}) async-start(bf16[8,256,256]{2,1,0:T(8,128)(2,1)} %back_attn.1), calls=%async_computation.4 | async-start | bytes 2097152 | tf_op jit(solution)/shard_map/all_to_all | solution.py:677
  533.9 151.1 %reduce-scatter.11.cloned.1.call-start = ((), (), s32[]{:S(2)}) async-start(), calls=%async_computation.19 | async-start | bytes 3932160 | tf_op jit(solution)/shard_map/reduce_scatter | solution.py:674
  640.4 32.4 %all-to-all-start.5 = ((bf16[8,64,1024]{2,1,0:T(8,128)(2,1)}), bf16[8,64,1024]{2,1,0:T(8,128)(2,1)}, u32[]{:S(2)}, u32[]{:S(2)}) async-start(bf16[8,64,1024]{2,1,0:T(8,128)(2,1)} %bitcast.90), calls=%async_computation.9 | async-start | bytes 2097152 | tf_op jit(solution)/shard_map/all_to_all | solution.py:677
  650.5 28.6 %collective-permute-start.49 = (bf16[256,1024]{1,0:T(8,128)(2,1)}, bf16[256,1024]{1,0:T(8,128)(2,1)}, u32[]{:S(2)}, u32[]{:S(2)}) collective-permute-start(bf16[256,1024]{1,0:T(8,128)(2,1)} %pad_maximum_fusion.24), channel_id=1, source_target_pairs={{0,4},{1,5},{2,6},{3,7},{4,0},{5,1},{6,2},{7,3},{8,12},{9,13},{10,... | collective-permute-start | bytes 1572872 | tf_op jit(solution)/shard_map/ppermute | solution.py:46
  653.9 28.3 %collective-permute-start.52 = (bf16[256,1024]{1,0:T(8,128)(2,1)}, bf16[256,1024]{1,0:T(8,128)(2,1)}, u32[]{:S(2)}, u32[]{:S(2)}) collective-permute-start(bf16[256,1024]{1,0:T(8,128)(2,1)} %pad_maximum_fusion.25), channel_id=1, source_target_pairs={{0,2},{1,3},{2,0},{3,1},{4,6},{5,7},{6,4},{7,5},{8,10},{9,11},{10,... | collective-permute-start | bytes 1572872 | tf_op jit(solution)/shard_map/ppermute | solution.py:46
  655.1 27.2 %collective-permute-start.54 = (bf16[256,1024]{1,0:T(8,128)(2,1)}, bf16[256,1024]{1,0:T(8,128)(2,1)}, u32[]{:S(2)}, u32[]{:S(2)}) collective-permute-start(bf16[256,1024]{1,0:T(8,128)(2,1)} %pad_maximum_fusion.26), channel_id=1, source_target_pairs={{0,4},{1,5},{2,6},{3,7},{4,0},{5,1},{6,2},{7,3},{8,12},{9,13},{10,... | collective-permute-start | bytes 1572872 | tf_op jit(solution)/shard_map/ppermute | solution.py:46
  655.1 49.5 %collective-permute-start.35 = (bf16[256,2048]{1,0:T(8,128)(2,1)}, bf16[256,2048]{1,0:T(8,128)(2,1)}, u32[]{:S(2)}, u32[]{:S(2)}) collective-permute-start(bf16[256,2048]{1,0:T(8,128)(2,1)} %pad_maximum_fusion.15), channel_id=1, source_target_pairs={{0,4},{1,5},{2,6},{3,7},{4,0},{5,1},{6,2},{7,3},{8,12},{9,13},{10,... | collective-permute-start | bytes 3145736 | tf_op jit(solution)/shard_map/ppermute | solution.py:46
  671.0 43.0 %collective-permute-start.33 = (bf16[256,2048]{1,0:T(8,128)(2,1)}, bf16[256,2048]{1,0:T(8,128)(2,1)}, u32[]{:S(2)}, u32[]{:S(2)}) collective-permute-start(bf16[256,2048]{1,0:T(8,128)(2,1)} %pad_maximum_fusion.14), channel_id=1, source_target_pairs={{0,2},{1,3},{2,0},{3,1},{4,6},{5,7},{6,4},{7,5},{8,10},{9,11},{10,... | collective-permute-start | bytes 3145736 | tf_op jit(solution)/shard_map/ppermute | solution.py:46
  686.8 35.0 %all-to-all-start.6 = ((bf16[8,64,512]{2,1,0:T(8,128)(2,1)}), bf16[8,64,512]{2,1,0:T(8,128)(2,1)}, u32[]{:S(2)}, u32[]{:S(2)}) async-start(bf16[8,64,512]{2,1,0:T(8,128)(2,1)} %bitcast.87), calls=%async_computation.10 | async-start | bytes 1048576 | tf_op jit(solution)/shard_map/all_to_all | solution.py:677
  693.9 27.0 %collective-permute-start.55 = (bf16[64,2048]{1,0:T(8,128)(2,1)}, bf16[64,2048]{1,0:T(8,128)(2,1)S(1)}, u32[]{:S(2)}, u32[]{:S(2)}) collective-permute-start(bf16[64,2048]{1,0:T(8,128)(2,1)} %reshape.156), channel_id=1, source_target_pairs={{0,0},{8,1},{16,2},{24,3},{1,4},{9,5},{17,6},{25,7},{2,8},{10,9},{... | collective-permute-start | bytes 786440 | tf_op jit(solution)/shard_map/ppermute | solution.py:796
  (88 other events, 1124.8 us)
Sparse Core Ops, SparseCore 0:
  29.2 69.3 all-gather.4
  100.1 79.4 all-gather.6
  181.8 79.2 all-gather.8
  262.5 79.4 all-gather.10
  344.1 75.2 reduce-scatter.6
  425.0 76.8 reduce-scatter.4
  504.2 77.2 reduce-scatter.8
  594.0 61.5 reduce-scatter.10

commit v3 on v2

--- a/solution.py
+++ b/solution.py
@@ -68,11 +68,12 @@
     return (left.astype(F32) + right.astype(F32)).astype(BF)
 
 
-def scatter_first(low, high, count):
-    return plus(low, swap(high, count, 1))
-
-
-def scatter_mid(acc, count):
+def scatter_first(low, high, count, *deps):
+    got = swap(high, count, 1)
+    return plus(low, after(got, *deps) if deps else got)
+
+
+def scatter_mid(acc, count, *deps):
     rows = 2 * acc.shape[0] // count
     half = rows // 2
     parts = [acc[i * rows : (i + 1) * rows] for i in range(count // 2)]
@@ -80,6 +81,8 @@
         own, to_x, to_y, far = parts
         from_x = swap(far[:half], count, 2)
         from_y = swap(far[half:], count, 4)
+        if deps:
+            from_x, from_y = lax.optimization_barrier((from_x, from_y, *deps))[:2]
         send_x = jnp.concatenate([to_x[:half], plus(to_x[half:], from_y)], 0)
         send_y = jnp.concatenate([plus(to_y[:half], from_x), to_y[half:]], 0)
         return own, send_x, send_y
@@ -91,10 +94,13 @@
     return tuple(parts)
 
 
-def scatter_last(state, count):
+def scatter_last(state, count, *deps):
+    got = [swap(part, count, offset) for offset, part in zip((2, 4), state[1:])]
+    if deps:
+        got = lax.optimization_barrier((*got, *deps))[: len(got)]
     total = state[0].astype(F32)
-    for offset, part in zip((2, 4), state[1:]):
-        total = total + swap(part, count, offset).astype(F32)
+    for part in got:
+        total = total + part.astype(F32)
     return total
 
 
@@ -685,8 +691,7 @@
     qkv_rows = give(qkv_own).reshape(n_cp * own, qkv_cols)
     wo_own = lax.ppermute(w_output, ("dp", "cp"), deal(n_dp, n_cp, 0))
     depth = n_cp * own
-    packs = own * width % qkv_cols == 0
-    if packs:
+    if own * width % qkv_cols == 0:
         joint = jnp.concatenate([qkv_rows, wo_own.reshape(-1, qkv_cols)], 0)
         joint = gather_z(joint).reshape(n_dp, -1, qkv_cols)
         wo_rows = joint[:, depth:].reshape(n_dp * own, width)
@@ -726,13 +731,13 @@
     g_outb = cotangent.reshape(rows, width)
     g_out = g_outb.astype(F32)
     g_out_all = gather_rows(after(g_outb, z_one_all), n_cp)
-    g_act = back_act_call(g_out_all, w_down_full, rows)
 
     q, k, v, kt, vt = qkv_call(z_one_all, joint, cos, sin, rows, heads)
     mixed, lse = attend_call(me_arr, q, k, vt, rows, heads, n_cp)
     feat = heads * HD
     attn = give(mixed.reshape(n_cp, rows, feat))
-    hid, z_two_b, rms_two = hidden_call(me_arr, after(attn, g_act), wo_rel, xb, n_cp)
+    hid, z_two_b, rms_two = hidden_call(me_arr, attn, wo_rel, xb, n_cp)
+    g_act = back_act_call(after(g_out_all, z_two_b), w_down_full, rows)
     z_two_all = gather_rows(z_two_b, n_cp)
 
     acts, gus, red_gu = [], [], []
@@ -744,62 +749,48 @@
         if h == 0:
             part_gu = mm(z_two_all, gu, TN).astype(BF)
             red_gu.append(scatter_z(part_gu))
-    chunks = 2
-    accs = []
-    for c in range(chunks):
-        at = slice(c * width // chunks, (c + 1) * width // chunks)
-        part = sum_call([(gus[h], w_gu[h][at]) for h in range(halves)], NT, rows, "g_two")
-        accs.append(scatter_first(*part, n_cp))
-    states = [scatter_mid(acc, n_cp) for acc in accs]
-    part_gu = mm(z_two_all, after(gus[1], accs[0]), TN).astype(BF)
+    part = sum_call([(gus[h], w_gu[h]) for h in range(halves)], NT, rows, "g_two")
+    part_gu = mm(z_two_all, after(gus[1], *part), TN).astype(BF)
     red_gu.append(scatter_z(part_gu))
-    downs = []
-    for c, act in enumerate(acts):
-        act = after(act, part_gu, *states[c])
-        downs.append(mm(act, g_out_all, TN).astype(BF))
+    acc = scatter_first(*part, n_cp, part_gu)
+    out_part = sum_call([(after(acts[h], acc), w_dn[h]) for h in range(halves)], NN, rows, "out")
+    state = scatter_mid(acc, n_cp, *out_part)
+    downs = [mm(after(act, *state), g_out_all, TN).astype(BF) for act in acts]
     grad_down = scatter_z(after(jnp.concatenate(downs, 0), red_gu[0]))
-    out_part = sum_call([(after(acts[h], *downs), w_dn[h]) for h in range(halves)], NN, rows, "out")
-    u = jnp.concatenate([scatter_last(state, n_cp) for state in states], 1)
+    out_acc = scatter_first(*out_part, n_cp, *downs)
+    u = scatter_last(state, n_cp, out_acc)
 
     z_two = hid * rms_two
     g_hidden = g_out + rms_two * (u - z_two * jnp.mean(u * z_two, -1, keepdims=True))
     g_hidb = g_hidden.astype(BF)
-    wo_part = grad_wo_call(me_arr, attn, after(g_hidb, *out_part), n_cp)
-    g_heads = back_attn_call(me_arr, after(g_hidb, *wo_part), wo_rel, n_cp)
+    g_heads = back_attn_call(me_arr, g_hidb, wo_rel, n_cp)
     g_mixed = give(g_heads).reshape(total, feat)
-    wo_state = scatter_mid(scatter_first(*wo_part, n_cp), n_cp)
-    out_state = scatter_mid(scatter_first(*out_part, n_cp), n_cp)
-    lse = after(lse, red_gu[1], *wo_state, *out_state)
+    wo_part = grad_wo_call(me_arr, attn, after(g_hidb, g_heads), n_cp)
+    back_gu = [give(after(red_gu[0].reshape(n_cp, own, 2 * cut), g_mixed))]
+    lse = after(lse, *wo_part)
     g_qkv = attend_back_call(me_arr, q, g_mixed, mixed, lse, k, kt, v, cos, sin, rows, heads, n_cp)
-    part_qkv = mm(z_one_all, g_qkv, TN).astype(BF)
-    back_gu = [give(after(red_gu[0].reshape(n_cp, own, 2 * cut), g_qkv))]
-    wo_sum = scatter_last(wo_state, n_cp).astype(BF)
-    if packs:
-        both = jnp.concatenate(
-            [part_qkv.reshape(n_dp, depth, qkv_cols), wo_sum.reshape(n_dp, -1, qkv_cols)], 1
-        ).reshape(-1, qkv_cols)
-        g_qkv = after(g_qkv, both)
-    w_states = []
+    out_state = scatter_mid(after(out_acc, g_mixed), n_cp, g_qkv)
+    wo_acc = scatter_first(*wo_part, n_cp, g_qkv)
+    part_qkv = mm(z_one_all, after(g_qkv, wo_acc, red_gu[1], *out_state), TN).astype(BF)
+    red_qkv = scatter_z(part_qkv)
+    back_gu.append(give(after(red_gu[1].reshape(n_cp, own, 2 * cut), g_qkv)))
+    wo_state = scatter_mid(wo_acc, n_cp, part_qkv)
     w_qkv = joint[:, :depth].reshape(width, qkv_cols)
-    for c in range(chunks):
-        at = slice(c * width // chunks, (c + 1) * width // chunks)
-        part = sum_call([(g_qkv, w_qkv[at])], NT, rows, "g_one")
-        w_states.append(scatter_mid(scatter_first(*part, n_cp), n_cp))
-
-    output = hid + scatter_last(out_state, n_cp)
+    part = sum_call([(after(g_qkv, back_gu[0], *wo_state), w_qkv)], NT, rows, "g_one")
+    out_sum = scatter_last(out_state, n_cp)
+    output = hid + out_sum
+    w_acc = scatter_first(*part, n_cp, back_gu[1], out_sum)
+    wo_sum = scatter_last(wo_state, n_cp, w_acc).astype(BF)
+    w_state = scatter_mid(w_acc, n_cp)
+
+    wo_sum = scatter_z(after(wo_sum, grad_down))
+    got = give(red_qkv.reshape(n_cp, own, qkv_cols))
     back_pairs = [(b, a) for a, b in deal(n_dp, n_cp, 0)]
-    if packs:
-        both = scatter_z(after(both, grad_down))
-        red_qkv, wo_sum = both[:depth], both[depth:].reshape(own, width)
-    else:
-        red_qkv, wo_sum = scatter_z(part_qkv), scatter_z(wo_sum)
     grad_output = lax.ppermute(wo_sum, ("dp", "cp"), back_pairs).astype(F32)
-    w_one = jnp.concatenate([scatter_last(state, n_cp) for state in w_states], 1)
+    w_one = scatter_last(w_state, n_cp, got)
     grad_in = g_hidden + rms_one * (w_one - z_one * jnp.mean(w_one * z_one, -1, keepdims=True))
 
-    back_gu.append(give(red_gu[1].reshape(n_cp, own, 2 * cut)))
     grad_g, grad_u, gain_two_sum = finish_feed_call(back_gu, w_gate, w_up, gain_two, per_half, unit)
-    got = give(after(red_qkv.reshape(n_cp, own, qkv_cols), back_gu[1]))
     grad_q, grad_k, grad_v, gain_one_sum = finish_qkv_call(
         got, w_query, w_key, w_value, gain_one, heads, reps
     )

time: 741 us -> 727 us (0.981)
  Pallas kernels: 200 us -> 192 us
  local copies, waits for them, and re-layouts: 86.6 us -> 78.6 us
  waiting for transfers between devices: 175 us -> 183 us
    ppermute x54 -> x44, waiting for transfers between devices: 150 us -> 111 us  [swap(): return lax.ppermute(value, 'cp', [(i, i ^ offset) for i in range(count)])]
    all_to_all x8, waiting for transfers between devices: 16.6 us -> 39.9 us  [give(): return lax.all_to_all(value, 'cp', 0, 0)]
    ppermute x1, waiting for transfers between devices: 0.01 us -> 13.1 us  [shards(): grad_output = lax.ppermute(wo_sum, ('dp', 'cp'), back_pairs).astype(F32)]
    all_gather x4, waiting for transfers between devices: 0.01 us -> 9.73 us  [gather_z(): return lax.all_gather(value, 'dp', axis=0, tiled=True)]
    slice x5 -> x3, local copies, waits for them, and re-layouts: 15.2 us -> 5.83 us  [the longest x2 4.37 us: scatter_mid(): send_y = jnp.concatenate([plus(to_y[:half], from_x), to_y[half:]], 0)]
    pallas_call x5 -> x3, Pallas kernels: 61.3 us -> 52 us  [sum_call(): pl.pallas_call(functools.partial(sum_kernel, dims=dims), grid=(total // r...]
    unnamed x125 -> x103, local copies, waits for them, and re-layouts: 38.6 us -> 43.9 us
    ppermute x54 -> x44, starting transfers between devices: 49.3 us -> 45.7 us  [swap(): return lax.ppermute(value, 'cp', [(i, i ^ offset) for i in range(count)])]
  transfers between devices with their start and end apart: 72 -> 63, of which waited for: 26 -> 22; matrix products, arithmetic and copies ran while one was open for 31% -> 31% of each run, Pallas kernels for 27% -> 27%
where the time goes in v3:
time: 727 us; the launch traced here: 719 us
  Pallas kernels  192 us (26%)
  waiting for transfers between devices  183 us (25%)
  starting transfers between devices  102 us (14%)
  other arithmetic  94.8 us (13%)
  local copies, waits for them, and re-layouts  78.6 us (11%)
  matrix products  54.6 us (8%)
  between operations  14.7 us (2%)
    ppermute x44, waiting for transfers between devices, swap(): return lax.ppermute(value, 'cp', [(i, i ^ offset) for i in range(count)])  111 us
    dot_general x5, matrix products, mm(): return lax.dot_general(left, right, dims, preferred_element_type=F32)  54.6 us
    pallas_call x3, Pallas kernels, sum_call(): pl.pallas_call(functools.partial(sum_kernel, dims=dims), grid=(total // r...  52 us
    all_to_all x8, starting transfers between devices, give(): return lax.all_to_all(value, 'cp', 0, 0)  48 us
    ppermute x44, starting transfers between devices, swap(): return lax.ppermute(value, 'cp', [(i, i ^ offset) for i in range(count)])  45.7 us
    unnamed x103, local copies, waits for them, and re-layouts  43.9 us
    all_to_all x8, waiting for transfers between devices, give(): return lax.all_to_all(value, 'cp', 0, 0)  39.9 us
    pallas_call x2, Pallas kernels, feed_call(): pl.pallas_call(feed_kernel, grid=(total // rows,), in_specs=[pl.BlockSpec...  31.5 us
  transfers between devices with their start and end apart: 63, of which 22 were waited for; matrix products, arithmetic and copies ran while one was open for 31% of the time, Pallas kernels for 27%

profile of v3, /device:TPU:1, one launch (start us, length us, event | category | flops | bytes accessed | tf_op | source)
XLA Modules:
  0.0 719.3 jit_solution(11605425167103150867)
XLA Ops:
  20.2 7.8 %collective-permute-done.6 = bf16[64,2048]{1,0:T(8,128)(2,1)S(1)} collective-permute-done((bf16[64,2048]{1,0:T(8,128)(2,1)S(1)}, bf16[64,2048]{1,0:T(8,128)(2,1)S(1)}, u32[]{:S(2)}, u32[]{:S(2)}) %collective-permute-start.6) | collective-permute-done | bytes 262176 | tf_op jit(solution)/shard_map/ppermute | solution.py:692
  35.1 10.4 %all-to-all-start.1 = ((bf16[8,64,1024]{2,1,0:T(8,128)(2,1)}), bf16[8,64,1024]{2,1,0:T(8,128)(2,1)}, u32[]{:S(2)}, u32[]{:S(2)}) async-start(bf16[8,64,1024]{2,1,0:T(8,128)(2,1)} %reshape.127), calls=%async_computation.1 | async-start | bytes 2097152 | tf_op jit(solution)/shard_map/all_to_all | solution.py:683
  57.4 7.6 %all-to-all-start.2 = ((bf16[8,64,1024]{2,1,0:T(8,128)(2,1)}), bf16[8,64,1024]{2,1,0:T(8,128)(2,1)S(1)}, u32[]{:S(2)}, u32[]{:S(2)}) async-start(bf16[8,64,1024]{2,1,0:T(8,128)(2,1)} %reshape.130), calls=%async_computation.2 | async-start | bytes 2097152 | tf_op jit(solution)/shard_map/all_to_all | solution.py:683
  70.8 9.8 %collective-permute-done.1 = bf16[256,2048]{1,0:T(8,128)(2,1)S(1)} collective-permute-done((bf16[256,2048]{1,0:T(8,128)(2,1)}, bf16[256,2048]{1,0:T(8,128)(2,1)S(1)}, u32[]{:S(2)}, u32[]{:S(2)}) %collective-permute-start.1) | collective-permute-done | bytes 1048608 | tf_op jit(solution)/shard_map/ppermute | solution.py:46
  80.6 10.6 %all-to-all-done.2 = bf16[8,64,1024]{2,1,0:T(8,128)(2,1)S(1)} async-done(((bf16[8,64,1024]{2,1,0:T(8,128)(2,1)}), bf16[8,64,1024]{2,1,0:T(8,128)(2,1)S(1)}, u32[]{:S(2)}, u32[]{:S(2)}) %all-to-all-start.2) | async-done | bytes 1048608 | tf_op jit(solution)/shard_map/all_to_all | solution.py:683
  105.9 32.2 %collective-permute-done.3 = bf16[128,2048]{1,0:T(8,128)(2,1)S(1)} collective-permute-done((bf16[128,2048]{1,0:T(8,128)(2,1)S(1)}, bf16[128,2048]{1,0:T(8,128)(2,1)S(1)}, u32[]{:S(2)}, u32[]{:S(2)}) %collective-permute-start.3) | collective-permute-done | bytes 524320 | tf_op jit(solution)/shard_map/ppermute | solution.py:46
  157.6 11.8 %qkv.1 = (bf16[2048,256]{1,0:T(8,128)(2,1)}, bf16[2048,128]{1,0:T(8,128)(2,1)}, bf16[2048,128]{1,0:T(8,128)(2,1)}, bf16[128,2048]{1,0:T(8,128)(2,1)}, bf16[128,2048]{1,0:T(8,128)(2,1)}) custom-call(bf16[2048,2048]{1,0:T(8,128)(2,1)} %constant_dynamic-update-slice_fusion.z_ref, bf16[4,768,512]{2,1,0:T(8,128)(2,1)} %bitcast.63, ...), custom_call_target="tpu_custom_call" | custom-call | flops 214748368 | bytes 524288 | tf_op jit(solution)/shard_map/qkv/pallas_call | solution.py:151
  169.4 21.5 %attend.1 = (bf16[2048,256]{1,0:T(8,128)(2,1)}, f32[8,1,512]{2,1,0:T(1,128)}) custom-call(s32[1]{0:T(128)} %bitcast.me_ref, bf16[2048,256]{1,0:T(8,128)(2,1)} %get-tuple-element.79.q_ref, bf16[2048,128]{1,0:T(8,128)(2,1)} %get-tuple-element.80.k_ref, bf16[128,2048]{1,0:T(8,128)(2,1)} %get-tuple-element.81.vt_ref), custom_call_target="tpu_custom_call" | custom-call | flops 214748368 | bytes 104857 | tf_op jit(solution)/shard_map/attend/pallas_call | solution.py:231
  215.2 10.1 %hidden.1 = (f32[256,2048]{1,0:T(8,128)}, bf16[256,2048]{1,0:T(8,128)(2,1)}, f32[256,1]{1,0:T(8,128)}) custom-call(s32[1]{0:T(128)} %bitcast.me_ref, bf16[8,256,256]{2,1,0:T(8,128)(2,1)} %copy-done.9, bf16[2048,2048]{1,0:T(8,128)(2,1)} %constant_dynamic-update-slice_fusion.7.w_ref, bf16[256,2048]{1,0:T(8,128)(2,1)} %bitcast.61), custom_call_target="tpu_custom_call" | custom-call | flops 107374184 | bytes 681574 | tf_op jit(solution)/shard_map/hidden/pallas_call | solution.py:487
  230.9 19.4 %collective-permute-done.14 = bf16[256,2048]{1,0:T(8,128)(2,1)S(1)} collective-permute-done((bf16[256,2048]{1,0:T(8,128)(2,1)}, bf16[256,2048]{1,0:T(8,128)(2,1)S(1)}, u32[]{:S(2)}, u32[]{:S(2)}) %collective-permute-start.14) | collective-permute-done | bytes 1048608 | tf_op jit(solution)/shard_map/ppermute | solution.py:46
  277.0 14.9 %back_act.1.g_ref = f32[2048,1024]{1,0:T(8,128)} custom-call(bf16[2048,2048]{1,0:T(8,128)(2,1)} %constant_dynamic-update-slice_fusion.21.g_ref, bf16[1024,2048]{1,0:T(8,128)(2,1)} %all-gather.7.cloned.1.call-done.d_ref), custom_call_target="tpu_custom_call" | custom-call | flops 429496736 | bytes 1048576 | tf_op jit(solution)/shard_map/back_act/pallas_call | solution.py:360
  302.8 15.7 %feed.2 = (bf16[2048,512]{1,0:T(8,128)(2,1)}, bf16[2048,1024]{1,0:T(8,128)(2,1)}) custom-call(bf16[2048,2048]{1,0:T(8,128)(2,1)} %constant_dynamic-update-slice_fusion.14.z_ref, f32[2048,1024]{1,0:T(8,128)} %back_act.1.g_ref, bf16[2048,1024]{1,0:T(8,128)(2,1)} %all-gather.9.cloned.1.call-done.w_ref.refs_1_), custom_call_target="tpu_custom_call" | custom-call | flops 429496736 | bytes 1153433 | tf_op jit(solution)/shard_map/feed/pallas_call | solution.py:393
  318.6 14.0 %convolution_convert_fusion.1 = bf16[2048,1024]{1,0:T(8,128)(2,1)} fusion(bf16[2048,2048]{1,0:T(8,128)(2,1)} %constant_dynamic-update-slice_fusion.14.z_ref, bf16[2048,1024]{1,0:T(8,128)(2,1)} %get-tuple-element.88.refs_0_), kind=kOutput, calls=%fused_computation.6 | convolution fusion | flops 8592031744 | bytes 16777216 | tf_op jit(solution)/shard_map/dot_general | solution.py:29
  333.0 9.0 %all-gather.11.cloned.1.call-done.w_ref.refs_3_ = bf16[2048,1024]{1,0:T(8,128)(2,1)} async-done(((bf16[512,1024]{1,0:T(8,128)(2,1)}), bf16[2048,1024]{1,0:T(8,128)(2,1)}) %all-gather.11.cloned.1.call-update) | async-done | bytes 4194320 | tf_op jit(solution)/shard_map/all_gather | solution.py:677
  342.0 15.8 %feed.3 = (bf16[2048,512]{1,0:T(8,128)(2,1)}, bf16[2048,1024]{1,0:T(8,128)(2,1)}) custom-call(bf16[2048,2048]{1,0:T(8,128)(2,1)} %constant_dynamic-update-slice_fusion.14.z_ref, f32[2048,1024]{1,0:T(8,128)} %back_act.1.g_ref, bf16[2048,1024]{1,0:T(8,128)(2,1)} %all-gather.11.cloned.1.call-done.w_ref.refs_3_), custom_call_target="tpu_custom_call" | custom-call | flops 429496736 | bytes 1153433 | tf_op jit(solution)/shard_map/feed/pallas_call | solution.py:393
  357.8 25.4 %g_two.1 = (bf16[1024,2048]{1,0:T(8,128)(2,1)}, bf16[1024,2048]{1,0:T(8,128)(2,1)}) custom-call(bf16[2048,1024]{1,0:T(8,128)(2,1)} %get-tuple-element.88.refs_0_, bf16[2048,1024]{1,0:T(8,128)(2,1)} %all-gather.9.cloned.1.call-done.w_ref.refs_1_, bf16[2048,1024]{1,0:T(8,128)(2,1)} %get-tuple-element.93.refs_2_, ...), custom_call_target="tpu_custom_call" | custom-call | flops 858993472 | bytes 1258291 | tf_op jit(solution)/shard_map/g_two/pallas_call | solution.py:444
  384.0 12.8 %convolution_convert_fusion = bf16[2048,1024]{1,0:T(8,128)(2,1)} fusion(bf16[2048,2048]{1,0:T(8,128)(2,1)} %constant_dynamic-update-slice_fusion.14.z_ref, bf16[2048,1024]{1,0:T(8,128)(2,1)S(1)} %copy-done.22), kind=kOutput, calls=%fused_computation.5 | convolution fusion | flops 8592031744 | bytes 16777216 | tf_op jit(solution)/shard_map/dot_general | solution.py:29
  409.2 15.2 %out.1 = (bf16[1024,2048]{1,0:T(8,128)(2,1)}, bf16[1024,2048]{1,0:T(8,128)(2,1)}) custom-call(bf16[2048,512]{1,0:T(8,128)(2,1)} %get-tuple-element.102.refs_0_, bf16[512,2048]{1,0:T(8,128)(2,1)} %get-tuple-element.172.refs_1_, bf16[2048,512]{1,0:T(8,128)(2,1)} %get-tuple-element.103.refs_2_, bf16[512,2048]{1,0:T(8,128)(2,1)} %get-tuple-element.171.refs_3_), custom_call_target="tpu_custom_call" | custom-call | flops 429496736 | bytes 838860 | tf_op jit(solution)/shard_map/out/pallas_call | solution.py:444
  430.4 9.1 %convolution_convert_fusion.3 = bf16[512,2048]{1,0:T(8,128)(2,1)} fusion(bf16[2048,512]{1,0:T(8,128)(2,1)S(1)} %copy-done.24, bf16[2048,2048]{1,0:T(8,128)(2,1)} %constant_dynamic-update-slice_fusion.21.g_ref), kind=kOutput, calls=%fused_computation.12 | convolution fusion | flops 4296015872 | bytes 12582912 | tf_op jit(solution)/shard_map/dot_general | solution.py:29
  439.5 9.2 %convolution_convert_fusion.4 = bf16[512,2048]{1,0:T(8,128)(2,1)} fusion(bf16[2048,512]{1,0:T(8,128)(2,1)S(1)} %copy-done.23, bf16[2048,2048]{1,0:T(8,128)(2,1)} %constant_dynamic-update-slice_fusion.21.g_ref), kind=kOutput, calls=%fused_computation.13 | convolution fusion | flops 4296015872 | bytes 12582912 | tf_op jit(solution)/shard_map/dot_general | solution.py:29
  458.6 8.8 %back_attn.1 = bf16[8,256,256]{2,1,0:T(8,128)(2,1)} custom-call(s32[1]{0:T(128)} %bitcast.me_ref, bf16[256,2048]{1,0:T(8,128)(2,1)} %get-tuple-element.110.g_ref, bf16[2048,2048]{1,0:T(8,128)(2,1)} %constant_dynamic-update-slice_fusion.7.w_ref), custom_call_target="tpu_custom_call" | custom-call | flops 107374184 | bytes 524288 | tf_op jit(solution)/shard_map/back_attn/pallas_call | solution.py:524
  467.4 9.2 %grad_wo.1 = (bf16[1024,2048]{1,0:T(8,128)(2,1)}, bf16[1024,2048]{1,0:T(8,128)(2,1)}) custom-call(s32[1]{0:T(128)} %bitcast.me_ref, bf16[8,256,256]{2,1,0:T(8,128)(2,1)} %copy-done.9, bf16[256,2048]{1,0:T(8,128)(2,1)} %get-tuple-element.110.g_ref), custom_call_target="tpu_custom_call" | custom-call | flops 107374184 | bytes 524288 | tf_op jit(solution)/shard_map/grad_wo/pallas_call | solution.py:556
  486.0 6.9 all-to-all-done.4
  505.9 24.4 %attend_back.1.refs_0_ = bf16[2048,512]{1,0:T(8,128)(2,1)} custom-call(s32[1]{0:T(128)} %bitcast.me_ref, bf16[2048,256]{1,0:T(8,128)(2,1)} %get-tuple-element.79.q_ref, bf16[2048,256]{1,0:T(8,128)(2,1)} %bitcast.71, bf16[2048,256]{1,0:T(8,128)(2,1)} %get-tuple-element.82.o_ref, f32[8,1,512]{2,1,0:T(1,128)} %get-tuple-element.113.lse_ref, ...), custom_call_target="tpu_custom_call" | custom-call | flops 536870912 | bytes 209715 | tf_op jit(solution)/shard_map/attend_back/pallas_call | solution.py:327
  546.1 9.5 %convolution_convert_fusion.2 = bf16[2048,512]{1,0:T(8,128)(2,1)} fusion(bf16[2048,2048]{1,0:T(8,128)(2,1)} %constant_dynamic-update-slice_fusion.z_ref, bf16[2048,512]{1,0:T(8,128)(2,1)S(1)} %copy-done.11), kind=kOutput, calls=%fused_computation.11 | convolution fusion | flops 4296015872 | bytes 12582912 | tf_op jit(solution)/shard_map/dot_general | solution.py:29
  563.3 11.3 %g_one.1 = (bf16[1024,2048]{1,0:T(8,128)(2,1)}, bf16[1024,2048]{1,0:T(8,128)(2,1)}) custom-call(bf16[2048,512]{1,0:T(8,128)(2,1)} %attend_back.1.refs_0_, bf16[2048,512]{1,0:T(8,128)(2,1)} %bitcast.69), custom_call_target="tpu_custom_call" | custom-call | flops 214748368 | bytes 629145 | tf_op jit(solution)/shard_map/g_one/pallas_call | solution.py:444
  585.4 16.0 %collective-permute-done.34 = bf16[256,2048]{1,0:T(8,128)(2,1)} collective-permute-done((bf16[256,2048]{1,0:T(8,128)(2,1)}, bf16[256,2048]{1,0:T(8,128)(2,1)}, u32[]{:S(2)}, u32[]{:S(2)}) %collective-permute-start.34) | collective-permute-done | bytes 1048608 | tf_op jit(solution)/shard_map/ppermute | solution.py:46
  617.1 17.9 %collective-permute-done.43 = bf16[256,2048]{1,0:T(8,128)(2,1)S(1)} collective-permute-done((bf16[256,2048]{1,0:T(8,128)(2,1)}, bf16[256,2048]{1,0:T(8,128)(2,1)S(1)}, u32[]{:S(2)}, u32[]{:S(2)}) %collective-permute-start.43) | collective-permute-done | bytes 1048608 | tf_op jit(solution)/shard_map/ppermute | solution.py:46
  641.6 7.4 %collective-permute-done.41 = bf16[128,2048]{1,0:T(8,128)(2,1)S(1)} collective-permute-done((bf16[128,2048]{1,0:T(8,128)(2,1)}, bf16[128,2048]{1,0:T(8,128)(2,1)S(1)}, u32[]{:S(2)}, u32[]{:S(2)}) %collective-permute-start.41) | collective-permute-done | bytes 524320 | tf_op jit(solution)/shard_map/ppermute | solution.py:46
  654.9 6.9 all-to-all-start.7
  672.4 11.3 %all-to-all-done.7.got_ref = bf16[8,64,512]{2,1,0:T(8,128)(2,1)} async-done(((bf16[8,64,512]{2,1,0:T(8,128)(2,1)}), bf16[8,64,512]{2,1,0:T(8,128)(2,1)}, u32[]{:S(2)}, u32[]{:S(2)}) %all-to-all-start.7) | async-done | bytes 524320 | tf_op jit(solution)/shard_map/all_to_all | solution.py:683
  698.6 13.1 %collective-permute-done.45 = bf16[64,2048]{1,0:T(8,128)(2,1)S(1)} collective-permute-done((bf16[64,2048]{1,0:T(8,128)(2,1)}, bf16[64,2048]{1,0:T(8,128)(2,1)S(1)}, u32[]{:S(2)}, u32[]{:S(2)}) %collective-permute-start.45) | collective-permute-done | bytes 262176 | tf_op jit(solution)/shard_map/ppermute | solution.py:789
  (309 shorter events, 279.4 us)
Async XLA Ops:
  17.1 81.6 %all-gather.5.cloned.1.call-start = ((), (), s32[]{:S(2)}) async-start(), calls=%async_computation.13 | async-start | bytes 3932160 | tf_op jit(solution)/shard_map/all_gather | solution.py:677
  29.2 247.8 %all-gather.7.cloned.1.call-start = ((), (), s32[]{:S(2)}) async-start(), calls=%async_computation.14 | async-start | bytes 5242880 | tf_op jit(solution)/shard_map/all_gather | solution.py:677
  47.0 33.6 %collective-permute-start.1 = (bf16[256,2048]{1,0:T(8,128)(2,1)}, bf16[256,2048]{1,0:T(8,128)(2,1)S(1)}, u32[]{:S(2)}, u32[]{:S(2)}) collective-permute-start(bf16[256,2048]{1,0:T(8,128)(2,1)} %get-tuple-element.146), channel_id=1, source_target_pairs={{0,4},{1,5},{2,6},{3,7},{4,0},{5,1},{6,2},{7,3},{8,12},{9,13},{10,... | collective-permute-start | bytes 3145736 | tf_op jit(solution)/shard_map/ppermute | solution.py:46
  48.4 42.8 %collective-permute-start = (bf16[256,2048]{1,0:T(8,128)(2,1)}, bf16[256,2048]{1,0:T(8,128)(2,1)S(1)}, u32[]{:S(2)}, u32[]{:S(2)}) collective-permute-start(bf16[256,2048]{1,0:T(8,128)(2,1)} %get-tuple-element.146), channel_id=1, source_target_pairs={{0,2},{1,3},{2,0},{3,1},{4,6},{5,7},{6,4},{7,5},{8,10},{9,11},{10,... | collective-permute-start | bytes 3145736 | tf_op jit(solution)/shard_map/ppermute | solution.py:46
  57.4 33.8 %all-to-all-start.2 = ((bf16[8,64,1024]{2,1,0:T(8,128)(2,1)}), bf16[8,64,1024]{2,1,0:T(8,128)(2,1)S(1)}, u32[]{:S(2)}, u32[]{:S(2)}) async-start(bf16[8,64,1024]{2,1,0:T(8,128)(2,1)} %reshape.130), calls=%async_computation.2 | async-start | bytes 2097152 | tf_op jit(solution)/shard_map/all_to_all | solution.py:683
  65.0 237.8 %all-gather.9.cloned.1.call-start = ((), (), s32[]{:S(2)}) async-start(), calls=%async_computation.15 | async-start | bytes 5242880 | tf_op jit(solution)/shard_map/all_gather | solution.py:677
  94.5 52.3 %collective-permute-start.4 = (bf16[768,2048]{1,0:T(8,128)(2,1)}, bf16[768,2048]{1,0:T(8,128)(2,1)}, u32[]{:S(2)}, u32[]{:S(2)}) collective-permute-start(bf16[768,2048]{1,0:T(8,128)(2,1)} %pad_maximum_fusion.1), channel_id=1, source_target_pairs={{0,1},{1,0},{2,3},{3,2},{4,5},{5,4},{6,7},{7,6},{8,9},{9,8},{10,11... | collective-permute-start | bytes 9437192 | tf_op jit(solution)/shard_map/ppermute | solution.py:46
  102.7 38.2 %collective-permute-start.8 = (bf16[256,2048]{1,0:T(8,128)(2,1)S(1)}, bf16[256,2048]{1,0:T(8,128)(2,1)S(1)}, u32[]{:S(2)}, u32[]{:S(2)}) collective-permute-start(bf16[256,2048]{1,0:T(8,128)(2,1)S(1)} %reshape.134), channel_id=1, source_target_pairs={{0,4},{1,5},{2,6},{3,7},{4,0},{5,1},{6,2},{7,3},{8,12},{9,13},{10,... | collective-permute-start | bytes 3145736 | tf_op jit(solution)/shard_map/ppermute | solution.py:46
  103.9 37.0 %collective-permute-start.7 = (bf16[256,2048]{1,0:T(8,128)(2,1)S(1)}, bf16[256,2048]{1,0:T(8,128)(2,1)S(1)}, u32[]{:S(2)}, u32[]{:S(2)}) collective-permute-start(bf16[256,2048]{1,0:T(8,128)(2,1)S(1)} %reshape.134), channel_id=1, source_target_pairs={{0,2},{1,3},{2,0},{3,1},{4,6},{5,7},{6,4},{7,5},{8,10},{9,11},{10,... | collective-permute-start | bytes 3145736 | tf_op jit(solution)/shard_map/ppermute | solution.py:46
  105.5 33.4 %collective-permute-start.2 = (bf16[128,2048]{1,0:T(8,128)(2,1)S(1)}, bf16[128,2048]{1,0:T(8,128)(2,1)S(1)}, u32[]{:S(2)}, u32[]{:S(2)}) collective-permute-start(bf16[128,2048]{1,0:T(8,128)(2,1)S(1)} %slice.172), channel_id=1, source_target_pairs={{0,2},{1,3},{2,0},{3,1},{4,6},{5,7},{6,4},{7,5},{8,10},{9,11},{10,... | collective-permute-start | bytes 1572872 | tf_op jit(solution)/shard_map/ppermute | solution.py:46
  142.9 66.3 %collective-permute-start.11 = (bf16[768,2048]{1,0:T(8,128)(2,1)}, bf16[768,2048]{1,0:T(8,128)(2,1)}, u32[]{:S(2)}, u32[]{:S(2)}) collective-permute-start(bf16[768,2048]{1,0:T(8,128)(2,1)} %pad_maximum_fusion.2), channel_id=1, source_target_pairs={{0,1},{1,0},{2,3},{3,2},{4,5},{5,4},{6,7},{7,6},{8,9},{9,8},{10,11... | collective-permute-start | bytes 9437192 | tf_op jit(solution)/shard_map/ppermute | solution.py:46
  151.9 50.2 %collective-permute-start.20 = (bf16[256,2048]{1,0:T(8,128)(2,1)S(1)}, bf16[256,2048]{1,0:T(8,128)(2,1)S(1)}, u32[]{:S(2)}, u32[]{:S(2)}) collective-permute-start(bf16[256,2048]{1,0:T(8,128)(2,1)S(1)} %bitcast.65), channel_id=1, source_target_pairs={{0,4},{1,5},{2,6},{3,7},{4,0},{5,1},{6,2},{7,3},{8,12},{9,13},{10,... | collective-permute-start | bytes 3145736 | tf_op jit(solution)/shard_map/ppermute | solution.py:46
  152.2 50.0 %collective-permute-start.19 = (bf16[256,2048]{1,0:T(8,128)(2,1)S(1)}, bf16[256,2048]{1,0:T(8,128)(2,1)}, u32[]{:S(2)}, u32[]{:S(2)}) collective-permute-start(bf16[256,2048]{1,0:T(8,128)(2,1)S(1)} %bitcast.66), channel_id=1, source_target_pairs={{0,2},{1,3},{2,0},{3,1},{4,6},{5,7},{6,4},{7,5},{8,10},{9,11},{10,... | collective-permute-start | bytes 3145736 | tf_op jit(solution)/shard_map/ppermute | solution.py:46
  155.2 45.4 %collective-permute-start.9 = (bf16[128,2048]{1,0:T(8,128)(2,1)}, bf16[128,2048]{1,0:T(8,128)(2,1)}, u32[]{:S(2)}, u32[]{:S(2)}) collective-permute-start(bf16[128,2048]{1,0:T(8,128)(2,1)} %slice.218), channel_id=1, source_target_pairs={{0,2},{1,3},{2,0},{3,1},{4,6},{5,7},{6,4},{7,5},{8,10},{9,11},{10,... | collective-permute-start | bytes 1572872 | tf_op jit(solution)/shard_map/ppermute | solution.py:46
  156.4 44.2 %collective-permute-start.10 = (bf16[128,2048]{1,0:T(8,128)(2,1)}, bf16[128,2048]{1,0:T(8,128)(2,1)}, u32[]{:S(2)}, u32[]{:S(2)}) collective-permute-start(bf16[128,2048]{1,0:T(8,128)(2,1)} %slice.219), channel_id=1, source_target_pairs={{0,4},{1,5},{2,6},{3,7},{4,0},{5,1},{6,2},{7,3},{8,12},{9,13},{10,... | collective-permute-start | bytes 1572872 | tf_op jit(solution)/shard_map/ppermute | solution.py:46
  195.9 146.1 %all-gather.11.cloned.1.call-start = ((), (), s32[]{:S(2)}) async-start(), calls=%async_computation.16 | async-start | bytes 5242880 | tf_op jit(solution)/shard_map/all_gather | solution.py:677
  205.0 66.8 %collective-permute-start.23 = (bf16[768,2048]{1,0:T(8,128)(2,1)}, bf16[768,2048]{1,0:T(8,128)(2,1)}, u32[]{:S(2)}, u32[]{:S(2)}) collective-permute-start(bf16[768,2048]{1,0:T(8,128)(2,1)} %pad_maximum_fusion.4), channel_id=1, source_target_pairs={{0,1},{1,0},{2,3},{3,2},{4,5},{5,4},{6,7},{7,6},{8,9},{9,8},{10,11... | collective-permute-start | bytes 9437192 | tf_op jit(solution)/shard_map/ppermute | solution.py:46
  228.0 258.0 %reduce-scatter.6.cloned.1.call-start = ((), (), s32[]{:S(2)}) async-start(), calls=%async_computation.17 | async-start | bytes 5242880 | tf_op jit(solution)/shard_map/reduce_scatter | solution.py:680
  254.0 43.7 %collective-permute-start.17 = (bf16[768,2048]{1,0:T(8,128)(2,1)}, bf16[768,2048]{1,0:T(8,128)(2,1)}, u32[]{:S(2)}, u32[]{:S(2)}) collective-permute-start(bf16[768,2048]{1,0:T(8,128)(2,1)} %pad_maximum_fusion.3), channel_id=1, source_target_pairs={{0,1},{1,0},{2,3},{3,2},{4,5},{5,4},{6,7},{7,6},{8,9},{9,8},{10,11... | collective-permute-start | bytes 9437192 | tf_op jit(solution)/shard_map/ppermute | solution.py:46
  332.6 208.0 %reduce-scatter.8.cloned.1.call-start = ((), (), s32[]{:S(2)}) async-start(), calls=%async_computation.18 | async-start | bytes 5242880 | tf_op jit(solution)/shard_map/reduce_scatter | solution.py:680
  476.6 58.0 %collective-permute-start.35 = (bf16[1024,2048]{1,0:T(8,128)(2,1)}, bf16[1024,2048]{1,0:T(8,128)(2,1)}, u32[]{:S(2)}, u32[]{:S(2)}) collective-permute-start(bf16[1024,2048]{1,0:T(8,128)(2,1)} %get-tuple-element.112), channel_id=1, source_target_pairs={{0,1},{1,0},{2,3},{3,2},{4,5},{5,4},{6,7},{7,6},{8,9},{9,8},{10,11... | collective-permute-start | bytes 12582920 | tf_op jit(solution)/shard_map/ppermute | solution.py:46
  481.0 160.6 %reduce-scatter.12.cloned.1.call-start = ((), (), s32[]{:S(2)}) async-start(), calls=%async_computation.20 | async-start | bytes 5242880 | tf_op jit(solution)/shard_map/reduce_scatter | solution.py:680
  496.2 34.1 %collective-permute-start.32 = (bf16[128,2048]{1,0:T(8,128)(2,1)}, bf16[128,2048]{1,0:T(8,128)(2,1)}, u32[]{:S(2)}, u32[]{:S(2)}) collective-permute-start(bf16[128,2048]{1,0:T(8,128)(2,1)} %get-tuple-element.161), channel_id=1, source_target_pairs={{0,4},{1,5},{2,6},{3,7},{4,0},{5,1},{6,2},{7,3},{8,12},{9,13},{10,... | collective-permute-start | bytes 1572872 | tf_op jit(solution)/shard_map/ppermute | solution.py:46
  501.1 62.2 %all-to-all-start.5 = ((bf16[8,64,1024]{2,1,0:T(8,128)(2,1)}), bf16[8,64,1024]{2,1,0:T(8,128)(2,1)S(1)}, u32[]{:S(2)}, u32[]{:S(2)}) async-start(bf16[8,64,1024]{2,1,0:T(8,128)(2,1)} %bitcast.80), calls=%async_computation.6 | async-start | bytes 2097152 | tf_op jit(solution)/shard_map/all_to_all | solution.py:683
  505.9 148.9 %reduce-scatter.10.cloned.1.call-start = ((), (), s32[]{:S(2)}) async-start(), calls=%async_computation.19 | async-start | bytes 2621440 | tf_op jit(solution)/shard_map/reduce_scatter | solution.py:680
  574.7 37.0 %collective-permute-start.38 = (bf16[1024,2048]{1,0:T(8,128)(2,1)}, bf16[1024,2048]{1,0:T(8,128)(2,1)}, u32[]{:S(2)}, u32[]{:S(2)}) collective-permute-start(bf16[1024,2048]{1,0:T(8,128)(2,1)} %get-tuple-element.125), channel_id=1, source_target_pairs={{0,1},{1,0},{2,3},{3,2},{4,5},{5,4},{6,7},{7,6},{8,9},{9,8},{10,11... | collective-permute-start | bytes 12582920 | tf_op jit(solution)/shard_map/ppermute | solution.py:46
  577.8 33.9 %all-to-all-start.6 = ((bf16[8,64,1024]{2,1,0:T(8,128)(2,1)}), bf16[8,64,1024]{2,1,0:T(8,128)(2,1)}, u32[]{:S(2)}, u32[]{:S(2)}) async-start(bf16[8,64,1024]{2,1,0:T(8,128)(2,1)} %bitcast.79), calls=%async_computation.8 | async-start | bytes 2097152 | tf_op jit(solution)/shard_map/all_to_all | solution.py:683
  582.5 107.5 %reduce-scatter.14.cloned.1.call-start = ((), (), s32[]{:S(2)}) async-start(), calls=%async_computation.21 | async-start | bytes 1310720 | tf_op jit(solution)/shard_map/reduce_scatter | solution.py:680
  582.7 52.3 %collective-permute-start.43 = (bf16[256,2048]{1,0:T(8,128)(2,1)}, bf16[256,2048]{1,0:T(8,128)(2,1)S(1)}, u32[]{:S(2)}, u32[]{:S(2)}) collective-permute-start(bf16[256,2048]{1,0:T(8,128)(2,1)} %pad_maximum_fusion.15), channel_id=1, source_target_pairs={{0,2},{1,3},{2,0},{3,1},{4,6},{5,7},{6,4},{7,5},{8,10},{9,11},{10,... | collective-permute-start | bytes 3145736 | tf_op jit(solution)/shard_map/ppermute | solution.py:46
  584.2 50.9 %collective-permute-start.44 = (bf16[256,2048]{1,0:T(8,128)(2,1)}, bf16[256,2048]{1,0:T(8,128)(2,1)}, u32[]{:S(2)}, u32[]{:S(2)}) collective-permute-start(bf16[256,2048]{1,0:T(8,128)(2,1)} %pad_maximum_fusion.16), channel_id=1, source_target_pairs={{0,4},{1,5},{2,6},{3,7},{4,0},{5,1},{6,2},{7,3},{8,12},{9,13},{10,... | collective-permute-start | bytes 3145736 | tf_op jit(solution)/shard_map/ppermute | solution.py:46
  652.6 34.8 %collective-permute-start.40 = (bf16[256,2048]{1,0:T(8,128)(2,1)}, bf16[256,2048]{1,0:T(8,128)(2,1)}, u32[]{:S(2)}, u32[]{:S(2)}) collective-permute-start(bf16[256,2048]{1,0:T(8,128)(2,1)} %pad_maximum_fusion.17), channel_id=1, source_target_pairs={{0,2},{1,3},{2,0},{3,1},{4,6},{5,7},{6,4},{7,5},{8,10},{9,11},{10,... | collective-permute-start | bytes 3145736 | tf_op jit(solution)/shard_map/ppermute | solution.py:46
  654.0 33.4 %collective-permute-start.42 = (bf16[256,2048]{1,0:T(8,128)(2,1)}, bf16[256,2048]{1,0:T(8,128)(2,1)}, u32[]{:S(2)}, u32[]{:S(2)}) collective-permute-start(bf16[256,2048]{1,0:T(8,128)(2,1)} %pad_maximum_fusion.18), channel_id=1, source_target_pairs={{0,4},{1,5},{2,6},{3,7},{4,0},{5,1},{6,2},{7,3},{8,12},{9,13},{10,... | collective-permute-start | bytes 3145736 | tf_op jit(solution)/shard_map/ppermute | solution.py:46
  (68 other events, 1105.8 us)
Sparse Core Ops, SparseCore 0:
  29.3 69.3 all-gather.4
  100.3 79.4 all-gather.6
  181.3 79.2 all-gather.8
  262.7 79.2 all-gather.10
  344.2 75.2 reduce-scatter.5
  421.8 77.2 reduce-scatter.7
  501.3 77.2 reduce-scatter.11
  581.6 44.1 reduce-scatter.9
  641.7 25.1 reduce-scatter.13

commit v4 on v3

--- a/solution.py
+++ b/solution.py
@@ -764,24 +764,23 @@
     g_hidden = g_out + rms_two * (u - z_two * jnp.mean(u * z_two, -1, keepdims=True))
     g_hidb = g_hidden.astype(BF)
     g_heads = back_attn_call(me_arr, g_hidb, wo_rel, n_cp)
-    g_mixed = give(g_heads).reshape(total, feat)
     wo_part = grad_wo_call(me_arr, attn, after(g_hidb, g_heads), n_cp)
+    out_state = scatter_mid(after(out_acc, g_hidb), n_cp, *wo_part)
+    g_mixed = give(after(g_heads, *out_state)).reshape(total, feat)
     back_gu = [give(after(red_gu[0].reshape(n_cp, own, 2 * cut), g_mixed))]
-    lse = after(lse, *wo_part)
     g_qkv = attend_back_call(me_arr, q, g_mixed, mixed, lse, k, kt, v, cos, sin, rows, heads, n_cp)
-    out_state = scatter_mid(after(out_acc, g_mixed), n_cp, g_qkv)
-    wo_acc = scatter_first(*wo_part, n_cp, g_qkv)
-    part_qkv = mm(z_one_all, after(g_qkv, wo_acc, red_gu[1], *out_state), TN).astype(BF)
+    out_sum = scatter_last(after(out_state, g_mixed), n_cp, g_qkv)
+    output = hid + out_sum
+    wo_acc = scatter_first(*wo_part, n_cp, g_qkv, out_sum)
+    w_qkv = joint[:, :depth].reshape(width, qkv_cols)
+    part = sum_call([(after(g_qkv, wo_acc), w_qkv)], NT, rows, "g_one")
+    wo_state = scatter_mid(wo_acc, n_cp, *part)
+    part_qkv = mm(z_one_all, after(g_qkv, red_gu[1], back_gu[0], *wo_state), TN).astype(BF)
     red_qkv = scatter_z(part_qkv)
-    back_gu.append(give(after(red_gu[1].reshape(n_cp, own, 2 * cut), g_qkv)))
-    wo_state = scatter_mid(wo_acc, n_cp, part_qkv)
-    w_qkv = joint[:, :depth].reshape(width, qkv_cols)
-    part = sum_call([(after(g_qkv, back_gu[0], *wo_state), w_qkv)], NT, rows, "g_one")
-    out_sum = scatter_last(out_state, n_cp)
-    output = hid + out_sum
-    w_acc = scatter_first(*part, n_cp, back_gu[1], out_sum)
+    back_gu.append(give(after(red_gu[1].reshape(n_cp, own, 2 * cut), part_qkv)))
+    w_acc = scatter_first(*part, n_cp, part_qkv)
     wo_sum = scatter_last(wo_state, n_cp, w_acc).astype(BF)
-    w_state = scatter_mid(w_acc, n_cp)
+    w_state = scatter_mid(w_acc, n_cp, back_gu[1])
 
     wo_sum = scatter_z(after(wo_sum, grad_down))
     got = give(red_qkv.reshape(n_cp, own, qkv_cols))

time: 727 us -> 699 us (0.961)
  waiting for transfers between devices: 183 us -> 151 us
  blocking collectives: 0 us -> 17.3 us
    ppermute x44, waiting for transfers between devices: 111 us -> 91.2 us  [swap(): return lax.ppermute(value, 'cp', [(i, i ^ offset) for i in range(count)])]
    all_to_all x0 -> x1, blocking collectives: none -> 17.3 us  [give(): return lax.all_to_all(value, 'cp', 0, 0)]
    all_to_all x8 -> x7, waiting for transfers between devices: 39.9 us -> 30.2 us  [give(): return lax.all_to_all(value, 'cp', 0, 0)]
    all_to_all x8 -> x7, starting transfers between devices: 48 us -> 44.1 us  [give(): return lax.all_to_all(value, 'cp', 0, 0)]
    unnamed x103 -> x107, local copies, waits for them, and re-layouts: 43.9 us -> 46.7 us
  transfers between devices with their start and end apart: 63 -> 62, of which waited for: 22 -> 18; matrix products, arithmetic and copies ran while one was open for 31% -> 30% of each run, Pallas kernels for 27% -> 28%
where the time goes in v4:
time: 699 us; the launch traced here: 691 us
  Pallas kernels  192 us (27%)
  waiting for transfers between devices  151 us (22%)
  starting transfers between devices  95.6 us (14%)
  other arithmetic  88.2 us (13%)
  local copies, waits for them, and re-layouts  77.5 us (11%)
  matrix products  55 us (8%)
  blocking collectives  17.3 us (2%)
  between operations  14.8 us (2%)
    ppermute x44, waiting for transfers between devices, swap(): return lax.ppermute(value, 'cp', [(i, i ^ offset) for i in range(count)])  91.2 us
    dot_general x5, matrix products, mm(): return lax.dot_general(left, right, dims, preferred_element_type=F32)  55 us
    pallas_call x3, Pallas kernels, sum_call(): pl.pallas_call(functools.partial(sum_kernel, dims=dims), grid=(total // r...  51.7 us
    unnamed x107, local copies, waits for them, and re-layouts  46.7 us
    all_to_all x7, starting transfers between devices, give(): return lax.all_to_all(value, 'cp', 0, 0)  44.1 us
    ppermute x44, starting transfers between devices, swap(): return lax.ppermute(value, 'cp', [(i, i ^ offset) for i in range(count)])  42 us
    pallas_call x2, Pallas kernels, feed_call(): pl.pallas_call(feed_kernel, grid=(total // rows,), in_specs=[pl.BlockSpec...  31.5 us
    all_to_all x7, waiting for transfers between devices, give(): return lax.all_to_all(value, 'cp', 0, 0)  30.2 us
  transfers between devices with their start and end apart: 62, of which 18 were waited for; matrix products, arithmetic and copies ran while one was open for 30% of the time, Pallas kernels for 28%

profile of v4, /device:TPU:1, one launch (start us, length us, event | category | flops | bytes accessed | tf_op | source)
XLA Modules:
  0.0 691.0 jit_solution(14860812115798620903)
XLA Ops:
  20.2 7.8 %collective-permute-done.6 = bf16[64,2048]{1,0:T(8,128)(2,1)S(1)} collective-permute-done((bf16[64,2048]{1,0:T(8,128)(2,1)S(1)}, bf16[64,2048]{1,0:T(8,128)(2,1)S(1)}, u32[]{:S(2)}, u32[]{:S(2)}) %collective-permute-start.6) | collective-permute-done | bytes 262176 | tf_op jit(solution)/shard_map/ppermute | solution.py:692
  35.0 10.4 %all-to-all-start.1 = ((bf16[8,64,1024]{2,1,0:T(8,128)(2,1)}), bf16[8,64,1024]{2,1,0:T(8,128)(2,1)}, u32[]{:S(2)}, u32[]{:S(2)}) async-start(bf16[8,64,1024]{2,1,0:T(8,128)(2,1)} %reshape.127), calls=%async_computation.1 | async-start | bytes 2097152 | tf_op jit(solution)/shard_map/all_to_all | solution.py:683
  57.4 7.6 %all-to-all-start.2 = ((bf16[8,64,1024]{2,1,0:T(8,128)(2,1)}), bf16[8,64,1024]{2,1,0:T(8,128)(2,1)S(1)}, u32[]{:S(2)}, u32[]{:S(2)}) async-start(bf16[8,64,1024]{2,1,0:T(8,128)(2,1)} %reshape.130), calls=%async_computation.2 | async-start | bytes 2097152 | tf_op jit(solution)/shard_map/all_to_all | solution.py:683
  70.8 9.8 %collective-permute-done.1 = bf16[256,2048]{1,0:T(8,128)(2,1)S(1)} collective-permute-done((bf16[256,2048]{1,0:T(8,128)(2,1)}, bf16[256,2048]{1,0:T(8,128)(2,1)S(1)}, u32[]{:S(2)}, u32[]{:S(2)}) %collective-permute-start.1) | collective-permute-done | bytes 1048608 | tf_op jit(solution)/shard_map/ppermute | solution.py:46
  80.6 10.6 %all-to-all-done.2 = bf16[8,64,1024]{2,1,0:T(8,128)(2,1)S(1)} async-done(((bf16[8,64,1024]{2,1,0:T(8,128)(2,1)}), bf16[8,64,1024]{2,1,0:T(8,128)(2,1)S(1)}, u32[]{:S(2)}, u32[]{:S(2)}) %all-to-all-start.2) | async-done | bytes 1048608 | tf_op jit(solution)/shard_map/all_to_all | solution.py:683
  105.9 32.2 %collective-permute-done.3 = bf16[128,2048]{1,0:T(8,128)(2,1)S(1)} collective-permute-done((bf16[128,2048]{1,0:T(8,128)(2,1)S(1)}, bf16[128,2048]{1,0:T(8,128)(2,1)S(1)}, u32[]{:S(2)}, u32[]{:S(2)}) %collective-permute-start.3) | collective-permute-done | bytes 524320 | tf_op jit(solution)/shard_map/ppermute | solution.py:46
  157.7 11.8 %qkv.1 = (bf16[2048,256]{1,0:T(8,128)(2,1)}, bf16[2048,128]{1,0:T(8,128)(2,1)}, bf16[2048,128]{1,0:T(8,128)(2,1)}, bf16[128,2048]{1,0:T(8,128)(2,1)}, bf16[128,2048]{1,0:T(8,128)(2,1)}) custom-call(bf16[2048,2048]{1,0:T(8,128)(2,1)} %constant_dynamic-update-slice_fusion.z_ref, bf16[4,768,512]{2,1,0:T(8,128)(2,1)} %bitcast.63, ...), custom_call_target="tpu_custom_call" | custom-call | flops 214748368 | bytes 524288 | tf_op jit(solution)/shard_map/qkv/pallas_call | solution.py:151
  169.5 21.5 %attend.1 = (bf16[2048,256]{1,0:T(8,128)(2,1)}, f32[8,1,512]{2,1,0:T(1,128)}) custom-call(s32[1]{0:T(128)} %bitcast.me_ref, bf16[2048,256]{1,0:T(8,128)(2,1)} %get-tuple-element.86.q_ref, bf16[2048,128]{1,0:T(8,128)(2,1)} %get-tuple-element.87.k_ref, bf16[128,2048]{1,0:T(8,128)(2,1)} %get-tuple-element.88.vt_ref), custom_call_target="tpu_custom_call" | custom-call | flops 214748368 | bytes 104857 | tf_op jit(solution)/shard_map/attend/pallas_call | solution.py:231
  215.3 10.1 %hidden.1 = (f32[256,2048]{1,0:T(8,128)}, bf16[256,2048]{1,0:T(8,128)(2,1)}, f32[256,1]{1,0:T(8,128)}) custom-call(s32[1]{0:T(128)} %bitcast.me_ref, bf16[8,256,256]{2,1,0:T(8,128)(2,1)} %copy-done.11, bf16[2048,2048]{1,0:T(8,128)(2,1)} %constant_dynamic-update-slice_fusion.7.w_ref, bf16[256,2048]{1,0:T(8,128)(2,1)} %bitcast.61), custom_call_target="tpu_custom_call" | custom-call | flops 107374184 | bytes 681574 | tf_op jit(solution)/shard_map/hidden/pallas_call | solution.py:487
  231.0 19.4 %collective-permute-done.14 = bf16[256,2048]{1,0:T(8,128)(2,1)S(1)} collective-permute-done((bf16[256,2048]{1,0:T(8,128)(2,1)}, bf16[256,2048]{1,0:T(8,128)(2,1)S(1)}, u32[]{:S(2)}, u32[]{:S(2)}) %collective-permute-start.14) | collective-permute-done | bytes 1048608 | tf_op jit(solution)/shard_map/ppermute | solution.py:46
  277.2 15.0 %back_act.1.g_ref = f32[2048,1024]{1,0:T(8,128)} custom-call(bf16[2048,2048]{1,0:T(8,128)(2,1)} %constant_dynamic-update-slice_fusion.21.g_ref, bf16[1024,2048]{1,0:T(8,128)(2,1)} %all-gather.7.cloned.1.call-done.d_ref), custom_call_target="tpu_custom_call" | custom-call | flops 429496736 | bytes 1048576 | tf_op jit(solution)/shard_map/back_act/pallas_call | solution.py:360
  303.1 15.7 %feed.2 = (bf16[2048,512]{1,0:T(8,128)(2,1)}, bf16[2048,1024]{1,0:T(8,128)(2,1)}) custom-call(bf16[2048,2048]{1,0:T(8,128)(2,1)} %constant_dynamic-update-slice_fusion.14.z_ref, f32[2048,1024]{1,0:T(8,128)} %back_act.1.g_ref, bf16[2048,1024]{1,0:T(8,128)(2,1)} %all-gather.9.cloned.1.call-done.w_ref.refs_1_), custom_call_target="tpu_custom_call" | custom-call | flops 429496736 | bytes 1153433 | tf_op jit(solution)/shard_map/feed/pallas_call | solution.py:393
  318.8 14.0 %convolution_convert_fusion.1 = bf16[2048,1024]{1,0:T(8,128)(2,1)} fusion(bf16[2048,2048]{1,0:T(8,128)(2,1)} %constant_dynamic-update-slice_fusion.14.z_ref, bf16[2048,1024]{1,0:T(8,128)(2,1)} %get-tuple-element.95.refs_0_), kind=kOutput, calls=%fused_computation.6 | convolution fusion | flops 8592031744 | bytes 16777216 | tf_op jit(solution)/shard_map/dot_general | solution.py:29
  333.3 8.8 %all-gather.11.cloned.1.call-done.w_ref.refs_3_ = bf16[2048,1024]{1,0:T(8,128)(2,1)} async-done(((bf16[512,1024]{1,0:T(8,128)(2,1)}), bf16[2048,1024]{1,0:T(8,128)(2,1)}) %all-gather.11.cloned.1.call-update) | async-done | bytes 4194320 | tf_op jit(solution)/shard_map/all_gather | solution.py:677
  342.0 15.8 %feed.3 = (bf16[2048,512]{1,0:T(8,128)(2,1)}, bf16[2048,1024]{1,0:T(8,128)(2,1)}) custom-call(bf16[2048,2048]{1,0:T(8,128)(2,1)} %constant_dynamic-update-slice_fusion.14.z_ref, f32[2048,1024]{1,0:T(8,128)} %back_act.1.g_ref, bf16[2048,1024]{1,0:T(8,128)(2,1)} %all-gather.11.cloned.1.call-done.w_ref.refs_3_), custom_call_target="tpu_custom_call" | custom-call | flops 429496736 | bytes 1153433 | tf_op jit(solution)/shard_map/feed/pallas_call | solution.py:393
  357.8 25.4 %g_two.1 = (bf16[1024,2048]{1,0:T(8,128)(2,1)}, bf16[1024,2048]{1,0:T(8,128)(2,1)}) custom-call(bf16[2048,1024]{1,0:T(8,128)(2,1)} %get-tuple-element.95.refs_0_, bf16[2048,1024]{1,0:T(8,128)(2,1)} %all-gather.9.cloned.1.call-done.w_ref.refs_1_, bf16[2048,1024]{1,0:T(8,128)(2,1)} %get-tuple-element.100.refs_2_, ...), custom_call_target="tpu_custom_call" | custom-call | flops 858993472 | bytes 1258291 | tf_op jit(solution)/shard_map/g_two/pallas_call | solution.py:444
  384.0 12.7 %convolution_convert_fusion = bf16[2048,1024]{1,0:T(8,128)(2,1)} fusion(bf16[2048,2048]{1,0:T(8,128)(2,1)} %constant_dynamic-update-slice_fusion.14.z_ref, bf16[2048,1024]{1,0:T(8,128)(2,1)S(1)} %copy-done.24), kind=kOutput, calls=%fused_computation.5 | convolution fusion | flops 8592031744 | bytes 16777216 | tf_op jit(solution)/shard_map/dot_general | solution.py:29
  396.8 5.4 add_convert_fusion.3
  409.2 15.2 %out.1 = (bf16[1024,2048]{1,0:T(8,128)(2,1)}, bf16[1024,2048]{1,0:T(8,128)(2,1)}) custom-call(bf16[2048,512]{1,0:T(8,128)(2,1)} %get-tuple-element.109.refs_0_, bf16[512,2048]{1,0:T(8,128)(2,1)} %get-tuple-element.186.refs_1_, bf16[2048,512]{1,0:T(8,128)(2,1)} %get-tuple-element.110.refs_2_, bf16[512,2048]{1,0:T(8,128)(2,1)} %get-tuple-element.185.refs_3_), custom_call_target="tpu_custom_call" | custom-call | flops 429496736 | bytes 838860 | tf_op jit(solution)/shard_map/out/pallas_call | solution.py:444
  431.2 9.1 %convolution_convert_fusion.3 = bf16[512,2048]{1,0:T(8,128)(2,1)} fusion(bf16[2048,512]{1,0:T(8,128)(2,1)S(1)} %copy-done.27, bf16[2048,2048]{1,0:T(8,128)(2,1)} %constant_dynamic-update-slice_fusion.21.g_ref), kind=kOutput, calls=%fused_computation.12 | convolution fusion | flops 4296015872 | bytes 12582912 | tf_op jit(solution)/shard_map/dot_general | solution.py:29
  440.3 9.3 %convolution_convert_fusion.4 = bf16[512,2048]{1,0:T(8,128)(2,1)} fusion(bf16[2048,512]{1,0:T(8,128)(2,1)S(1)} %copy-done.26, bf16[2048,2048]{1,0:T(8,128)(2,1)} %constant_dynamic-update-slice_fusion.21.g_ref), kind=kOutput, calls=%fused_computation.13 | convolution fusion | flops 4296015872 | bytes 12582912 | tf_op jit(solution)/shard_map/dot_general | solution.py:29
  457.6 8.8 %back_attn.1 = bf16[8,256,256]{2,1,0:T(8,128)(2,1)} custom-call(s32[1]{0:T(128)} %bitcast.me_ref, bf16[256,2048]{1,0:T(8,128)(2,1)} %get-tuple-element.116.g_ref, bf16[2048,2048]{1,0:T(8,128)(2,1)} %constant_dynamic-update-slice_fusion.7.w_ref), custom_call_target="tpu_custom_call" | custom-call | flops 107374184 | bytes 524288 | tf_op jit(solution)/shard_map/back_attn/pallas_call | solution.py:524
  469.4 9.2 %grad_wo.1 = (bf16[1024,2048]{1,0:T(8,128)(2,1)}, bf16[1024,2048]{1,0:T(8,128)(2,1)}) custom-call(s32[1]{0:T(128)} %bitcast.me_ref, bf16[8,256,256]{2,1,0:T(8,128)(2,1)} %copy-done.11, bf16[256,2048]{1,0:T(8,128)(2,1)} %get-tuple-element.116.g_ref), custom_call_target="tpu_custom_call" | custom-call | flops 107374184 | bytes 524288 | tf_op jit(solution)/shard_map/grad_wo/pallas_call | solution.py:556
  488.4 17.3 %all_to_all.40 = bf16[8,256,256]{2,1,0:T(8,128)(2,1)} all-to-all(bf16[8,256,256]{2,1,0:T(8,128)(2,1)S(1)} %copy-done.25), channel_id=1, replica_groups=mesh['dp'=4,'cp'=8] {'cp'}, dimensions={0} | all-to-all | bytes 2097152 | tf_op jit(solution)/shard_map/all_to_all | solution.py:683
  507.0 24.8 %attend_back.1.refs_0_ = bf16[2048,512]{1,0:T(8,128)(2,1)} custom-call(s32[1]{0:T(128)} %bitcast.me_ref, bf16[2048,256]{1,0:T(8,128)(2,1)} %get-tuple-element.86.q_ref, bf16[2048,256]{1,0:T(8,128)(2,1)} %bitcast.71, bf16[2048,256]{1,0:T(8,128)(2,1)} %get-tuple-element.89.o_ref, f32[8,1,512]{2,1,0:T(1,128)} %get-tuple-element.125.lse_ref, ...), custom_call_target="tpu_custom_call" | custom-call | flops 536870912 | bytes 209715 | tf_op jit(solution)/shard_map/attend_back/pallas_call | solution.py:327
  549.0 11.1 %g_one.1 = (bf16[1024,2048]{1,0:T(8,128)(2,1)}, bf16[1024,2048]{1,0:T(8,128)(2,1)}) custom-call(bf16[2048,512]{1,0:T(8,128)(2,1)} %attend_back.1.refs_0_, bf16[2048,512]{1,0:T(8,128)(2,1)} %bitcast.69), custom_call_target="tpu_custom_call" | custom-call | flops 214748368 | bytes 629145 | tf_op jit(solution)/shard_map/g_one/pallas_call | solution.py:444
  564.5 9.9 %convolution_convert_fusion.2 = bf16[2048,512]{1,0:T(8,128)(2,1)} fusion(bf16[2048,2048]{1,0:T(8,128)(2,1)} %constant_dynamic-update-slice_fusion.z_ref, bf16[2048,512]{1,0:T(8,128)(2,1)S(1)} %copy-done.13), kind=kOutput, calls=%fused_computation.11 | convolution fusion | flops 4296015872 | bytes 12582912 | tf_op jit(solution)/shard_map/dot_general | solution.py:29
  587.7 10.4 %collective-permute-done.43 = bf16[256,2048]{1,0:T(8,128)(2,1)S(1)} collective-permute-done((bf16[256,2048]{1,0:T(8,128)(2,1)}, bf16[256,2048]{1,0:T(8,128)(2,1)S(1)}, u32[]{:S(2)}, u32[]{:S(2)}) %collective-permute-start.43) | collective-permute-done | bytes 1048608 | tf_op jit(solution)/shard_map/ppermute | solution.py:46
  610.4 12.1 %collective-permute-done.40 = bf16[128,2048]{1,0:T(8,128)(2,1)} collective-permute-done((bf16[128,2048]{1,0:T(8,128)(2,1)}, bf16[128,2048]{1,0:T(8,128)(2,1)}, u32[]{:S(2)}, u32[]{:S(2)}) %collective-permute-start.40) | collective-permute-done | bytes 524320 | tf_op jit(solution)/shard_map/ppermute | solution.py:46
  628.1 6.6 all-to-all-start.7
  645.4 10.8 %all-to-all-done.7.got_ref = bf16[8,64,512]{2,1,0:T(8,128)(2,1)} async-done(((bf16[8,64,512]{2,1,0:T(8,128)(2,1)}), bf16[8,64,512]{2,1,0:T(8,128)(2,1)}, u32[]{:S(2)}, u32[]{:S(2)}) %all-to-all-start.7) | async-done | bytes 524320 | tf_op jit(solution)/shard_map/all_to_all | solution.py:683
  671.8 11.5 %collective-permute-done.45 = bf16[64,2048]{1,0:T(8,128)(2,1)S(1)} collective-permute-done((bf16[64,2048]{1,0:T(8,128)(2,1)}, bf16[64,2048]{1,0:T(8,128)(2,1)S(1)}, u32[]{:S(2)}, u32[]{:S(2)}) %collective-permute-start.45) | collective-permute-done | bytes 262176 | tf_op jit(solution)/shard_map/ppermute | solution.py:788
  (314 shorter events, 256.1 us)
Async XLA Ops:
  17.1 81.6 %all-gather.5.cloned.1.call-start = ((), (), s32[]{:S(2)}) async-start(), calls=%async_computation.13 | async-start | bytes 3932160 | tf_op jit(solution)/shard_map/all_gather | solution.py:677
  29.2 248.0 %all-gather.7.cloned.1.call-start = ((), (), s32[]{:S(2)}) async-start(), calls=%async_computation.14 | async-start | bytes 5242880 | tf_op jit(solution)/shard_map/all_gather | solution.py:677
  47.0 33.6 %collective-permute-start.1 = (bf16[256,2048]{1,0:T(8,128)(2,1)}, bf16[256,2048]{1,0:T(8,128)(2,1)S(1)}, u32[]{:S(2)}, u32[]{:S(2)}) collective-permute-start(bf16[256,2048]{1,0:T(8,128)(2,1)} %get-tuple-element.160), channel_id=1, source_target_pairs={{0,4},{1,5},{2,6},{3,7},{4,0},{5,1},{6,2},{7,3},{8,12},{9,13},{10,... | collective-permute-start | bytes 3145736 | tf_op jit(solution)/shard_map/ppermute | solution.py:46
  48.4 42.8 %collective-permute-start = (bf16[256,2048]{1,0:T(8,128)(2,1)}, bf16[256,2048]{1,0:T(8,128)(2,1)S(1)}, u32[]{:S(2)}, u32[]{:S(2)}) collective-permute-start(bf16[256,2048]{1,0:T(8,128)(2,1)} %get-tuple-element.160), channel_id=1, source_target_pairs={{0,2},{1,3},{2,0},{3,1},{4,6},{5,7},{6,4},{7,5},{8,10},{9,11},{10,... | collective-permute-start | bytes 3145736 | tf_op jit(solution)/shard_map/ppermute | solution.py:46
  57.4 33.8 %all-to-all-start.2 = ((bf16[8,64,1024]{2,1,0:T(8,128)(2,1)}), bf16[8,64,1024]{2,1,0:T(8,128)(2,1)S(1)}, u32[]{:S(2)}, u32[]{:S(2)}) async-start(bf16[8,64,1024]{2,1,0:T(8,128)(2,1)} %reshape.130), calls=%async_computation.2 | async-start | bytes 2097152 | tf_op jit(solution)/shard_map/all_to_all | solution.py:683
  64.9 238.1 %all-gather.9.cloned.1.call-start = ((), (), s32[]{:S(2)}) async-start(), calls=%async_computation.15 | async-start | bytes 5242880 | tf_op jit(solution)/shard_map/all_gather | solution.py:677
  94.4 52.3 %collective-permute-start.4 = (bf16[768,2048]{1,0:T(8,128)(2,1)}, bf16[768,2048]{1,0:T(8,128)(2,1)}, u32[]{:S(2)}, u32[]{:S(2)}) collective-permute-start(bf16[768,2048]{1,0:T(8,128)(2,1)} %pad_maximum_fusion.1), channel_id=1, source_target_pairs={{0,1},{1,0},{2,3},{3,2},{4,5},{5,4},{6,7},{7,6},{8,9},{9,8},{10,11... | collective-permute-start | bytes 9437192 | tf_op jit(solution)/shard_map/ppermute | solution.py:46
  102.7 38.2 %collective-permute-start.8 = (bf16[256,2048]{1,0:T(8,128)(2,1)S(1)}, bf16[256,2048]{1,0:T(8,128)(2,1)S(1)}, u32[]{:S(2)}, u32[]{:S(2)}) collective-permute-start(bf16[256,2048]{1,0:T(8,128)(2,1)S(1)} %reshape.134), channel_id=1, source_target_pairs={{0,4},{1,5},{2,6},{3,7},{4,0},{5,1},{6,2},{7,3},{8,12},{9,13},{10,... | collective-permute-start | bytes 3145736 | tf_op jit(solution)/shard_map/ppermute | solution.py:46
  104.0 37.0 %collective-permute-start.7 = (bf16[256,2048]{1,0:T(8,128)(2,1)S(1)}, bf16[256,2048]{1,0:T(8,128)(2,1)S(1)}, u32[]{:S(2)}, u32[]{:S(2)}) collective-permute-start(bf16[256,2048]{1,0:T(8,128)(2,1)S(1)} %reshape.134), channel_id=1, source_target_pairs={{0,2},{1,3},{2,0},{3,1},{4,6},{5,7},{6,4},{7,5},{8,10},{9,11},{10,... | collective-permute-start | bytes 3145736 | tf_op jit(solution)/shard_map/ppermute | solution.py:46
  105.2 32.9 %collective-permute-start.3 = (bf16[128,2048]{1,0:T(8,128)(2,1)S(1)}, bf16[128,2048]{1,0:T(8,128)(2,1)S(1)}, u32[]{:S(2)}, u32[]{:S(2)}) collective-permute-start(bf16[128,2048]{1,0:T(8,128)(2,1)S(1)} %slice.216), channel_id=1, source_target_pairs={{0,4},{1,5},{2,6},{3,7},{4,0},{5,1},{6,2},{7,3},{8,12},{9,13},{10,... | collective-permute-start | bytes 1572872 | tf_op jit(solution)/shard_map/ppermute | solution.py:46
  105.5 33.4 %collective-permute-start.2 = (bf16[128,2048]{1,0:T(8,128)(2,1)S(1)}, bf16[128,2048]{1,0:T(8,128)(2,1)S(1)}, u32[]{:S(2)}, u32[]{:S(2)}) collective-permute-start(bf16[128,2048]{1,0:T(8,128)(2,1)S(1)} %slice.172), channel_id=1, source_target_pairs={{0,2},{1,3},{2,0},{3,1},{4,6},{5,7},{6,4},{7,5},{8,10},{9,11},{10,... | collective-permute-start | bytes 1572872 | tf_op jit(solution)/shard_map/ppermute | solution.py:46
  142.9 66.3 %collective-permute-start.11 = (bf16[768,2048]{1,0:T(8,128)(2,1)}, bf16[768,2048]{1,0:T(8,128)(2,1)}, u32[]{:S(2)}, u32[]{:S(2)}) collective-permute-start(bf16[768,2048]{1,0:T(8,128)(2,1)} %pad_maximum_fusion.2), channel_id=1, source_target_pairs={{0,1},{1,0},{2,3},{3,2},{4,5},{5,4},{6,7},{7,6},{8,9},{9,8},{10,11... | collective-permute-start | bytes 9437192 | tf_op jit(solution)/shard_map/ppermute | solution.py:46
  152.0 50.3 %collective-permute-start.20 = (bf16[256,2048]{1,0:T(8,128)(2,1)S(1)}, bf16[256,2048]{1,0:T(8,128)(2,1)S(1)}, u32[]{:S(2)}, u32[]{:S(2)}) collective-permute-start(bf16[256,2048]{1,0:T(8,128)(2,1)S(1)} %bitcast.65), channel_id=1, source_target_pairs={{0,4},{1,5},{2,6},{3,7},{4,0},{5,1},{6,2},{7,3},{8,12},{9,13},{10,... | collective-permute-start | bytes 3145736 | tf_op jit(solution)/shard_map/ppermute | solution.py:46
  152.3 50.0 %collective-permute-start.19 = (bf16[256,2048]{1,0:T(8,128)(2,1)S(1)}, bf16[256,2048]{1,0:T(8,128)(2,1)}, u32[]{:S(2)}, u32[]{:S(2)}) collective-permute-start(bf16[256,2048]{1,0:T(8,128)(2,1)S(1)} %bitcast.66), channel_id=1, source_target_pairs={{0,2},{1,3},{2,0},{3,1},{4,6},{5,7},{6,4},{7,5},{8,10},{9,11},{10,... | collective-permute-start | bytes 3145736 | tf_op jit(solution)/shard_map/ppermute | solution.py:46
  155.3 45.4 %collective-permute-start.9 = (bf16[128,2048]{1,0:T(8,128)(2,1)}, bf16[128,2048]{1,0:T(8,128)(2,1)}, u32[]{:S(2)}, u32[]{:S(2)}) collective-permute-start(bf16[128,2048]{1,0:T(8,128)(2,1)} %slice.218), channel_id=1, source_target_pairs={{0,2},{1,3},{2,0},{3,1},{4,6},{5,7},{6,4},{7,5},{8,10},{9,11},{10,... | collective-permute-start | bytes 1572872 | tf_op jit(solution)/shard_map/ppermute | solution.py:46
  156.5 44.3 %collective-permute-start.10 = (bf16[128,2048]{1,0:T(8,128)(2,1)}, bf16[128,2048]{1,0:T(8,128)(2,1)}, u32[]{:S(2)}, u32[]{:S(2)}) collective-permute-start(bf16[128,2048]{1,0:T(8,128)(2,1)} %slice.219), channel_id=1, source_target_pairs={{0,4},{1,5},{2,6},{3,7},{4,0},{5,1},{6,2},{7,3},{8,12},{9,13},{10,... | collective-permute-start | bytes 1572872 | tf_op jit(solution)/shard_map/ppermute | solution.py:46
  196.0 146.0 %all-gather.11.cloned.1.call-start = ((), (), s32[]{:S(2)}) async-start(), calls=%async_computation.16 | async-start | bytes 5242880 | tf_op jit(solution)/shard_map/all_gather | solution.py:677
  205.2 66.8 %collective-permute-start.23 = (bf16[768,2048]{1,0:T(8,128)(2,1)}, bf16[768,2048]{1,0:T(8,128)(2,1)}, u32[]{:S(2)}, u32[]{:S(2)}) collective-permute-start(bf16[768,2048]{1,0:T(8,128)(2,1)} %pad_maximum_fusion.4), channel_id=1, source_target_pairs={{0,1},{1,0},{2,3},{3,2},{4,5},{5,4},{6,7},{7,6},{8,9},{9,8},{10,11... | collective-permute-start | bytes 9437192 | tf_op jit(solution)/shard_map/ppermute | solution.py:46
  228.1 257.1 %reduce-scatter.8.cloned.1.call-start = ((), (), s32[]{:S(2)}) async-start(), calls=%async_computation.18 | async-start | bytes 5242880 | tf_op jit(solution)/shard_map/reduce_scatter | solution.py:680
  229.5 32.9 %collective-permute-start.21 = (bf16[128,2048]{1,0:T(8,128)(2,1)S(1)}, bf16[128,2048]{1,0:T(8,128)(2,1)S(1)}, u32[]{:S(2)}, u32[]{:S(2)}) collective-permute-start(bf16[128,2048]{1,0:T(8,128)(2,1)S(1)} %slice.222), channel_id=1, source_target_pairs={{0,2},{1,3},{2,0},{3,1},{4,6},{5,7},{6,4},{7,5},{8,10},{9,11},{10,... | collective-permute-start | bytes 1572872 | tf_op jit(solution)/shard_map/ppermute | solution.py:46
  230.9 31.5 %collective-permute-start.22 = (bf16[128,2048]{1,0:T(8,128)(2,1)S(1)}, bf16[128,2048]{1,0:T(8,128)(2,1)S(1)}, u32[]{:S(2)}, u32[]{:S(2)}) collective-permute-start(bf16[128,2048]{1,0:T(8,128)(2,1)S(1)} %slice.223), channel_id=1, source_target_pairs={{0,4},{1,5},{2,6},{3,7},{4,0},{5,1},{6,2},{7,3},{8,12},{9,13},{10,... | collective-permute-start | bytes 1572872 | tf_op jit(solution)/shard_map/ppermute | solution.py:46
  254.2 43.8 %collective-permute-start.17 = (bf16[768,2048]{1,0:T(8,128)(2,1)}, bf16[768,2048]{1,0:T(8,128)(2,1)}, u32[]{:S(2)}, u32[]{:S(2)}) collective-permute-start(bf16[768,2048]{1,0:T(8,128)(2,1)} %pad_maximum_fusion.3), channel_id=1, source_target_pairs={{0,1},{1,0},{2,3},{3,2},{4,5},{5,4},{6,7},{7,6},{8,9},{9,8},{10,11... | collective-permute-start | bytes 9437192 | tf_op jit(solution)/shard_map/ppermute | solution.py:46
  332.8 231.7 %reduce-scatter.6.cloned.1.call-start = ((), (), s32[]{:S(2)}) async-start(), calls=%async_computation.17 | async-start | bytes 5242880 | tf_op jit(solution)/shard_map/reduce_scatter | solution.py:680
  396.7 209.5 %reduce-scatter.12.cloned.1.call-start = ((), (), s32[]{:S(2)}) async-start(), calls=%async_computation.20 | async-start | bytes 5242880 | tf_op jit(solution)/shard_map/reduce_scatter | solution.py:680
  478.6 55.1 %collective-permute-start.35 = (bf16[1024,2048]{1,0:T(8,128)(2,1)}, bf16[1024,2048]{1,0:T(8,128)(2,1)}, u32[]{:S(2)}, u32[]{:S(2)}) collective-permute-start(bf16[1024,2048]{1,0:T(8,128)(2,1)} %get-tuple-element.118), channel_id=1, source_target_pairs={{0,1},{1,0},{2,3},{3,2},{4,5},{5,4},{6,7},{7,6},{8,9},{9,8},{10,11... | collective-permute-start | bytes 12582920 | tf_op jit(solution)/shard_map/ppermute | solution.py:46
  505.7 26.1 %collective-permute-start.33 = (bf16[256,2048]{1,0:T(8,128)(2,1)}, bf16[256,2048]{1,0:T(8,128)(2,1)S(1)}, u32[]{:S(2)}, u32[]{:S(2)}) collective-permute-start(bf16[256,2048]{1,0:T(8,128)(2,1)} %pad_maximum_fusion.13), channel_id=1, source_target_pairs={{0,2},{1,3},{2,0},{3,1},{4,6},{5,7},{6,4},{7,5},{8,10},{9,11},{10,... | collective-permute-start | bytes 3145736 | tf_op jit(solution)/shard_map/ppermute | solution.py:46
  549.0 79.0 %reduce-scatter.10.cloned.1.call-start = ((), (), s32[]{:S(2)}) async-start(), calls=%async_computation.19 | async-start | bytes 2621440 | tf_op jit(solution)/shard_map/reduce_scatter | solution.py:680
  577.4 33.0 %all-to-all-start.6 = ((bf16[8,64,1024]{2,1,0:T(8,128)(2,1)}), bf16[8,64,1024]{2,1,0:T(8,128)(2,1)S(1)}, u32[]{:S(2)}, u32[]{:S(2)}) async-start(bf16[8,64,1024]{2,1,0:T(8,128)(2,1)} %bitcast.79), calls=%async_computation.8 | async-start | bytes 2097152 | tf_op jit(solution)/shard_map/all_to_all | solution.py:683
  582.0 80.4 %reduce-scatter.14.cloned.1.call-start = ((), (), s32[]{:S(2)}) async-start(), calls=%async_computation.21 | async-start | bytes 1310720 | tf_op jit(solution)/shard_map/reduce_scatter | solution.py:680
  625.5 34.4 %collective-permute-start.41 = (bf16[256,2048]{1,0:T(8,128)(2,1)}, bf16[256,2048]{1,0:T(8,128)(2,1)}, u32[]{:S(2)}, u32[]{:S(2)}) collective-permute-start(bf16[256,2048]{1,0:T(8,128)(2,1)} %pad_maximum_fusion.17), channel_id=1, source_target_pairs={{0,2},{1,3},{2,0},{3,1},{4,6},{5,7},{6,4},{7,5},{8,10},{9,11},{10,... | collective-permute-start | bytes 3145736 | tf_op jit(solution)/shard_map/ppermute | solution.py:46
  626.6 33.3 %collective-permute-start.42 = (bf16[256,2048]{1,0:T(8,128)(2,1)}, bf16[256,2048]{1,0:T(8,128)(2,1)}, u32[]{:S(2)}, u32[]{:S(2)}) collective-permute-start(bf16[256,2048]{1,0:T(8,128)(2,1)} %pad_maximum_fusion.18), channel_id=1, source_target_pairs={{0,4},{1,5},{2,6},{3,7},{4,0},{5,1},{6,2},{7,3},{8,12},{9,13},{10,... | collective-permute-start | bytes 3145736 | tf_op jit(solution)/shard_map/ppermute | solution.py:46
  628.1 28.1 %all-to-all-start.7 = ((bf16[8,64,512]{2,1,0:T(8,128)(2,1)}), bf16[8,64,512]{2,1,0:T(8,128)(2,1)}, u32[]{:S(2)}, u32[]{:S(2)}) async-start(bf16[8,64,512]{2,1,0:T(8,128)(2,1)} %bitcast.81), calls=%async_computation.10 | async-start | bytes 1048576 | tf_op jit(solution)/shard_map/all_to_all | solution.py:683
  (70 other events, 1099.0 us)
Sparse Core Ops, SparseCore 0:
  29.3 69.3 all-gather.4
  100.3 79.4 all-gather.6
  181.4 79.2 all-gather.8
  262.7 79.2 all-gather.10
  344.2 75.3 reduce-scatter.7
  421.8 77.2 reduce-scatter.5
  501.4 77.2 reduce-scatter.11
  581.7 44.1 reduce-scatter.9
  628.2 26.4 reduce-scatter.13

commit v5 on v4

--- a/solution.py
+++ b/solution.py
@@ -46,7 +46,7 @@
     return lax.ppermute(value, "cp", [(i, i ^ offset) for i in range(count)])
 
 
-def gather_rows(part, count, dep=None):
+def gather_rows(part, count, dep=None, late=()):
     half = part.shape[0] // 2
     if count == 8:
         by_x = swap(part, count, 2)
@@ -55,7 +55,8 @@
             by_y = after(by_y, *dep)
         near = jnp.concatenate([part, by_x, by_y], 0)
         near_other = swap(near, count, 1)
-        far = jnp.concatenate([swap(by_y[:half], count, 2), swap(by_x[half:], count, 4)], 0)
+        far = [swap(by_y[:half], count, 2), swap(by_x[half:], count, 4)]
+        far = jnp.concatenate(lax.optimization_barrier((*far, *late))[:2], 0)
         return jnp.concatenate([near, far, near_other, swap(far, count, 1)], 0)
     inner, bit = part, 2
     while bit < count:
@@ -351,32 +352,45 @@
 
 
 def back_act_kernel(g_ref, d_ref, out_ref):
-    out_ref[...] = mm(g_ref[...], d_ref[...], NT)
-
-
-def back_act_call(g_out, w_down, rows):
+    blocks, _, wide = d_ref.shape
+    unit = out_ref.shape[1] // blocks
+    for b in range(blocks):
+        acc = None
+        for c in range(g_ref.shape[1] // wide):
+            part = d_ref[b, c * unit : (c + 1) * unit, :]
+            term = mm(g_ref[:, c * wide : (c + 1) * wide], part, NT)
+            acc = term if acc is None else acc + term
+        out_ref[:, b * unit : (b + 1) * unit] = acc
+
+
+def back_act_call(g_out, packed, rows):
     total, width = g_out.shape
-    cols = w_down.shape[0]
+    blocks, depth, wide = packed.shape
+    depth = depth // 2
+    cols = blocks * depth * wide // width
     return pl.pallas_call(
         back_act_kernel,
         grid=(total // rows,),
         in_specs=[
             pl.BlockSpec((rows, width), lambda i: (i, 0)),
-            pl.BlockSpec((cols, width), lambda i: (0, 0)),
+            pl.BlockSpec((blocks, depth, wide), lambda i: (0, 1, 0)),
         ],
         out_specs=pl.BlockSpec((rows, cols), lambda i: (i, 0)),
         out_shape=jax.ShapeDtypeStruct((total, cols), F32),
         compiler_params=params(("arbitrary",)),
         cost_estimate=cost(2 * total * width * cols, 2 * total * width + 2 * cols * width + 4 * total * cols),
         name="back_act",
-    )(g_out, w_down)
+    )(g_out, packed)
 
 
 def feed_kernel(z_ref, g_ref, w_ref, act_ref, grads_ref):
     cut = g_ref.shape[1]
-    z = z_ref[...]
-    gate = mm(z, w_ref[:, :cut], NN)
-    up = mm(z, w_ref[:, cut:], NN)
+    blocks, depth, _ = w_ref.shape
+    both = None
+    for b in range(blocks):
+        term = mm(z_ref[:, b * depth : (b + 1) * depth], w_ref[b], NN)
+        both = term if both is None else both + term
+    gate, up = both[:, :cut], both[:, cut:]
     back = g_ref[...]
     sig = jax.nn.sigmoid(gate)
     silu = gate * sig
@@ -387,16 +401,16 @@
 
 def feed_call(z_two, g_act, w_gu, part, rows):
     total, width = z_two.shape
-    cut = w_gu.shape[1] // 2
+    cut = w_gu.shape[2] // 2
+    blocks = w_gu.shape[0]
     row = lambda i: (i, 0)
-    whole = lambda i: (0, 0)
     return pl.pallas_call(
         feed_kernel,
         grid=(total // rows,),
         in_specs=[
             pl.BlockSpec((rows, width), row),
             pl.BlockSpec((rows, cut), lambda i: (i, part)),
-            pl.BlockSpec((width, 2 * cut), whole),
+            pl.BlockSpec((blocks, width // blocks, 2 * cut), lambda i: (0, 0, 0)),
         ],
         out_specs=[pl.BlockSpec((rows, cut), row), pl.BlockSpec((rows, 2 * cut), row)],
         out_shape=[
@@ -574,6 +588,59 @@
         cost_estimate=cost(2 * rows * feat * count * width, 2 * feat * count * width + 4 * rows * width),
         name="grad_wo",
     )(me, attn, g)
+
+
+def packed_kernel(*refs, down):
+    *ins, low_ref, high_ref = refs
+    lefts, weights = ins[:2], ins[2:]
+    blocks, depth, wide = weights[0].shape
+    pieces = []
+    if down:
+        per = blocks // 2
+        unit = lefts[0].shape[1] // per
+        for c in range(depth // unit):
+            acc = None
+            for b in range(blocks):
+                left = lefts[b // per][:, (b % per) * unit : (b % per + 1) * unit]
+                term = mm(left, weights[0][b, c * unit : (c + 1) * unit, :], NN)
+                acc = term if acc is None else acc + term
+            pieces.append(acc.astype(BF))
+    else:
+        for b in range(blocks):
+            acc = mm(lefts[0][...], weights[0][b], NT) + mm(lefts[1][...], weights[1][b], NT)
+            pieces.append(acc.astype(BF))
+    out = jnp.concatenate(pieces, 1)
+    half = pl.num_programs(0) // 2
+
+    @pl.when(pl.program_id(0) < half)
+    def _():
+        high_ref[...] = out
+
+    @pl.when(pl.program_id(0) >= half)
+    def _():
+        low_ref[...] = out
+
+
+def packed_call(lefts, weights, down, width, rows, name):
+    total, cols = lefts[0].shape
+    blocks, _, wide = weights[0].shape
+    depth = width // blocks
+    half, row, low, high = split_rows(total // rows)
+    left = pl.BlockSpec((rows, cols), lambda i: (row(i), 0))
+    weight = pl.BlockSpec((blocks, depth, wide), lambda i: (0, 1 if down else 0, 0))
+    return pl.pallas_call(
+        functools.partial(packed_kernel, down=down),
+        grid=(total // rows,),
+        in_specs=[left, left] + [weight] * len(weights),
+        out_specs=[
+            pl.BlockSpec((rows, width), lambda i: (low(i), 0)),
+            pl.BlockSpec((rows, width), lambda i: (high(i), 0)),
+        ],
+        out_shape=[jax.ShapeDtypeStruct((total // 2, width), BF)] * 2,
+        compiler_params=params(("arbitrary",)),
+        cost_estimate=cost(4 * total * cols * width, 2 * total * (2 * cols + width) + 4 * cols * width),
+        name=name,
+    )(*lefts, *weights)
 
 
 def finish_feed_kernel(*refs, halves, per_half, unit, count):
@@ -699,19 +766,22 @@
         joint = gather_z(qkv_rows).reshape(n_dp, -1, qkv_cols)
         wo_rows = gather_z(wo_own)
 
-    w_down_full = gather_z(w_down)
     scaled_g = (w_gate.astype(F32) * gain_two).astype(BF).reshape(own, n_dp, n_cp, unit)
     scaled_u = (w_up.astype(F32) * gain_two).astype(BF).reshape(own, n_dp, n_cp, unit)
     cut = per_half * unit
-    w_gu, w_dn, last, given = [], [], qkv_rows, []
+    w_gu, last, given = [], qkv_rows, []
     for h in range(halves):
         at = slice(h * per_half, (h + 1) * per_half)
         both = jnp.concatenate([scaled_g[:, at], scaled_u[:, at]], 1)
         both = both.transpose(2, 0, 1, 3).reshape(n_cp, own, 2 * cut)
         last = give(after(both, last))
         given.append(last)
-        w_gu.append(gather_z(last.reshape(n_cp * own, 2 * cut)))
-        w_dn.append(w_down_full[h * cut : (h + 1) * cut])
+        block = last.reshape(depth, 2 * cut)
+        if h == 0:
+            columns = [w_down[:, c : c + 2 * cut] for c in range(0, width, 2 * cut)]
+            block = jnp.concatenate([block, *columns], 0)
+        w_gu.append(gather_z(block).reshape(n_dp, -1, 2 * cut))
+    packed = w_gu[0]
 
     shard_at = jnp.array([offset_of(p, n_cp) for p in range(n_cp)], jnp.int32) ^ me
     positions = (shard_at[:, None] * rows + jnp.arange(rows, dtype=jnp.int32)[None, :]).reshape(-1)
@@ -737,8 +807,8 @@
     feat = heads * HD
     attn = give(mixed.reshape(n_cp, rows, feat))
     hid, z_two_b, rms_two = hidden_call(me_arr, attn, wo_rel, xb, n_cp)
-    g_act = back_act_call(after(g_out_all, z_two_b), w_down_full, rows)
-    z_two_all = gather_rows(z_two_b, n_cp)
+    g_act = back_act_call(after(g_out_all, z_two_b), packed, rows)
+    z_two_all = gather_rows(z_two_b, n_cp, late=(g_act,))
 
     acts, gus, red_gu = [], [], []
     for h in range(halves):
@@ -749,11 +819,11 @@
         if h == 0:
             part_gu = mm(z_two_all, gu, TN).astype(BF)
             red_gu.append(scatter_z(part_gu))
-    part = sum_call([(gus[h], w_gu[h]) for h in range(halves)], NT, rows, "g_two")
+    part = packed_call(gus, w_gu, False, width, rows, "g_two")
     part_gu = mm(z_two_all, after(gus[1], *part), TN).astype(BF)
     red_gu.append(scatter_z(part_gu))
     acc = scatter_first(*part, n_cp, part_gu)
-    out_part = sum_call([(after(acts[h], acc), w_dn[h]) for h in range(halves)], NN, rows, "out")
+    out_part = packed_call([after(a, acc) for a in acts], [packed], True, width, rows, "out")
     state = scatter_mid(acc, n_cp, *out_part)
     downs = [mm(after(act, *state), g_out_all, TN).astype(BF) for act in acts]
     grad_down = scatter_z(after(jnp.concatenate(downs, 0), red_gu[0]))
@@ -791,7 +861,7 @@
 
     grad_g, grad_u, gain_two_sum = finish_feed_call(back_gu, w_gate, w_up, gain_two, per_half, unit)
     grad_q, grad_k, grad_v, gain_one_sum = finish_qkv_call(
-        got, w_query, w_key, w_value, gain_one, heads, reps
+        after(got, wo_sum), w_query, w_key, w_value, gain_one, heads, reps
     )
 
     return (

time: 699 us -> 693 us (level)
  waiting for transfers between devices: 151 us -> 141 us
    pallas_call x3 -> x1, Pallas kernels: 51.7 us -> 11 us  [sum_call(): pl.pallas_call(functools.partial(sum_kernel, dims=dims), grid=(total // r...]
    pallas_call x0 -> x2, Pallas kernels: none -> 40.6 us  [packed_call(): pl.pallas_call(functools.partial(packed_kernel, down=down), grid=(total /...]
    all_to_all x7, waiting for transfers between devices: 30.2 us -> 41.4 us  [give(): return lax.all_to_all(value, 'cp', 0, 0)]
    all_gather x4 -> x3, waiting for transfers between devices: 9.55 us -> 0.02 us  [gather_z(): return lax.all_gather(value, 'dp', axis=0, tiled=True)]
    ppermute x44, waiting for transfers between devices: 91.2 us -> 81.9 us  [swap(): return lax.ppermute(value, 'cp', [(i, i ^ offset) for i in range(count)])]
    unnamed x107 -> x109, local copies, waits for them, and re-layouts: 46.7 us -> 50.9 us
  transfers between devices with their start and end apart: 62 -> 61, of which waited for: 18 -> 17; matrix products, arithmetic and copies ran while one was open for 30% -> 31% of each run, Pallas kernels for 28% -> 28%
where the time goes in v5:
time: 693 us; the launch traced here: 683 us
  Pallas kernels  191 us (28%)
  waiting for transfers between devices  141 us (20%)
  starting transfers between devices  91.8 us (13%)
  other arithmetic  90.8 us (13%)
  local copies, waits for them, and re-layouts  80.1 us (12%)
  matrix products  55 us (8%)
  blocking collectives  18.2 us (3%)
  between operations  15 us (2%)
    ppermute x44, waiting for transfers between devices, swap(): return lax.ppermute(value, 'cp', [(i, i ^ offset) for i in range(count)])  81.9 us
    dot_general x5, matrix products, mm(): return lax.dot_general(left, right, dims, preferred_element_type=F32)  55 us
    unnamed x109, local copies, waits for them, and re-layouts  50.9 us
    all_to_all x7, starting transfers between devices, give(): return lax.all_to_all(value, 'cp', 0, 0)  42 us
    all_to_all x7, waiting for transfers between devices, give(): return lax.all_to_all(value, 'cp', 0, 0)  41.4 us
    pallas_call x2, Pallas kernels, packed_call(): pl.pallas_call(functools.partial(packed_kernel, down=down), grid=(total /...  40.6 us
    ppermute x44, starting transfers between devices, swap(): return lax.ppermute(value, 'cp', [(i, i ^ offset) for i in range(count)])  40.3 us
    pallas_call x2, Pallas kernels, feed_call(): pl.pallas_call(feed_kernel, grid=(total // rows,), in_specs=[pl.BlockSpec...  31.4 us
  transfers between devices with their start and end apart: 61, of which 17 were waited for; matrix products, arithmetic and copies ran while one was open for 31% of the time, Pallas kernels for 28%

profile of v5, /device:TPU:1, one launch (start us, length us, event | category | flops | bytes accessed | tf_op | source)
XLA Modules:
  0.0 683.1 jit_solution(9252062856077139120)
XLA Ops:
  20.2 7.8 %collective-permute-done.6 = bf16[64,2048]{1,0:T(8,128)(2,1)S(1)} collective-permute-done((bf16[64,2048]{1,0:T(8,128)(2,1)S(1)}, bf16[64,2048]{1,0:T(8,128)(2,1)S(1)}, u32[]{:S(2)}, u32[]{:S(2)}) %collective-permute-start.6) | collective-permute-done | bytes 262176 | tf_op jit(solution)/shard_map/ppermute | solution.py:759
  35.9 10.4 %all-to-all-start.1 = ((bf16[8,64,1024]{2,1,0:T(8,128)(2,1)}), bf16[8,64,1024]{2,1,0:T(8,128)(2,1)S(1)}, u32[]{:S(2)}, u32[]{:S(2)}) async-start(bf16[8,64,1024]{2,1,0:T(8,128)(2,1)} %reshape.133), calls=%async_computation.1 | async-start | bytes 2097152 | tf_op jit(solution)/shard_map/all_to_all | solution.py:750
  47.6 10.6 %all-to-all-done.1 = bf16[8,64,1024]{2,1,0:T(8,128)(2,1)S(1)} async-done(((bf16[8,64,1024]{2,1,0:T(8,128)(2,1)}), bf16[8,64,1024]{2,1,0:T(8,128)(2,1)S(1)}, u32[]{:S(2)}, u32[]{:S(2)}) %all-to-all-start.1) | async-done | bytes 1048608 | tf_op jit(solution)/shard_map/all_to_all | solution.py:750
  83.1 15.0 %all-to-all-done.2 = bf16[8,64,1024]{2,1,0:T(8,128)(2,1)S(1)} async-done(((bf16[8,64,1024]{2,1,0:T(8,128)(2,1)}), bf16[8,64,1024]{2,1,0:T(8,128)(2,1)S(1)}, u32[]{:S(2)}, u32[]{:S(2)}) %all-to-all-start.2) | async-done | bytes 1048608 | tf_op jit(solution)/shard_map/all_to_all | solution.py:750
  112.3 33.0 %collective-permute-done.3 = bf16[128,2048]{1,0:T(8,128)(2,1)S(1)} collective-permute-done((bf16[128,2048]{1,0:T(8,128)(2,1)S(1)}, bf16[128,2048]{1,0:T(8,128)(2,1)S(1)}, u32[]{:S(2)}, u32[]{:S(2)}) %collective-permute-start.3) | collective-permute-done | bytes 524320 | tf_op jit(solution)/shard_map/ppermute | solution.py:46
  163.1 11.9 %qkv.1 = (bf16[2048,256]{1,0:T(8,128)(2,1)}, bf16[2048,128]{1,0:T(8,128)(2,1)}, bf16[2048,128]{1,0:T(8,128)(2,1)}, bf16[128,2048]{1,0:T(8,128)(2,1)}, bf16[128,2048]{1,0:T(8,128)(2,1)}) custom-call(bf16[2048,2048]{1,0:T(8,128)(2,1)} %constant_dynamic-update-slice_fusion.z_ref, bf16[4,768,512]{2,1,0:T(8,128)(2,1)} %bitcast.71, ...), custom_call_target="tpu_custom_call" | custom-call | flops 214748368 | bytes 524288 | tf_op jit(solution)/shard_map/qkv/pallas_call | solution.py:152
  175.0 21.5 %attend.1 = (bf16[2048,256]{1,0:T(8,128)(2,1)}, f32[8,1,512]{2,1,0:T(1,128)}) custom-call(s32[1]{0:T(128)} %bitcast.me_ref, bf16[2048,256]{1,0:T(8,128)(2,1)} %get-tuple-element.97.q_ref, bf16[2048,128]{1,0:T(8,128)(2,1)} %get-tuple-element.98.k_ref, bf16[128,2048]{1,0:T(8,128)(2,1)} %get-tuple-element.99.vt_ref), custom_call_target="tpu_custom_call" | custom-call | flops 214748368 | bytes 104857 | tf_op jit(solution)/shard_map/attend/pallas_call | solution.py:232
  220.9 10.1 %hidden.1 = (f32[256,2048]{1,0:T(8,128)}, bf16[256,2048]{1,0:T(8,128)(2,1)}, f32[256,1]{1,0:T(8,128)}) custom-call(s32[1]{0:T(128)} %bitcast.me_ref, bf16[8,256,256]{2,1,0:T(8,128)(2,1)} %copy-done.10, bf16[2048,2048]{1,0:T(8,128)(2,1)} %constant_dynamic-update-slice_fusion.7.w_ref, bf16[256,2048]{1,0:T(8,128)(2,1)} %bitcast.67), custom_call_target="tpu_custom_call" | custom-call | flops 107374184 | bytes 681574 | tf_op jit(solution)/shard_map/hidden/pallas_call | solution.py:501
  236.8 19.1 %collective-permute-done.14 = bf16[256,2048]{1,0:T(8,128)(2,1)S(1)} collective-permute-done((bf16[256,2048]{1,0:T(8,128)(2,1)}, bf16[256,2048]{1,0:T(8,128)(2,1)S(1)}, u32[]{:S(2)}, u32[]{:S(2)}) %collective-permute-start.14) | collective-permute-done | bytes 1048608 | tf_op jit(solution)/shard_map/ppermute | solution.py:46
  282.6 15.0 %back_act.1.g_ref = f32[2048,1024]{1,0:T(8,128)} custom-call(bf16[2048,2048]{1,0:T(8,128)(2,1)} %constant_dynamic-update-slice_fusion.14.g_ref, bf16[4,1024,1024]{2,1,0:T(8,128)(2,1)} %bitcast.63), custom_call_target="tpu_custom_call" | custom-call | flops 429496736 | bytes 1048576 | tf_op jit(solution)/shard_map/back_act/pallas_call | solution.py:371
  308.5 15.4 %feed.2 = (bf16[2048,512]{1,0:T(8,128)(2,1)}, bf16[2048,1024]{1,0:T(8,128)(2,1)}) custom-call(bf16[2048,2048]{1,0:T(8,128)(2,1)} %constant_dynamic-update-slice_fusion.21.z_ref, f32[2048,1024]{1,0:T(8,128)} %back_act.1.g_ref, bf16[4,1024,1024]{2,1,0:T(8,128)(2,1)} %bitcast.64), custom_call_target="tpu_custom_call" | custom-call | flops 429496736 | bytes 1153433 | tf_op jit(solution)/shard_map/feed/pallas_call | solution.py:407
  323.9 14.0 %convolution_convert_fusion.1 = bf16[2048,1024]{1,0:T(8,128)(2,1)} fusion(bf16[2048,2048]{1,0:T(8,128)(2,1)} %constant_dynamic-update-slice_fusion.21.z_ref, bf16[2048,1024]{1,0:T(8,128)(2,1)} %get-tuple-element.112.refs_0_), kind=kOutput, calls=%fused_computation.6 | convolution fusion | flops 8592031744 | bytes 16777216 | tf_op jit(solution)/shard_map/dot_general | solution.py:29
  338.1 16.0 %feed.3 = (bf16[2048,512]{1,0:T(8,128)(2,1)}, bf16[2048,1024]{1,0:T(8,128)(2,1)}) custom-call(bf16[2048,2048]{1,0:T(8,128)(2,1)} %constant_dynamic-update-slice_fusion.21.z_ref, f32[2048,1024]{1,0:T(8,128)} %back_act.1.g_ref, bf16[4,512,1024]{2,1,0:T(8,128)(2,1)} %bitcast.68), custom_call_target="tpu_custom_call" | custom-call | flops 429496736 | bytes 1153433 | tf_op jit(solution)/shard_map/feed/pallas_call | solution.py:407
  354.1 25.5 %g_two.1 = (bf16[1024,2048]{1,0:T(8,128)(2,1)}, bf16[1024,2048]{1,0:T(8,128)(2,1)}) custom-call(bf16[2048,1024]{1,0:T(8,128)(2,1)} %get-tuple-element.112.refs_0_, bf16[2048,1024]{1,0:T(8,128)(2,1)} %get-tuple-element.117.refs_1_, bf16[4,1024,1024]{2,1,0:T(8,128)(2,1)} %bitcast.65, bf16[4,512,1024]{2,1,0:T(8,128)(2,1)} %bitcast.69), custom_call_target="tpu_custom_call" | custom-call | flops 858993472 | bytes 1258291 | tf_op jit(solution)/shard_map/g_two/pallas_call | solution.py:631
  379.6 12.7 %convolution_convert_fusion = bf16[2048,1024]{1,0:T(8,128)(2,1)} fusion(bf16[2048,2048]{1,0:T(8,128)(2,1)} %constant_dynamic-update-slice_fusion.21.z_ref, bf16[2048,1024]{1,0:T(8,128)(2,1)S(1)} %copy-done.17), kind=kOutput, calls=%fused_computation.5 | convolution fusion | flops 8592031744 | bytes 16777216 | tf_op jit(solution)/shard_map/dot_general | solution.py:29
  392.4 5.4 add_convert_fusion.3
  402.6 15.1 %out.1 = (bf16[1024,2048]{1,0:T(8,128)(2,1)}, bf16[1024,2048]{1,0:T(8,128)(2,1)}) custom-call(bf16[2048,512]{1,0:T(8,128)(2,1)} %get-tuple-element.126.refs_0_, bf16[2048,512]{1,0:T(8,128)(2,1)} %get-tuple-element.127.refs_1_, bf16[4,1024,1024]{2,1,0:T(8,128)(2,1)} %bitcast.66), custom_call_target="tpu_custom_call" | custom-call | flops 429496736 | bytes 838860 | tf_op jit(solution)/shard_map/out/pallas_call | solution.py:631
  424.6 9.1 %convolution_convert_fusion.3 = bf16[512,2048]{1,0:T(8,128)(2,1)} fusion(bf16[2048,512]{1,0:T(8,128)(2,1)S(1)} %copy-done.26, bf16[2048,2048]{1,0:T(8,128)(2,1)} %constant_dynamic-update-slice_fusion.14.g_ref), kind=kOutput, calls=%fused_computation.12 | convolution fusion | flops 4296015872 | bytes 12582912 | tf_op jit(solution)/shard_map/dot_general | solution.py:29
  433.7 9.3 %convolution_convert_fusion.4 = bf16[512,2048]{1,0:T(8,128)(2,1)} fusion(bf16[2048,512]{1,0:T(8,128)(2,1)S(1)} %copy-done.25, bf16[2048,2048]{1,0:T(8,128)(2,1)} %constant_dynamic-update-slice_fusion.14.g_ref), kind=kOutput, calls=%fused_computation.13 | convolution fusion | flops 4296015872 | bytes 12582912 | tf_op jit(solution)/shard_map/dot_general | solution.py:29
  452.4 8.8 %back_attn.1 = bf16[8,256,256]{2,1,0:T(8,128)(2,1)} custom-call(s32[1]{0:T(128)} %bitcast.me_ref, bf16[256,2048]{1,0:T(8,128)(2,1)} %get-tuple-element.133.g_ref, bf16[2048,2048]{1,0:T(8,128)(2,1)} %constant_dynamic-update-slice_fusion.7.w_ref), custom_call_target="tpu_custom_call" | custom-call | flops 107374184 | bytes 524288 | tf_op jit(solution)/shard_map/back_attn/pallas_call | solution.py:538
  463.1 9.1 %grad_wo.1 = (bf16[1024,2048]{1,0:T(8,128)(2,1)}, bf16[1024,2048]{1,0:T(8,128)(2,1)}) custom-call(s32[1]{0:T(128)} %bitcast.me_ref, bf16[8,256,256]{2,1,0:T(8,128)(2,1)} %copy-done.10, bf16[256,2048]{1,0:T(8,128)(2,1)} %get-tuple-element.133.g_ref), custom_call_target="tpu_custom_call" | custom-call | flops 107374184 | bytes 524288 | tf_op jit(solution)/shard_map/grad_wo/pallas_call | solution.py:570
  481.6 18.2 %all_to_all.40 = bf16[8,256,256]{2,1,0:T(8,128)(2,1)} all-to-all(bf16[8,256,256]{2,1,0:T(8,128)(2,1)S(1)} %copy-done.24), channel_id=1, replica_groups=mesh['dp'=4,'cp'=8] {'cp'}, dimensions={0} | all-to-all | bytes 2097152 | tf_op jit(solution)/shard_map/all_to_all | solution.py:750
  501.0 24.6 %attend_back.1.refs_0_ = bf16[2048,512]{1,0:T(8,128)(2,1)} custom-call(s32[1]{0:T(128)} %bitcast.me_ref, bf16[2048,256]{1,0:T(8,128)(2,1)} %get-tuple-element.97.q_ref, bf16[2048,256]{1,0:T(8,128)(2,1)} %bitcast.79, bf16[2048,256]{1,0:T(8,128)(2,1)} %get-tuple-element.100.o_ref, f32[8,1,512]{2,1,0:T(1,128)} %get-tuple-element.142.lse_ref, ...), custom_call_target="tpu_custom_call" | custom-call | flops 536870912 | bytes 209715 | tf_op jit(solution)/shard_map/attend_back/pallas_call | solution.py:328
  542.8 11.0 %g_one.1 = (bf16[1024,2048]{1,0:T(8,128)(2,1)}, bf16[1024,2048]{1,0:T(8,128)(2,1)}) custom-call(bf16[2048,512]{1,0:T(8,128)(2,1)} %attend_back.1.refs_0_, bf16[2048,512]{1,0:T(8,128)(2,1)} %bitcast.77), custom_call_target="tpu_custom_call" | custom-call | flops 214748368 | bytes 629145 | tf_op jit(solution)/shard_map/g_one/pallas_call | solution.py:458
  558.2 9.9 %convolution_convert_fusion.2 = bf16[2048,512]{1,0:T(8,128)(2,1)} fusion(bf16[2048,2048]{1,0:T(8,128)(2,1)} %constant_dynamic-update-slice_fusion.z_ref, bf16[2048,512]{1,0:T(8,128)(2,1)S(1)} %copy-done.12), kind=kOutput, calls=%fused_computation.11 | convolution fusion | flops 4296015872 | bytes 12582912 | tf_op jit(solution)/shard_map/dot_general | solution.py:29
  576.2 5.4 add_convert_fusion
  581.6 9.5 %collective-permute-done.43 = bf16[256,2048]{1,0:T(8,128)(2,1)S(1)} collective-permute-done((bf16[256,2048]{1,0:T(8,128)(2,1)}, bf16[256,2048]{1,0:T(8,128)(2,1)S(1)}, u32[]{:S(2)}, u32[]{:S(2)}) %collective-permute-start.43) | collective-permute-done | bytes 1048608 | tf_op jit(solution)/shard_map/ppermute | solution.py:46
  604.9 10.7 %collective-permute-done.40 = bf16[128,2048]{1,0:T(8,128)(2,1)} collective-permute-done((bf16[128,2048]{1,0:T(8,128)(2,1)}, bf16[128,2048]{1,0:T(8,128)(2,1)}, u32[]{:S(2)}, u32[]{:S(2)}) %collective-permute-start.40) | collective-permute-done | bytes 524320 | tf_op jit(solution)/shard_map/ppermute | solution.py:46
  621.8 6.8 all-to-all-start.7
  639.2 10.5 %all-to-all-done.7.got_ref = bf16[8,64,512]{2,1,0:T(8,128)(2,1)} async-done(((bf16[8,64,512]{2,1,0:T(8,128)(2,1)}), bf16[8,64,512]{2,1,0:T(8,128)(2,1)}, u32[]{:S(2)}, u32[]{:S(2)}) %all-to-all-start.7) | async-done | bytes 524320 | tf_op jit(solution)/shard_map/all_to_all | solution.py:750
  652.3 5.4 collective-permute-start.45
  665.5 9.7 %collective-permute-done.45 = bf16[64,2048]{1,0:T(8,128)(2,1)S(1)} collective-permute-done((bf16[64,2048]{1,0:T(8,128)(2,1)}, bf16[64,2048]{1,0:T(8,128)(2,1)S(1)}, u32[]{:S(2)}, u32[]{:S(2)}) %collective-permute-start.45) | collective-permute-done | bytes 262176 | tf_op jit(solution)/shard_map/ppermute | solution.py:858
  (313 shorter events, 251.6 us)
Async XLA Ops:
  17.0 88.0 %all-gather.4.cloned.1.call-start = ((), (), s32[]{:S(2)}) async-start(), calls=%async_computation.13 | async-start | bytes 3932160 | tf_op jit(solution)/shard_map/all_gather | solution.py:744
  46.3 236.3 %all-gather.6.cloned.1.call-start = ((), (), s32[]{:S(2)}) async-start(), calls=%async_computation.14 | async-start | bytes 10485760 | tf_op jit(solution)/shard_map/all_gather | solution.py:744
  62.5 35.7 %collective-permute-start = (bf16[256,2048]{1,0:T(8,128)(2,1)}, bf16[256,2048]{1,0:T(8,128)(2,1)S(1)}, u32[]{:S(2)}, u32[]{:S(2)}) collective-permute-start(bf16[256,2048]{1,0:T(8,128)(2,1)} %get-tuple-element.178), channel_id=1, source_target_pairs={{0,2},{1,3},{2,0},{3,1},{4,6},{5,7},{6,4},{7,5},{8,10},{9,11},{10,... | collective-permute-start | bytes 3145736 | tf_op jit(solution)/shard_map/ppermute | solution.py:46
  70.7 27.5 %all-to-all-start.2 = ((bf16[8,64,1024]{2,1,0:T(8,128)(2,1)}), bf16[8,64,1024]{2,1,0:T(8,128)(2,1)S(1)}, u32[]{:S(2)}, u32[]{:S(2)}) async-start(bf16[8,64,1024]{2,1,0:T(8,128)(2,1)} %reshape.136), calls=%async_computation.2 | async-start | bytes 2097152 | tf_op jit(solution)/shard_map/all_to_all | solution.py:750
  101.5 50.7 %collective-permute-start.4 = (bf16[768,2048]{1,0:T(8,128)(2,1)}, bf16[768,2048]{1,0:T(8,128)(2,1)}, u32[]{:S(2)}, u32[]{:S(2)}) collective-permute-start(bf16[768,2048]{1,0:T(8,128)(2,1)} %pad_maximum_fusion.1), channel_id=1, source_target_pairs={{0,1},{1,0},{2,3},{3,2},{4,5},{5,4},{6,7},{7,6},{8,9},{9,8},{10,11... | collective-permute-start | bytes 9437192 | tf_op jit(solution)/shard_map/ppermute | solution.py:46
  109.1 37.3 %collective-permute-start.8 = (bf16[256,2048]{1,0:T(8,128)(2,1)S(1)}, bf16[256,2048]{1,0:T(8,128)(2,1)S(1)}, u32[]{:S(2)}, u32[]{:S(2)}) collective-permute-start(bf16[256,2048]{1,0:T(8,128)(2,1)S(1)} %reshape.140), channel_id=1, source_target_pairs={{0,4},{1,5},{2,6},{3,7},{4,0},{5,1},{6,2},{7,3},{8,12},{9,13},{10,... | collective-permute-start | bytes 3145736 | tf_op jit(solution)/shard_map/ppermute | solution.py:46
  109.3 37.1 %collective-permute-start.7 = (bf16[256,2048]{1,0:T(8,128)(2,1)S(1)}, bf16[256,2048]{1,0:T(8,128)(2,1)S(1)}, u32[]{:S(2)}, u32[]{:S(2)}) collective-permute-start(bf16[256,2048]{1,0:T(8,128)(2,1)S(1)} %reshape.140), channel_id=1, source_target_pairs={{0,2},{1,3},{2,0},{3,1},{4,6},{5,7},{6,4},{7,5},{8,10},{9,11},{10,... | collective-permute-start | bytes 3145736 | tf_op jit(solution)/shard_map/ppermute | solution.py:46
  110.9 34.4 %collective-permute-start.3 = (bf16[128,2048]{1,0:T(8,128)(2,1)S(1)}, bf16[128,2048]{1,0:T(8,128)(2,1)S(1)}, u32[]{:S(2)}, u32[]{:S(2)}) collective-permute-start(bf16[128,2048]{1,0:T(8,128)(2,1)S(1)} %slice.216), channel_id=1, source_target_pairs={{0,4},{1,5},{2,6},{3,7},{4,0},{5,1},{6,2},{7,3},{8,12},{9,13},{10,... | collective-permute-start | bytes 1572872 | tf_op jit(solution)/shard_map/ppermute | solution.py:46
  111.1 34.3 %collective-permute-start.2 = (bf16[128,2048]{1,0:T(8,128)(2,1)S(1)}, bf16[128,2048]{1,0:T(8,128)(2,1)S(1)}, u32[]{:S(2)}, u32[]{:S(2)}) collective-permute-start(bf16[128,2048]{1,0:T(8,128)(2,1)S(1)} %slice.172), channel_id=1, source_target_pairs={{0,2},{1,3},{2,0},{3,1},{4,6},{5,7},{6,4},{7,5},{8,10},{9,11},{10,... | collective-permute-start | bytes 1572872 | tf_op jit(solution)/shard_map/ppermute | solution.py:46
  148.4 66.4 %collective-permute-start.11 = (bf16[768,2048]{1,0:T(8,128)(2,1)}, bf16[768,2048]{1,0:T(8,128)(2,1)}, u32[]{:S(2)}, u32[]{:S(2)}) collective-permute-start(bf16[768,2048]{1,0:T(8,128)(2,1)} %pad_maximum_fusion.2), channel_id=1, source_target_pairs={{0,1},{1,0},{2,3},{3,2},{4,5},{5,4},{6,7},{7,6},{8,9},{9,8},{10,11... | collective-permute-start | bytes 9437192 | tf_op jit(solution)/shard_map/ppermute | solution.py:46
  157.5 50.3 %collective-permute-start.18 = (bf16[256,2048]{1,0:T(8,128)(2,1)S(1)}, bf16[256,2048]{1,0:T(8,128)(2,1)S(1)}, u32[]{:S(2)}, u32[]{:S(2)}) collective-permute-start(bf16[256,2048]{1,0:T(8,128)(2,1)S(1)} %bitcast.73), channel_id=1, source_target_pairs={{0,4},{1,5},{2,6},{3,7},{4,0},{5,1},{6,2},{7,3},{8,12},{9,13},{10,... | collective-permute-start | bytes 3145736 | tf_op jit(solution)/shard_map/ppermute | solution.py:46
  158.7 49.1 %collective-permute-start.17 = (bf16[256,2048]{1,0:T(8,128)(2,1)S(1)}, bf16[256,2048]{1,0:T(8,128)(2,1)}, u32[]{:S(2)}, u32[]{:S(2)}) collective-permute-start(bf16[256,2048]{1,0:T(8,128)(2,1)S(1)} %bitcast.74), channel_id=1, source_target_pairs={{0,2},{1,3},{2,0},{3,1},{4,6},{5,7},{6,4},{7,5},{8,10},{9,11},{10,... | collective-permute-start | bytes 3145736 | tf_op jit(solution)/shard_map/ppermute | solution.py:46
  160.9 45.3 %collective-permute-start.9 = (bf16[128,2048]{1,0:T(8,128)(2,1)}, bf16[128,2048]{1,0:T(8,128)(2,1)}, u32[]{:S(2)}, u32[]{:S(2)}) collective-permute-start(bf16[128,2048]{1,0:T(8,128)(2,1)} %slice.218), channel_id=1, source_target_pairs={{0,2},{1,3},{2,0},{3,1},{4,6},{5,7},{6,4},{7,5},{8,10},{9,11},{10,... | collective-permute-start | bytes 1572872 | tf_op jit(solution)/shard_map/ppermute | solution.py:46
  162.9 43.4 %collective-permute-start.10 = (bf16[128,2048]{1,0:T(8,128)(2,1)}, bf16[128,2048]{1,0:T(8,128)(2,1)}, u32[]{:S(2)}, u32[]{:S(2)}) collective-permute-start(bf16[128,2048]{1,0:T(8,128)(2,1)} %slice.219), channel_id=1, source_target_pairs={{0,4},{1,5},{2,6},{3,7},{4,0},{5,1},{6,2},{7,3},{8,12},{9,13},{10,... | collective-permute-start | bytes 1572872 | tf_op jit(solution)/shard_map/ppermute | solution.py:46
  201.6 136.5 %all-gather.8.cloned.1.call-start = ((), (), s32[]{:S(2)}) async-start(), calls=%async_computation.15 | async-start | bytes 5242880 | tf_op jit(solution)/shard_map/all_gather | solution.py:744
  210.7 66.8 %collective-permute-start.21 = (bf16[768,2048]{1,0:T(8,128)(2,1)}, bf16[768,2048]{1,0:T(8,128)(2,1)}, u32[]{:S(2)}, u32[]{:S(2)}) collective-permute-start(bf16[768,2048]{1,0:T(8,128)(2,1)} %pad_maximum_fusion.3), channel_id=1, source_target_pairs={{0,1},{1,0},{2,3},{3,2},{4,5},{5,4},{6,7},{7,6},{8,9},{9,8},{10,11... | collective-permute-start | bytes 9437192 | tf_op jit(solution)/shard_map/ppermute | solution.py:46
  233.6 244.8 %reduce-scatter.8.cloned.1.call-start = ((), (), s32[]{:S(2)}) async-start(), calls=%async_computation.17 | async-start | bytes 5242880 | tf_op jit(solution)/shard_map/reduce_scatter | solution.py:747
  235.3 32.7 %collective-permute-start.19 = (bf16[128,2048]{1,0:T(8,128)(2,1)S(1)}, bf16[128,2048]{1,0:T(8,128)(2,1)S(1)}, u32[]{:S(2)}, u32[]{:S(2)}) collective-permute-start(bf16[128,2048]{1,0:T(8,128)(2,1)S(1)} %slice.222), channel_id=1, source_target_pairs={{0,2},{1,3},{2,0},{3,1},{4,6},{5,7},{6,4},{7,5},{8,10},{9,11},{10,... | collective-permute-start | bytes 1572872 | tf_op jit(solution)/shard_map/ppermute | solution.py:46
  236.7 31.3 %collective-permute-start.20 = (bf16[128,2048]{1,0:T(8,128)(2,1)S(1)}, bf16[128,2048]{1,0:T(8,128)(2,1)S(1)}, u32[]{:S(2)}, u32[]{:S(2)}) collective-permute-start(bf16[128,2048]{1,0:T(8,128)(2,1)S(1)} %slice.223), channel_id=1, source_target_pairs={{0,4},{1,5},{2,6},{3,7},{4,0},{5,1},{6,2},{7,3},{8,12},{9,13},{10,... | collective-permute-start | bytes 1572872 | tf_op jit(solution)/shard_map/ppermute | solution.py:46
  259.8 43.6 %collective-permute-start.23 = (bf16[768,2048]{1,0:T(8,128)(2,1)}, bf16[768,2048]{1,0:T(8,128)(2,1)}, u32[]{:S(2)}, u32[]{:S(2)}) collective-permute-start(bf16[768,2048]{1,0:T(8,128)(2,1)} %pad_maximum_fusion.4), channel_id=1, source_target_pairs={{0,1},{1,0},{2,3},{3,2},{4,5},{5,4},{6,7},{7,6},{8,9},{9,8},{10,11... | collective-permute-start | bytes 9437192 | tf_op jit(solution)/shard_map/ppermute | solution.py:46
  337.9 220.4 %reduce-scatter.6.cloned.1.call-start = ((), (), s32[]{:S(2)}) async-start(), calls=%async_computation.16 | async-start | bytes 5242880 | tf_op jit(solution)/shard_map/reduce_scatter | solution.py:747
  392.3 207.2 %reduce-scatter.12.cloned.1.call-start = ((), (), s32[]{:S(2)}) async-start(), calls=%async_computation.19 | async-start | bytes 5242880 | tf_op jit(solution)/shard_map/reduce_scatter | solution.py:747
  417.7 25.2 %collective-permute-start.26 = (bf16[1024,2048]{1,0:T(8,128)(2,1)}, bf16[1024,2048]{1,0:T(8,128)(2,1)}, u32[]{:S(2)}, u32[]{:S(2)}) collective-permute-start(bf16[1024,2048]{1,0:T(8,128)(2,1)} %get-tuple-element.123), channel_id=1, source_target_pairs={{0,1},{1,0},{2,3},{3,2},{4,5},{5,4},{6,7},{7,6},{8,9},{9,8},{10,11... | collective-permute-start | bytes 12582920 | tf_op jit(solution)/shard_map/ppermute | solution.py:46
  423.1 25.0 %collective-permute-start.29 = (bf16[256,2048]{1,0:T(8,128)(2,1)}, bf16[256,2048]{1,0:T(8,128)(2,1)S(1)}, u32[]{:S(2)}, u32[]{:S(2)}) collective-permute-start(bf16[256,2048]{1,0:T(8,128)(2,1)} %pad_maximum_fusion.12), channel_id=1, source_target_pairs={{0,2},{1,3},{2,0},{3,1},{4,6},{5,7},{6,4},{7,5},{8,10},{9,11},{10,... | collective-permute-start | bytes 3145736 | tf_op jit(solution)/shard_map/ppermute | solution.py:46
  472.2 55.3 %collective-permute-start.35 = (bf16[1024,2048]{1,0:T(8,128)(2,1)}, bf16[1024,2048]{1,0:T(8,128)(2,1)}, u32[]{:S(2)}, u32[]{:S(2)}) collective-permute-start(bf16[1024,2048]{1,0:T(8,128)(2,1)} %get-tuple-element.135), channel_id=1, source_target_pairs={{0,1},{1,0},{2,3},{3,2},{4,5},{5,4},{6,7},{7,6},{8,9},{9,8},{10,11... | collective-permute-start | bytes 12582920 | tf_op jit(solution)/shard_map/ppermute | solution.py:46
  499.8 25.8 %collective-permute-start.33 = (bf16[256,2048]{1,0:T(8,128)(2,1)}, bf16[256,2048]{1,0:T(8,128)(2,1)S(1)}, u32[]{:S(2)}, u32[]{:S(2)}) collective-permute-start(bf16[256,2048]{1,0:T(8,128)(2,1)} %pad_maximum_fusion.14), channel_id=1, source_target_pairs={{0,2},{1,3},{2,0},{3,1},{4,6},{5,7},{6,4},{7,5},{8,10},{9,11},{10,... | collective-permute-start | bytes 3145736 | tf_op jit(solution)/shard_map/ppermute | solution.py:46
  542.8 79.0 %reduce-scatter.10.cloned.1.call-start = ((), (), s32[]{:S(2)}) async-start(), calls=%async_computation.18 | async-start | bytes 2621440 | tf_op jit(solution)/shard_map/reduce_scatter | solution.py:747
  571.1 33.7 %all-to-all-start.6 = ((bf16[8,64,1024]{2,1,0:T(8,128)(2,1)}), bf16[8,64,1024]{2,1,0:T(8,128)(2,1)S(1)}, u32[]{:S(2)}, u32[]{:S(2)}) async-start(bf16[8,64,1024]{2,1,0:T(8,128)(2,1)} %bitcast.88), calls=%async_computation.8 | async-start | bytes 2097152 | tf_op jit(solution)/shard_map/all_to_all | solution.py:750
  576.0 76.3 %reduce-scatter.14.cloned.1.call-start = ((), (), s32[]{:S(2)}) async-start(), calls=%async_computation.20 | async-start | bytes 1310720 | tf_op jit(solution)/shard_map/reduce_scatter | solution.py:747
  618.5 31.2 %collective-permute-start.41 = (bf16[256,2048]{1,0:T(8,128)(2,1)}, bf16[256,2048]{1,0:T(8,128)(2,1)}, u32[]{:S(2)}, u32[]{:S(2)}) collective-permute-start(bf16[256,2048]{1,0:T(8,128)(2,1)} %pad_maximum_fusion.18), channel_id=1, source_target_pairs={{0,2},{1,3},{2,0},{3,1},{4,6},{5,7},{6,4},{7,5},{8,10},{9,11},{10,... | collective-permute-start | bytes 3145736 | tf_op jit(solution)/shard_map/ppermute | solution.py:46
  619.7 30.1 %collective-permute-start.42 = (bf16[256,2048]{1,0:T(8,128)(2,1)}, bf16[256,2048]{1,0:T(8,128)(2,1)}, u32[]{:S(2)}, u32[]{:S(2)}) collective-permute-start(bf16[256,2048]{1,0:T(8,128)(2,1)} %pad_maximum_fusion.19), channel_id=1, source_target_pairs={{0,4},{1,5},{2,6},{3,7},{4,0},{5,1},{6,2},{7,3},{8,12},{9,13},{10,... | collective-permute-start | bytes 3145736 | tf_op jit(solution)/shard_map/ppermute | solution.py:46
  621.8 27.9 %all-to-all-start.7 = ((bf16[8,64,512]{2,1,0:T(8,128)(2,1)}), bf16[8,64,512]{2,1,0:T(8,128)(2,1)}, u32[]{:S(2)}, u32[]{:S(2)}) async-start(bf16[8,64,512]{2,1,0:T(8,128)(2,1)} %bitcast.90), calls=%async_computation.10 | async-start | bytes 1048576 | tf_op jit(solution)/shard_map/all_to_all | solution.py:750
  (68 other events, 1066.7 us)
Sparse Core Ops, SparseCore 0:
  29.3 69.3 all-gather.3
  100.8 148.5 all-gather.5
  251.6 78.7 all-gather.7
  338.0 75.0 reduce-scatter.7
  415.3 77.2 reduce-scatter.5
  494.8 77.2 reduce-scatter.11
  575.1 44.1 reduce-scatter.9
  621.6 26.4 reduce-scatter.13

commit v6 on v5

--- a/solution.py
+++ b/solution.py
@@ -856,7 +856,7 @@
     got = give(red_qkv.reshape(n_cp, own, qkv_cols))
     back_pairs = [(b, a) for a, b in deal(n_dp, n_cp, 0)]
     grad_output = lax.ppermute(wo_sum, ("dp", "cp"), back_pairs).astype(F32)
-    w_one = scatter_last(w_state, n_cp, got)
+    w_one = scatter_last(w_state, n_cp)
     grad_in = g_hidden + rms_one * (w_one - z_one * jnp.mean(w_one * z_one, -1, keepdims=True))
 
     grad_g, grad_u, gain_two_sum = finish_feed_call(back_gu, w_gate, w_up, gain_two, per_half, unit)

time: 693 us -> 687 us (level)
  waiting for transfers between devices: 141 us -> 134 us
    all_to_all x7, waiting for transfers between devices: 41.4 us -> 30.9 us  [give(): return lax.all_to_all(value, 'cp', 0, 0)]
  transfers between devices with their start and end apart: 61 -> 61, of which waited for: 17 -> 19; matrix products, arithmetic and copies ran while one was open for 31% -> 32% of each run, Pallas kernels for 28% -> 28%
where the time goes in v6:
time: 687 us; the launch traced here: 678 us
  Pallas kernels  191 us (28%)
  waiting for transfers between devices  134 us (20%)
  starting transfers between devices  93.7 us (14%)
  other arithmetic  90.8 us (13%)
  local copies, waits for them, and re-layouts  80.1 us (12%)
  matrix products  55 us (8%)
  blocking collectives  18.2 us (3%)
  between operations  15 us (2%)
    ppermute x44, waiting for transfers between devices, swap(): return lax.ppermute(value, 'cp', [(i, i ^ offset) for i in range(count)])  86.6 us
    dot_general x5, matrix products, mm(): return lax.dot_general(left, right, dims, preferred_element_type=F32)  55 us
    unnamed x109, local copies, waits for them, and re-layouts  50.9 us
    all_to_all x7, starting transfers between devices, give(): return lax.all_to_all(value, 'cp', 0, 0)  42.1 us
    pallas_call x2, Pallas kernels, packed_call(): pl.pallas_call(functools.partial(packed_kernel, down=down), grid=(total /...  40.6 us
    ppermute x44, starting transfers between devices, swap(): return lax.ppermute(value, 'cp', [(i, i ^ offset) for i in range(count)])  40.3 us
    pallas_call x2, Pallas kernels, feed_call(): pl.pallas_call(feed_kernel, grid=(total // rows,), in_specs=[pl.BlockSpec...  31.4 us
    all_to_all x7, waiting for transfers between devices, give(): return lax.all_to_all(value, 'cp', 0, 0)  30.9 us
  transfers between devices with their start and end apart: 61, of which 19 were waited for; matrix products, arithmetic and copies ran while one was open for 32% of the time, Pallas kernels for 28%

profile of v6, /device:TPU:1, one launch (start us, length us, event | category | flops | bytes accessed | tf_op | source)
XLA Modules:
  0.0 677.6 jit_solution(10879370427839786663)
XLA Ops:
  20.2 7.8 %collective-permute-done.6 = bf16[64,2048]{1,0:T(8,128)(2,1)S(1)} collective-permute-done((bf16[64,2048]{1,0:T(8,128)(2,1)S(1)}, bf16[64,2048]{1,0:T(8,128)(2,1)S(1)}, u32[]{:S(2)}, u32[]{:S(2)}) %collective-permute-start.6) | collective-permute-done | bytes 262176 | tf_op jit(solution)/shard_map/ppermute | solution.py:759
  35.9 10.4 %all-to-all-start.1 = ((bf16[8,64,1024]{2,1,0:T(8,128)(2,1)}), bf16[8,64,1024]{2,1,0:T(8,128)(2,1)S(1)}, u32[]{:S(2)}, u32[]{:S(2)}) async-start(bf16[8,64,1024]{2,1,0:T(8,128)(2,1)} %reshape.133), calls=%async_computation.1 | async-start | bytes 2097152 | tf_op jit(solution)/shard_map/all_to_all | solution.py:750
  47.6 10.6 %all-to-all-done.1 = bf16[8,64,1024]{2,1,0:T(8,128)(2,1)S(1)} async-done(((bf16[8,64,1024]{2,1,0:T(8,128)(2,1)}), bf16[8,64,1024]{2,1,0:T(8,128)(2,1)S(1)}, u32[]{:S(2)}, u32[]{:S(2)}) %all-to-all-start.1) | async-done | bytes 1048608 | tf_op jit(solution)/shard_map/all_to_all | solution.py:750
  83.1 15.0 %all-to-all-done.2 = bf16[8,64,1024]{2,1,0:T(8,128)(2,1)S(1)} async-done(((bf16[8,64,1024]{2,1,0:T(8,128)(2,1)}), bf16[8,64,1024]{2,1,0:T(8,128)(2,1)S(1)}, u32[]{:S(2)}, u32[]{:S(2)}) %all-to-all-start.2) | async-done | bytes 1048608 | tf_op jit(solution)/shard_map/all_to_all | solution.py:750
  112.3 33.0 %collective-permute-done.3 = bf16[128,2048]{1,0:T(8,128)(2,1)S(1)} collective-permute-done((bf16[128,2048]{1,0:T(8,128)(2,1)S(1)}, bf16[128,2048]{1,0:T(8,128)(2,1)S(1)}, u32[]{:S(2)}, u32[]{:S(2)}) %collective-permute-start.3) | collective-permute-done | bytes 524320 | tf_op jit(solution)/shard_map/ppermute | solution.py:46
  163.1 11.9 %qkv.1 = (bf16[2048,256]{1,0:T(8,128)(2,1)}, bf16[2048,128]{1,0:T(8,128)(2,1)}, bf16[2048,128]{1,0:T(8,128)(2,1)}, bf16[128,2048]{1,0:T(8,128)(2,1)}, bf16[128,2048]{1,0:T(8,128)(2,1)}) custom-call(bf16[2048,2048]{1,0:T(8,128)(2,1)} %constant_dynamic-update-slice_fusion.z_ref, bf16[4,768,512]{2,1,0:T(8,128)(2,1)} %bitcast.71, ...), custom_call_target="tpu_custom_call" | custom-call | flops 214748368 | bytes 524288 | tf_op jit(solution)/shard_map/qkv/pallas_call | solution.py:152
  175.0 21.5 %attend.1 = (bf16[2048,256]{1,0:T(8,128)(2,1)}, f32[8,1,512]{2,1,0:T(1,128)}) custom-call(s32[1]{0:T(128)} %bitcast.me_ref, bf16[2048,256]{1,0:T(8,128)(2,1)} %get-tuple-element.95.q_ref, bf16[2048,128]{1,0:T(8,128)(2,1)} %get-tuple-element.96.k_ref, bf16[128,2048]{1,0:T(8,128)(2,1)} %get-tuple-element.97.vt_ref), custom_call_target="tpu_custom_call" | custom-call | flops 214748368 | bytes 104857 | tf_op jit(solution)/shard_map/attend/pallas_call | solution.py:232
  220.9 10.1 %hidden.1 = (f32[256,2048]{1,0:T(8,128)}, bf16[256,2048]{1,0:T(8,128)(2,1)}, f32[256,1]{1,0:T(8,128)}) custom-call(s32[1]{0:T(128)} %bitcast.me_ref, bf16[8,256,256]{2,1,0:T(8,128)(2,1)} %copy-done.10, bf16[2048,2048]{1,0:T(8,128)(2,1)} %constant_dynamic-update-slice_fusion.7.w_ref, bf16[256,2048]{1,0:T(8,128)(2,1)} %bitcast.67), custom_call_target="tpu_custom_call" | custom-call | flops 107374184 | bytes 681574 | tf_op jit(solution)/shard_map/hidden/pallas_call | solution.py:501
  236.8 19.1 %collective-permute-done.14 = bf16[256,2048]{1,0:T(8,128)(2,1)S(1)} collective-permute-done((bf16[256,2048]{1,0:T(8,128)(2,1)}, bf16[256,2048]{1,0:T(8,128)(2,1)S(1)}, u32[]{:S(2)}, u32[]{:S(2)}) %collective-permute-start.14) | collective-permute-done | bytes 1048608 | tf_op jit(solution)/shard_map/ppermute | solution.py:46
  282.6 15.0 %back_act.1.g_ref = f32[2048,1024]{1,0:T(8,128)} custom-call(bf16[2048,2048]{1,0:T(8,128)(2,1)} %constant_dynamic-update-slice_fusion.14.g_ref, bf16[4,1024,1024]{2,1,0:T(8,128)(2,1)} %bitcast.63), custom_call_target="tpu_custom_call" | custom-call | flops 429496736 | bytes 1048576 | tf_op jit(solution)/shard_map/back_act/pallas_call | solution.py:371
  308.5 15.4 %feed.2 = (bf16[2048,512]{1,0:T(8,128)(2,1)}, bf16[2048,1024]{1,0:T(8,128)(2,1)}) custom-call(bf16[2048,2048]{1,0:T(8,128)(2,1)} %constant_dynamic-update-slice_fusion.21.z_ref, f32[2048,1024]{1,0:T(8,128)} %back_act.1.g_ref, bf16[4,1024,1024]{2,1,0:T(8,128)(2,1)} %bitcast.64), custom_call_target="tpu_custom_call" | custom-call | flops 429496736 | bytes 1153433 | tf_op jit(solution)/shard_map/feed/pallas_call | solution.py:407
  323.9 14.0 %convolution_convert_fusion.1 = bf16[2048,1024]{1,0:T(8,128)(2,1)} fusion(bf16[2048,2048]{1,0:T(8,128)(2,1)} %constant_dynamic-update-slice_fusion.21.z_ref, bf16[2048,1024]{1,0:T(8,128)(2,1)} %get-tuple-element.110.refs_0_), kind=kOutput, calls=%fused_computation.6 | convolution fusion | flops 8592031744 | bytes 16777216 | tf_op jit(solution)/shard_map/dot_general | solution.py:29
  338.1 16.0 %feed.3 = (bf16[2048,512]{1,0:T(8,128)(2,1)}, bf16[2048,1024]{1,0:T(8,128)(2,1)}) custom-call(bf16[2048,2048]{1,0:T(8,128)(2,1)} %constant_dynamic-update-slice_fusion.21.z_ref, f32[2048,1024]{1,0:T(8,128)} %back_act.1.g_ref, bf16[4,512,1024]{2,1,0:T(8,128)(2,1)} %bitcast.68), custom_call_target="tpu_custom_call" | custom-call | flops 429496736 | bytes 1153433 | tf_op jit(solution)/shard_map/feed/pallas_call | solution.py:407
  354.1 25.5 %g_two.1 = (bf16[1024,2048]{1,0:T(8,128)(2,1)}, bf16[1024,2048]{1,0:T(8,128)(2,1)}) custom-call(bf16[2048,1024]{1,0:T(8,128)(2,1)} %get-tuple-element.110.refs_0_, bf16[2048,1024]{1,0:T(8,128)(2,1)} %get-tuple-element.115.refs_1_, bf16[4,1024,1024]{2,1,0:T(8,128)(2,1)} %bitcast.65, bf16[4,512,1024]{2,1,0:T(8,128)(2,1)} %bitcast.69), custom_call_target="tpu_custom_call" | custom-call | flops 858993472 | bytes 1258291 | tf_op jit(solution)/shard_map/g_two/pallas_call | solution.py:631
  379.6 12.7 %convolution_convert_fusion = bf16[2048,1024]{1,0:T(8,128)(2,1)} fusion(bf16[2048,2048]{1,0:T(8,128)(2,1)} %constant_dynamic-update-slice_fusion.21.z_ref, bf16[2048,1024]{1,0:T(8,128)(2,1)S(1)} %copy-done.17), kind=kOutput, calls=%fused_computation.5 | convolution fusion | flops 8592031744 | bytes 16777216 | tf_op jit(solution)/shard_map/dot_general | solution.py:29
  392.4 5.4 add_convert_fusion.3
  402.6 15.1 %out.1 = (bf16[1024,2048]{1,0:T(8,128)(2,1)}, bf16[1024,2048]{1,0:T(8,128)(2,1)}) custom-call(bf16[2048,512]{1,0:T(8,128)(2,1)} %get-tuple-element.124.refs_0_, bf16[2048,512]{1,0:T(8,128)(2,1)} %get-tuple-element.125.refs_1_, bf16[4,1024,1024]{2,1,0:T(8,128)(2,1)} %bitcast.66), custom_call_target="tpu_custom_call" | custom-call | flops 429496736 | bytes 838860 | tf_op jit(solution)/shard_map/out/pallas_call | solution.py:631
  424.6 9.1 %convolution_convert_fusion.3 = bf16[512,2048]{1,0:T(8,128)(2,1)} fusion(bf16[2048,512]{1,0:T(8,128)(2,1)S(1)} %copy-done.26, bf16[2048,2048]{1,0:T(8,128)(2,1)} %constant_dynamic-update-slice_fusion.14.g_ref), kind=kOutput, calls=%fused_computation.12 | convolution fusion | flops 4296015872 | bytes 12582912 | tf_op jit(solution)/shard_map/dot_general | solution.py:29
  433.7 9.3 %convolution_convert_fusion.4 = bf16[512,2048]{1,0:T(8,128)(2,1)} fusion(bf16[2048,512]{1,0:T(8,128)(2,1)S(1)} %copy-done.25, bf16[2048,2048]{1,0:T(8,128)(2,1)} %constant_dynamic-update-slice_fusion.14.g_ref), kind=kOutput, calls=%fused_computation.13 | convolution fusion | flops 4296015872 | bytes 12582912 | tf_op jit(solution)/shard_map/dot_general | solution.py:29
  452.4 8.8 %back_attn.1 = bf16[8,256,256]{2,1,0:T(8,128)(2,1)} custom-call(s32[1]{0:T(128)} %bitcast.me_ref, bf16[256,2048]{1,0:T(8,128)(2,1)} %get-tuple-element.131.g_ref, bf16[2048,2048]{1,0:T(8,128)(2,1)} %constant_dynamic-update-slice_fusion.7.w_ref), custom_call_target="tpu_custom_call" | custom-call | flops 107374184 | bytes 524288 | tf_op jit(solution)/shard_map/back_attn/pallas_call | solution.py:538
  463.1 9.1 %grad_wo.1 = (bf16[1024,2048]{1,0:T(8,128)(2,1)}, bf16[1024,2048]{1,0:T(8,128)(2,1)}) custom-call(s32[1]{0:T(128)} %bitcast.me_ref, bf16[8,256,256]{2,1,0:T(8,128)(2,1)} %copy-done.10, bf16[256,2048]{1,0:T(8,128)(2,1)} %get-tuple-element.131.g_ref), custom_call_target="tpu_custom_call" | custom-call | flops 107374184 | bytes 524288 | tf_op jit(solution)/shard_map/grad_wo/pallas_call | solution.py:570
  481.6 18.2 %all_to_all.40 = bf16[8,256,256]{2,1,0:T(8,128)(2,1)} all-to-all(bf16[8,256,256]{2,1,0:T(8,128)(2,1)S(1)} %copy-done.24), channel_id=1, replica_groups=mesh['dp'=4,'cp'=8] {'cp'}, dimensions={0} | all-to-all | bytes 2097152 | tf_op jit(solution)/shard_map/all_to_all | solution.py:750
  501.0 24.6 %attend_back.1.refs_0_ = bf16[2048,512]{1,0:T(8,128)(2,1)} custom-call(s32[1]{0:T(128)} %bitcast.me_ref, bf16[2048,256]{1,0:T(8,128)(2,1)} %get-tuple-element.95.q_ref, bf16[2048,256]{1,0:T(8,128)(2,1)} %bitcast.79, bf16[2048,256]{1,0:T(8,128)(2,1)} %get-tuple-element.98.o_ref, f32[8,1,512]{2,1,0:T(1,128)} %get-tuple-element.140.lse_ref, ...), custom_call_target="tpu_custom_call" | custom-call | flops 536870912 | bytes 209715 | tf_op jit(solution)/shard_map/attend_back/pallas_call | solution.py:328
  542.8 11.0 %g_one.1 = (bf16[1024,2048]{1,0:T(8,128)(2,1)}, bf16[1024,2048]{1,0:T(8,128)(2,1)}) custom-call(bf16[2048,512]{1,0:T(8,128)(2,1)} %attend_back.1.refs_0_, bf16[2048,512]{1,0:T(8,128)(2,1)} %bitcast.77), custom_call_target="tpu_custom_call" | custom-call | flops 214748368 | bytes 629145 | tf_op jit(solution)/shard_map/g_one/pallas_call | solution.py:458
  558.2 9.9 %convolution_convert_fusion.2 = bf16[2048,512]{1,0:T(8,128)(2,1)} fusion(bf16[2048,2048]{1,0:T(8,128)(2,1)} %constant_dynamic-update-slice_fusion.z_ref, bf16[2048,512]{1,0:T(8,128)(2,1)S(1)} %copy-done.12), kind=kOutput, calls=%fused_computation.11 | convolution fusion | flops 4296015872 | bytes 12582912 | tf_op jit(solution)/shard_map/dot_general | solution.py:29
  576.3 5.4 add_convert_fusion
  581.7 9.5 %collective-permute-done.43 = bf16[256,2048]{1,0:T(8,128)(2,1)S(1)} collective-permute-done((bf16[256,2048]{1,0:T(8,128)(2,1)}, bf16[256,2048]{1,0:T(8,128)(2,1)S(1)}, u32[]{:S(2)}, u32[]{:S(2)}) %collective-permute-start.43) | collective-permute-done | bytes 1048608 | tf_op jit(solution)/shard_map/ppermute | solution.py:46
  599.7 5.2 all-to-all-done.6.refs_1_
  604.9 10.7 %collective-permute-done.40 = bf16[128,2048]{1,0:T(8,128)(2,1)} collective-permute-done((bf16[128,2048]{1,0:T(8,128)(2,1)}, bf16[128,2048]{1,0:T(8,128)(2,1)}, u32[]{:S(2)}, u32[]{:S(2)}) %collective-permute-start.40) | collective-permute-done | bytes 524320 | tf_op jit(solution)/shard_map/ppermute | solution.py:46
  632.4 6.9 %all-to-all-start.7 = ((bf16[8,64,512]{2,1,0:T(8,128)(2,1)}), bf16[8,64,512]{2,1,0:T(8,128)(2,1)}, u32[]{:S(2)}, u32[]{:S(2)}) async-start(bf16[8,64,512]{2,1,0:T(8,128)(2,1)} %bitcast.90), calls=%async_computation.10 | async-start | bytes 1048576 | tf_op jit(solution)/shard_map/all_to_all | solution.py:750
  647.5 7.1 %collective-permute-start.45 = (bf16[64,2048]{1,0:T(8,128)(2,1)}, bf16[64,2048]{1,0:T(8,128)(2,1)S(1)}, u32[]{:S(2)}, u32[]{:S(2)}) collective-permute-start(bf16[64,2048]{1,0:T(8,128)(2,1)} %reduce-scatter.14.cloned.1.call-done), channel_id=1, source_target_pairs={{0,0},{8,1},{16,2},{24,3},{1,4},{9,5},{17,6},{25,7},{2,8},{10,9},{... | collective-permute-start | bytes 786440 | tf_op jit(solution)/shard_map/ppermute | solution.py:858
  662.4 7.3 %collective-permute-done.45 = bf16[64,2048]{1,0:T(8,128)(2,1)S(1)} collective-permute-done((bf16[64,2048]{1,0:T(8,128)(2,1)}, bf16[64,2048]{1,0:T(8,128)(2,1)S(1)}, u32[]{:S(2)}, u32[]{:S(2)}) %collective-permute-start.45) | collective-permute-done | bytes 262176 | tf_op jit(solution)/shard_map/ppermute | solution.py:858
  (313 shorter events, 251.9 us)
Async XLA Ops:
  17.0 88.0 %all-gather.4.cloned.1.call-start = ((), (), s32[]{:S(2)}) async-start(), calls=%async_computation.13 | async-start | bytes 3932160 | tf_op jit(solution)/shard_map/all_gather | solution.py:744
  46.3 236.3 %all-gather.6.cloned.1.call-start = ((), (), s32[]{:S(2)}) async-start(), calls=%async_computation.14 | async-start | bytes 10485760 | tf_op jit(solution)/shard_map/all_gather | solution.py:744
  62.5 35.7 %collective-permute-start = (bf16[256,2048]{1,0:T(8,128)(2,1)}, bf16[256,2048]{1,0:T(8,128)(2,1)S(1)}, u32[]{:S(2)}, u32[]{:S(2)}) collective-permute-start(bf16[256,2048]{1,0:T(8,128)(2,1)} %get-tuple-element.174), channel_id=1, source_target_pairs={{0,2},{1,3},{2,0},{3,1},{4,6},{5,7},{6,4},{7,5},{8,10},{9,11},{10,... | collective-permute-start | bytes 3145736 | tf_op jit(solution)/shard_map/ppermute | solution.py:46
  70.7 27.5 %all-to-all-start.2 = ((bf16[8,64,1024]{2,1,0:T(8,128)(2,1)}), bf16[8,64,1024]{2,1,0:T(8,128)(2,1)S(1)}, u32[]{:S(2)}, u32[]{:S(2)}) async-start(bf16[8,64,1024]{2,1,0:T(8,128)(2,1)} %reshape.136), calls=%async_computation.2 | async-start | bytes 2097152 | tf_op jit(solution)/shard_map/all_to_all | solution.py:750
  101.5 50.7 %collective-permute-start.4 = (bf16[768,2048]{1,0:T(8,128)(2,1)}, bf16[768,2048]{1,0:T(8,128)(2,1)}, u32[]{:S(2)}, u32[]{:S(2)}) collective-permute-start(bf16[768,2048]{1,0:T(8,128)(2,1)} %pad_maximum_fusion.1), channel_id=1, source_target_pairs={{0,1},{1,0},{2,3},{3,2},{4,5},{5,4},{6,7},{7,6},{8,9},{9,8},{10,11... | collective-permute-start | bytes 9437192 | tf_op jit(solution)/shard_map/ppermute | solution.py:46
  109.1 37.3 %collective-permute-start.8 = (bf16[256,2048]{1,0:T(8,128)(2,1)S(1)}, bf16[256,2048]{1,0:T(8,128)(2,1)S(1)}, u32[]{:S(2)}, u32[]{:S(2)}) collective-permute-start(bf16[256,2048]{1,0:T(8,128)(2,1)S(1)} %reshape.140), channel_id=1, source_target_pairs={{0,4},{1,5},{2,6},{3,7},{4,0},{5,1},{6,2},{7,3},{8,12},{9,13},{10,... | collective-permute-start | bytes 3145736 | tf_op jit(solution)/shard_map/ppermute | solution.py:46
  109.3 37.1 %collective-permute-start.7 = (bf16[256,2048]{1,0:T(8,128)(2,1)S(1)}, bf16[256,2048]{1,0:T(8,128)(2,1)S(1)}, u32[]{:S(2)}, u32[]{:S(2)}) collective-permute-start(bf16[256,2048]{1,0:T(8,128)(2,1)S(1)} %reshape.140), channel_id=1, source_target_pairs={{0,2},{1,3},{2,0},{3,1},{4,6},{5,7},{6,4},{7,5},{8,10},{9,11},{10,... | collective-permute-start | bytes 3145736 | tf_op jit(solution)/shard_map/ppermute | solution.py:46
  110.9 34.4 %collective-permute-start.3 = (bf16[128,2048]{1,0:T(8,128)(2,1)S(1)}, bf16[128,2048]{1,0:T(8,128)(2,1)S(1)}, u32[]{:S(2)}, u32[]{:S(2)}) collective-permute-start(bf16[128,2048]{1,0:T(8,128)(2,1)S(1)} %slice.216), channel_id=1, source_target_pairs={{0,4},{1,5},{2,6},{3,7},{4,0},{5,1},{6,2},{7,3},{8,12},{9,13},{10,... | collective-permute-start | bytes 1572872 | tf_op jit(solution)/shard_map/ppermute | solution.py:46
  111.1 34.3 %collective-permute-start.2 = (bf16[128,2048]{1,0:T(8,128)(2,1)S(1)}, bf16[128,2048]{1,0:T(8,128)(2,1)S(1)}, u32[]{:S(2)}, u32[]{:S(2)}) collective-permute-start(bf16[128,2048]{1,0:T(8,128)(2,1)S(1)} %slice.172), channel_id=1, source_target_pairs={{0,2},{1,3},{2,0},{3,1},{4,6},{5,7},{6,4},{7,5},{8,10},{9,11},{10,... | collective-permute-start | bytes 1572872 | tf_op jit(solution)/shard_map/ppermute | solution.py:46
  148.4 66.4 %collective-permute-start.11 = (bf16[768,2048]{1,0:T(8,128)(2,1)}, bf16[768,2048]{1,0:T(8,128)(2,1)}, u32[]{:S(2)}, u32[]{:S(2)}) collective-permute-start(bf16[768,2048]{1,0:T(8,128)(2,1)} %pad_maximum_fusion.2), channel_id=1, source_target_pairs={{0,1},{1,0},{2,3},{3,2},{4,5},{5,4},{6,7},{7,6},{8,9},{9,8},{10,11... | collective-permute-start | bytes 9437192 | tf_op jit(solution)/shard_map/ppermute | solution.py:46
  157.5 50.3 %collective-permute-start.18 = (bf16[256,2048]{1,0:T(8,128)(2,1)S(1)}, bf16[256,2048]{1,0:T(8,128)(2,1)S(1)}, u32[]{:S(2)}, u32[]{:S(2)}) collective-permute-start(bf16[256,2048]{1,0:T(8,128)(2,1)S(1)} %bitcast.73), channel_id=1, source_target_pairs={{0,4},{1,5},{2,6},{3,7},{4,0},{5,1},{6,2},{7,3},{8,12},{9,13},{10,... | collective-permute-start | bytes 3145736 | tf_op jit(solution)/shard_map/ppermute | solution.py:46
  158.7 49.1 %collective-permute-start.17 = (bf16[256,2048]{1,0:T(8,128)(2,1)S(1)}, bf16[256,2048]{1,0:T(8,128)(2,1)}, u32[]{:S(2)}, u32[]{:S(2)}) collective-permute-start(bf16[256,2048]{1,0:T(8,128)(2,1)S(1)} %bitcast.74), channel_id=1, source_target_pairs={{0,2},{1,3},{2,0},{3,1},{4,6},{5,7},{6,4},{7,5},{8,10},{9,11},{10,... | collective-permute-start | bytes 3145736 | tf_op jit(solution)/shard_map/ppermute | solution.py:46
  160.9 45.3 %collective-permute-start.9 = (bf16[128,2048]{1,0:T(8,128)(2,1)}, bf16[128,2048]{1,0:T(8,128)(2,1)}, u32[]{:S(2)}, u32[]{:S(2)}) collective-permute-start(bf16[128,2048]{1,0:T(8,128)(2,1)} %slice.218), channel_id=1, source_target_pairs={{0,2},{1,3},{2,0},{3,1},{4,6},{5,7},{6,4},{7,5},{8,10},{9,11},{10,... | collective-permute-start | bytes 1572872 | tf_op jit(solution)/shard_map/ppermute | solution.py:46
  162.9 43.4 %collective-permute-start.10 = (bf16[128,2048]{1,0:T(8,128)(2,1)}, bf16[128,2048]{1,0:T(8,128)(2,1)}, u32[]{:S(2)}, u32[]{:S(2)}) collective-permute-start(bf16[128,2048]{1,0:T(8,128)(2,1)} %slice.219), channel_id=1, source_target_pairs={{0,4},{1,5},{2,6},{3,7},{4,0},{5,1},{6,2},{7,3},{8,12},{9,13},{10,... | collective-permute-start | bytes 1572872 | tf_op jit(solution)/shard_map/ppermute | solution.py:46
  201.6 136.5 %all-gather.8.cloned.1.call-start = ((), (), s32[]{:S(2)}) async-start(), calls=%async_computation.15 | async-start | bytes 5242880 | tf_op jit(solution)/shard_map/all_gather | solution.py:744
  210.7 66.8 %collective-permute-start.21 = (bf16[768,2048]{1,0:T(8,128)(2,1)}, bf16[768,2048]{1,0:T(8,128)(2,1)}, u32[]{:S(2)}, u32[]{:S(2)}) collective-permute-start(bf16[768,2048]{1,0:T(8,128)(2,1)} %pad_maximum_fusion.3), channel_id=1, source_target_pairs={{0,1},{1,0},{2,3},{3,2},{4,5},{5,4},{6,7},{7,6},{8,9},{9,8},{10,11... | collective-permute-start | bytes 9437192 | tf_op jit(solution)/shard_map/ppermute | solution.py:46
  231.0 24.9 %collective-permute-start.14 = (bf16[256,2048]{1,0:T(8,128)(2,1)}, bf16[256,2048]{1,0:T(8,128)(2,1)S(1)}, u32[]{:S(2)}, u32[]{:S(2)}) collective-permute-start(bf16[256,2048]{1,0:T(8,128)(2,1)} %get-tuple-element.102), channel_id=1, source_target_pairs={{0,4},{1,5},{2,6},{3,7},{4,0},{5,1},{6,2},{7,3},{8,12},{9,13},{10,... | collective-permute-start | bytes 3145736 | tf_op jit(solution)/shard_map/ppermute | solution.py:46
  233.6 244.8 %reduce-scatter.8.cloned.1.call-start = ((), (), s32[]{:S(2)}) async-start(), calls=%async_computation.17 | async-start | bytes 5242880 | tf_op jit(solution)/shard_map/reduce_scatter | solution.py:747
  235.3 32.7 %collective-permute-start.19 = (bf16[128,2048]{1,0:T(8,128)(2,1)S(1)}, bf16[128,2048]{1,0:T(8,128)(2,1)S(1)}, u32[]{:S(2)}, u32[]{:S(2)}) collective-permute-start(bf16[128,2048]{1,0:T(8,128)(2,1)S(1)} %slice.222), channel_id=1, source_target_pairs={{0,2},{1,3},{2,0},{3,1},{4,6},{5,7},{6,4},{7,5},{8,10},{9,11},{10,... | collective-permute-start | bytes 1572872 | tf_op jit(solution)/shard_map/ppermute | solution.py:46
  236.7 31.3 %collective-permute-start.20 = (bf16[128,2048]{1,0:T(8,128)(2,1)S(1)}, bf16[128,2048]{1,0:T(8,128)(2,1)S(1)}, u32[]{:S(2)}, u32[]{:S(2)}) collective-permute-start(bf16[128,2048]{1,0:T(8,128)(2,1)S(1)} %slice.223), channel_id=1, source_target_pairs={{0,4},{1,5},{2,6},{3,7},{4,0},{5,1},{6,2},{7,3},{8,12},{9,13},{10,... | collective-permute-start | bytes 1572872 | tf_op jit(solution)/shard_map/ppermute | solution.py:46
  259.8 43.6 %collective-permute-start.23 = (bf16[768,2048]{1,0:T(8,128)(2,1)}, bf16[768,2048]{1,0:T(8,128)(2,1)}, u32[]{:S(2)}, u32[]{:S(2)}) collective-permute-start(bf16[768,2048]{1,0:T(8,128)(2,1)} %pad_maximum_fusion.4), channel_id=1, source_target_pairs={{0,1},{1,0},{2,3},{3,2},{4,5},{5,4},{6,7},{7,6},{8,9},{9,8},{10,11... | collective-permute-start | bytes 9437192 | tf_op jit(solution)/shard_map/ppermute | solution.py:46
  337.9 220.4 %reduce-scatter.6.cloned.1.call-start = ((), (), s32[]{:S(2)}) async-start(), calls=%async_computation.16 | async-start | bytes 5242880 | tf_op jit(solution)/shard_map/reduce_scatter | solution.py:747
  392.3 207.3 %reduce-scatter.12.cloned.1.call-start = ((), (), s32[]{:S(2)}) async-start(), calls=%async_computation.19 | async-start | bytes 5242880 | tf_op jit(solution)/shard_map/reduce_scatter | solution.py:747
  417.7 25.2 %collective-permute-start.26 = (bf16[1024,2048]{1,0:T(8,128)(2,1)}, bf16[1024,2048]{1,0:T(8,128)(2,1)}, u32[]{:S(2)}, u32[]{:S(2)}) collective-permute-start(bf16[1024,2048]{1,0:T(8,128)(2,1)} %get-tuple-element.121), channel_id=1, source_target_pairs={{0,1},{1,0},{2,3},{3,2},{4,5},{5,4},{6,7},{7,6},{8,9},{9,8},{10,11... | collective-permute-start | bytes 12582920 | tf_op jit(solution)/shard_map/ppermute | solution.py:46
  423.1 25.0 %collective-permute-start.29 = (bf16[256,2048]{1,0:T(8,128)(2,1)}, bf16[256,2048]{1,0:T(8,128)(2,1)S(1)}, u32[]{:S(2)}, u32[]{:S(2)}) collective-permute-start(bf16[256,2048]{1,0:T(8,128)(2,1)} %pad_maximum_fusion.12), channel_id=1, source_target_pairs={{0,2},{1,3},{2,0},{3,1},{4,6},{5,7},{6,4},{7,5},{8,10},{9,11},{10,... | collective-permute-start | bytes 3145736 | tf_op jit(solution)/shard_map/ppermute | solution.py:46
  472.2 55.3 %collective-permute-start.35 = (bf16[1024,2048]{1,0:T(8,128)(2,1)}, bf16[1024,2048]{1,0:T(8,128)(2,1)}, u32[]{:S(2)}, u32[]{:S(2)}) collective-permute-start(bf16[1024,2048]{1,0:T(8,128)(2,1)} %get-tuple-element.133), channel_id=1, source_target_pairs={{0,1},{1,0},{2,3},{3,2},{4,5},{5,4},{6,7},{7,6},{8,9},{9,8},{10,11... | collective-permute-start | bytes 12582920 | tf_op jit(solution)/shard_map/ppermute | solution.py:46
  499.8 25.8 %collective-permute-start.33 = (bf16[256,2048]{1,0:T(8,128)(2,1)}, bf16[256,2048]{1,0:T(8,128)(2,1)S(1)}, u32[]{:S(2)}, u32[]{:S(2)}) collective-permute-start(bf16[256,2048]{1,0:T(8,128)(2,1)} %pad_maximum_fusion.14), channel_id=1, source_target_pairs={{0,2},{1,3},{2,0},{3,1},{4,6},{5,7},{6,4},{7,5},{8,10},{9,11},{10,... | collective-permute-start | bytes 3145736 | tf_op jit(solution)/shard_map/ppermute | solution.py:46
  500.8 24.8 %collective-permute-start.34 = (bf16[256,2048]{1,0:T(8,128)(2,1)S(1)}, bf16[256,2048]{1,0:T(8,128)(2,1)S(1)}, u32[]{:S(2)}, u32[]{:S(2)}) collective-permute-start(bf16[256,2048]{1,0:T(8,128)(2,1)S(1)} %pad_maximum_fusion.15), channel_id=1, source_target_pairs={{0,4},{1,5},{2,6},{3,7},{4,0},{5,1},{6,2},{7,3},{8,12},{9,13},{10,... | collective-permute-start | bytes 3145736 | tf_op jit(solution)/shard_map/ppermute | solution.py:46
  542.8 89.6 %reduce-scatter.10.cloned.1.call-start = ((), (), s32[]{:S(2)}) async-start(), calls=%async_computation.18 | async-start | bytes 2621440 | tf_op jit(solution)/shard_map/reduce_scatter | solution.py:747
  571.2 33.7 %all-to-all-start.6 = ((bf16[8,64,1024]{2,1,0:T(8,128)(2,1)}), bf16[8,64,1024]{2,1,0:T(8,128)(2,1)S(1)}, u32[]{:S(2)}, u32[]{:S(2)}) async-start(bf16[8,64,1024]{2,1,0:T(8,128)(2,1)} %bitcast.88), calls=%async_computation.8 | async-start | bytes 2097152 | tf_op jit(solution)/shard_map/all_to_all | solution.py:750
  576.1 71.4 %reduce-scatter.14.cloned.1.call-start = ((), (), s32[]{:S(2)}) async-start(), calls=%async_computation.20 | async-start | bytes 1310720 | tf_op jit(solution)/shard_map/reduce_scatter | solution.py:747
  632.4 26.3 %all-to-all-start.7 = ((bf16[8,64,512]{2,1,0:T(8,128)(2,1)}), bf16[8,64,512]{2,1,0:T(8,128)(2,1)}, u32[]{:S(2)}, u32[]{:S(2)}) async-start(bf16[8,64,512]{2,1,0:T(8,128)(2,1)} %bitcast.90), calls=%async_computation.10 | async-start | bytes 1048576 | tf_op jit(solution)/shard_map/all_to_all | solution.py:750
  (68 other events, 1037.8 us)
Sparse Core Ops, SparseCore 0:
  29.3 69.3 all-gather.3
  100.8 148.5 all-gather.5
  251.6 78.7 all-gather.7
  338.0 75.0 reduce-scatter.7
  415.3 77.2 reduce-scatter.5
  494.8 77.2 reduce-scatter.11
  574.5 44.1 reduce-scatter.9
  621.0 26.4 reduce-scatter.13
